TPU v7x, 512 devices: a whole 4x8x8 slice. The times are simulated.
512 devices in a mesh: dp: 32 (over x, z_lo, core), ffn: 16 (over y, z_hi).
Axes of the slice: x: 4, y: 8, z: 8 (z_hi: 2, z_lo: 4; z = z_hi * 4 + z_lo), core: 2. Of those that a mesh axis runs over, the one named last changes fastest.
Arguments:
- train_act: bfloat16 [16384, 25600], P('dp', 'ffn'), may hold values from -6 to 6
- train_grad: bfloat16 [16384, 5120], P('dp', 'ffn'), may hold values from -6 to 6
- train_seg: int32 [32, 512], P('dp'), may hold values from 0 to 3, never falling along the last dimension, each value on 1 to 256 neighbouring positions
- train_mask: int32 [32, 512], P('dp'), may hold values 0 or 1
- test_act: bfloat16 [1024, 25600], P('dp', 'ffn'), may hold values from -6 to 6
- test_grad: bfloat16 [1024, 5120], P('dp', 'ffn'), may hold values from -6 to 6
- test_seg: int32 [1024], replicated, may hold values from 0 to 7, never falling along the last dimension, each value on 1 to 256 neighbouring positions
- test_mask: int32 [1024], replicated, may hold values 0 or 1
Outputs:
- scores: float32 [128, 8], P('dp')
Inputs may be any that keep to these rules, and one draw needn't show every extreme that they name: `train_seg`: each block holds 4 sequences of 1 to 256 tokens in order, one of exactly 256. `test_seg`: sequences in order, each 1 to 256 tokens, one of exactly 256.
All inputs are finite; a program needn't handle non-finite values. No bound on the sum of `train_mask` on one device may be relied on, other than what follows from the above.
Results may differ from a plain program's by a relative error of at most 0.0003.
Values may be sent and summed in bfloat16 or wider, within the bound.
No kernel may reach another device: no remote copies, remote signals or barrier semaphores. Data moves between devices by JAX's collectives and lax.ppermute only.
A program may use at most 64 MiB of HBM per device.

v0:
```python
import math

import jax
import jax.numpy as jnp
from jax import lax
from jax.sharding import PartitionSpec as P

D = 5120
FF = 25600
SEG_LEN = 256
SEQ_PACK = 4


def cross_rows(left, right):
    return lax.dot_general(
        left, right, (((1,), (1,)), ((), ())), preferred_element_type=jnp.float32
    )


def on_device(
    train_act, train_grad, train_seg, train_mask, test_act, test_grad, test_seg, test_mask
):
    masked_train = train_grad * train_mask.reshape(-1, 1).astype(jnp.bfloat16)
    test_total = test_seg.shape[0]
    local_rows = test_act.shape[0]
    start_row = lax.axis_index("dp") * local_rows
    local_mask = lax.dynamic_slice_in_dim(test_mask, start_row, local_rows, 0)
    masked_test = test_grad * local_mask.reshape(-1, 1).astype(jnp.bfloat16)
    all_act, all_grad = (
        lax.all_gather(test_act, "dp", axis=0, tiled=True),
        lax.all_gather(masked_test, "dp", axis=0, tiled=True),
    )
    act_gram = cross_rows(train_act, all_act)
    grad_gram = cross_rows(masked_train, all_grad)
    train_onehot = (train_seg == jnp.arange(SEQ_PACK, dtype=jnp.int32)[:, None]).astype(jnp.float32)
    scale = 1.0 / (SEG_LEN * math.sqrt(FF * D))
    act_total, grad_total = lax.psum((act_gram, grad_gram), "ffn")
    joint = act_total * grad_total
    test_onehot = (
        test_seg[:, None] == jnp.arange(2 * test_total // SEG_LEN, dtype=jnp.int32)[None, :]
    ).astype(jnp.float32)
    per_train = jnp.dot(train_onehot, joint, precision=lax.Precision.HIGHEST)
    scores = jnp.dot(per_train, test_onehot, precision=lax.Precision.HIGHEST)
    return scores * scale


def solution(mesh):
    return jax.shard_map(
        on_device,
        mesh=mesh,
        in_specs=(
            P("dp", "ffn"),
            P("dp", "ffn"),
            P("dp", None),
            P("dp", None),
            P("dp", "ffn"),
            P("dp", "ffn"),
            P(),
            P(),
        ),
        out_specs=P("dp", None),
        check_vma=False,
    )
```

profile of v0, /device:TPU:6, one launch (start us, length us, event | category | flops | bytes accessed | tf_op | source)
XLA Modules:
  0.0 500.0 jit_solution(11396429578777060638)
XLA Ops:
  6.5 0.0 copy-start
  6.5 0.0 all-gather.2.cloned.1.call-start
  6.5 0.7 all-gather.2.cloned.1.call-update
  7.3 0.0 all-reduce.3.cloned.1.call-start
  7.3 0.8 dynamic-slice_convert_fusion
  8.1 0.7 convert_reduce_fusion
  8.8 0.8 broadcast_multiply_fusion
  9.6 43.6 %all_gather.7 = bf16[1024,320]{1,0:T(8,128)(2,1)S(1)} all-gather(bf16[32,320]{1,0:T(8,128)(2,1)S(1)} %broadcast_multiply_fusion), channel_id=1, replica_groups=mesh['dp'=32,'ffn'=16] {'dp'}, dimensions={0}, use_global_device_ids=true | all-gather | bytes 675840 | tf_op jit(solution)/shard_map/all_gather | solution.py:31
  53.2 3.1 fusion.2
  56.2 22.4 %all-gather.2.cloned.1.call-done = bf16[1024,1600]{1,0:T(8,128)(2,1)} async-done(((bf16[32,1600]{1,0:T(8,128)(2,1)}), bf16[1024,1600]{1,0:T(8,128)(2,1)}) %all-gather.2.cloned.1.call-update) | async-done | bytes 3276816 | tf_op jit(solution)/shard_map/all_gather | solution.py:30
  78.6 0.0 copy-done
  78.6 5.4 %fusion.7 = f32[512,1024]{1,0:T(8,128)} fusion(bf16[512,1600]{0,1:T(8,128)(2,1)S(1)} %copy-done, bf16[1024,1600]{1,0:T(8,128)(2,1)} %all-gather.2.cloned.1.call-done), kind=kOutput, calls=%fused_computation.13 | convolution fusion | flops 1677721600 | bytes 7012352 | tf_op jit(solution)/shard_map/dot_general | solution.py:15
  84.0 0.0 copy-start.1
  84.0 0.0 all-reduce.3.cloned.1.call-update
  84.0 405.1 %all-reduce.3.cloned.1.call-done = (f32[512,1024]{1,0:T(8,128)}, f32[512,1024]{1,0:T(8,128)}) async-done(((f32[512,1024]{1,0:T(8,128)}, f32[512,1024]{1,0:T(8,128)}), (f32[512,1024]{1,0:T(8,128)}, f32[512,1024]{1,0:T(8,128)})) %all-reduce.3.cloned.1.call-update) | async-done | bytes 4194320 | tf_op jit(solution)/shard_map/psum | solution.py:37
  489.1 0.0 copy-done.1
  489.1 0.0 copy-start.2
  489.1 3.1 fusion
  492.2 0.0 copy-done.2
  492.2 1.0 convolution_multiply_fusion
Async XLA Ops:
  6.5 72.0 %copy-start = (bf16[512,1600]{0,1:T(8,128)(2,1)S(1)}, bf16[512,1600]{0,1:T(8,128)(2,1)}, u32[]{:S(2)}) copy-start(bf16[512,1600]{0,1:T(8,128)(2,1)} %param.8) | copy-start | bytes 4915204
  6.5 72.0 %all-gather.2.cloned.1.call-start = ((), (), s32[]{:S(2)}) async-start(), calls=%async_computation | async-start | bytes 3514368 | tf_op jit(solution)/shard_map/all_gather | solution.py:30
  7.3 481.9 %all-reduce.3.cloned.1.call-start = ((), (), s32[]{:S(2)}) async-start(), calls=%async_computation.1 | async-start | bytes 8388608 | tf_op jit(solution)/shard_map/psum | solution.py:37
  84.0 405.1 %copy-start.1 = (s32[1,512]{1,0:T(1,128)S(1)}, s32[1,512]{1,0:T(1,128)}, u32[]{:S(2)}) copy-start(s32[1,512]{1,0:T(1,128)} %param.10) | copy-start | bytes 6148
  489.1 3.1 copy-start.2
Sparse Core Ops, SparseCore 0:
  9.5 69.0 all-gather.1
  84.1 404.9 all-reduce.2
where the time goes:
time: 506 us; the launch traced here: 500 us
  waiting for transfers between devices  428 us (85%)
  blocking collectives  43.6 us (9%)
  between operations  13.4 us (3%)
  matrix products  12.5 us (2%)
    psum x1, waiting for transfers between devices, on_device(): act_total, grad_total = lax.psum((act_gram, grad_gram), 'ffn')  405 us
    all_gather x1, blocking collectives, on_device(): lax.all_gather(masked_test, 'dp', axis=0, tiled=True)  43.6 us
    all_gather x1, waiting for transfers between devices, on_device(): lax.all_gather(test_act, 'dp', axis=0, tiled=True)  22.4 us
  transfers between devices with their start and end apart: 2, of which 2 were waited for; matrix products, arithmetic and copies ran while one was open for 1% of the time, Pallas kernels for 0%

commit v1 on v0

v1 whole, which is shorter than its diff:
```python
import math

import jax
import jax.numpy as jnp
from jax import lax
from jax.sharding import Mesh, PartitionSpec as P

D = 5120
FF = 25600
SEG_LEN = 256
SEQ_PACK = 4
TEST_SEQS = 8
NX, NZ, NC, NY, NH = 4, 4, 2, 8, 2
DP = ("x", "z", "c")
FFN = ("y", "h")


def cross_rows(left, right):
    return lax.dot_general(
        left, right, (((1,), (1,)), ((), ())), preferred_element_type=jnp.float32
    )


def swap(value, axis):
    return lax.ppermute(value, axis, [(0, 1), (1, 0)])


def over_x(value):
    return [value] + [
        lax.ppermute(value, "x", [(i, (i + step) % NX) for i in range(NX)]) for step in (1, 3, 2)
    ]


def on_device(
    train_act, train_grad, train_seg, train_mask, test_act, test_grad, test_seg, test_mask
):
    x, y, h, c = (lax.axis_index(a) for a in ("x", "y", "h", "c"))
    grad_z = lax.all_gather(test_grad, "z", axis=0, tiled=True)
    act_z = lax.all_gather(test_act, "z", axis=0, tiled=True)
    other_grad, other_act = swap(train_grad, "c"), swap(train_act, "c")
    grads = over_x(grad_z)
    acts = over_x(act_z)

    def gram(chunks, own, other):
        both = jnp.concatenate([own, other], 0)
        return jnp.concatenate([cross_rows(t, both) for t in chunks], 0)

    grad_gram = gram(grads, train_grad, other_grad)
    grad_part = lax.psum_scatter(grad_gram, "y", scatter_dimension=0, tiled=True)
    act_gram = gram(acts, train_act, other_act)
    act_part = lax.psum_scatter(act_gram, "y", scatter_dimension=0, tiled=True)

    half = act_part.shape[0] // 2

    def over_h(part):
        keep = lax.dynamic_slice_in_dim(part, h * half, half, 0)
        send = lax.dynamic_slice_in_dim(part, (1 - h) * half, half, 0)
        return keep + swap(send, "h")

    joint = over_h(act_part) * over_h(grad_part)
    behind = (y // 2) ^ (y // 4)
    first = (((x - behind) % NX * NZ + 2 * (y % 2) + h) * NC + c) * half
    seg = lax.dynamic_slice_in_dim(test_seg, first, half, 0)
    mask = lax.dynamic_slice_in_dim(test_mask, first, half, 0)
    test_onehot = (
        (seg[None, :] == jnp.arange(TEST_SEQS, dtype=jnp.int32)[:, None]) & (mask != 0)[None, :]
    ).astype(jnp.float32)
    rows = jnp.dot(test_onehot, joint, precision=lax.Precision.HIGHEST)
    n = train_act.shape[0]
    mine, theirs = rows[:, :n], rows[:, n:]
    ordered = jnp.where(
        c == 0, jnp.concatenate([mine, theirs], 1), jnp.concatenate([theirs, mine], 1)
    )
    total = lax.psum(ordered, ("y", "c"))
    total = lax.dynamic_slice_in_dim(total, c * n, n, 1)
    total = total + swap(total, "h")
    train_onehot = (
        (train_seg == jnp.arange(SEQ_PACK, dtype=jnp.int32)[:, None]) & (train_mask != 0)
    ).astype(jnp.float32)
    scores = lax.dot_general(
        train_onehot, total, (((1,), (1,)), ((), ())), precision=lax.Precision.HIGHEST
    )
    return scores * (1.0 / (SEG_LEN * math.sqrt(FF * D)))


def solution(mesh):
    fine = Mesh(mesh.devices.reshape(NX, NZ, NC, NY, NH), ("x", "z", "c", "y", "h"))
    return jax.shard_map(
        on_device,
        mesh=fine,
        in_specs=(P(DP, FFN), P(DP, FFN), P(DP, None), P(DP, None), P(DP, FFN), P(DP, FFN), P(), P()),
        out_specs=P(DP, None),
        check_vma=False,
    )
```

time: 506 us -> 211 us (0.42); the launches traced: 500 us -> 210 us
  waiting for transfers between devices: 428 us -> 56.6 us
  starting transfers between devices: 0.04 us -> 48 us
  blocking collectives: 43.6 us -> 76.8 us
  matrix products: 12.5 us -> 5.64 us
  local copies, waits for them, and re-layouts: 0.01 us -> 5.48 us
    psum x1 -> x0, waiting for transfers between devices: 405 us -> none  [on_device(): act_total, grad_total = lax.psum((act_gram, grad_gram), 'ffn')]
    ppermute x0 -> x11, starting transfers between devices: none -> 48 us  [the longest x5 28.1 us: swap(): return lax.ppermute(value, axis, [(0, 1), (1, 0)])]
    psum x0 -> x1, blocking collectives: none -> 45.7 us  [on_device(): total = lax.psum(ordered, ('y', 'c'))]
    reduce_scatter x0 -> x2, waiting for transfers between devices: none -> 39.6 us  [the longest x1 37.7 us: on_device(): act_part = lax.psum_scatter(act_gram, 'y', scatter_dimension=0, tiled=True)]
    all_gather x1 -> x0, waiting for transfers between devices: 22.4 us -> none  [on_device(): lax.all_gather(test_act, 'dp', axis=0, tiled=True)]
    ppermute x0 -> x11, waiting for transfers between devices: none -> 16.9 us  [the longest x6 12.9 us: over_x(): lax.ppermute(value, 'x', [(i, (i + step) % NX) for i in range(NX)])]
    all_gather x1 -> x2, blocking collectives: 43.6 us -> 31.1 us  [the longest x1 15.8 us: on_device(): grad_z = lax.all_gather(test_grad, 'z', axis=0, tiled=True)]
  transfers between devices with their start and end apart: 2 -> 13, of which waited for: 2 -> 7; matrix products, arithmetic and copies ran while one was open for 1% -> 5% of each run, Pallas kernels for 0% -> 0%
where the time goes in v1:
time: 211 us; the launch traced here: 210 us
  blocking collectives  76.8 us (36%)
  waiting for transfers between devices  56.6 us (27%)
  starting transfers between devices  48 us (23%)
  between operations  13.7 us (6%)
  matrix products  5.64 us (3%)
  local copies, waits for them, and re-layouts  5.48 us (3%)
  other arithmetic  3.84 us (2%)
    psum x1, blocking collectives, on_device(): total = lax.psum(ordered, ('y', 'c'))  45.7 us
    reduce_scatter x1, waiting for transfers between devices, on_device(): act_part = lax.psum_scatter(act_gram, 'y', scatter_dimension=0, tiled=True)  37.7 us
    ppermute x5, starting transfers between devices, swap(): return lax.ppermute(value, axis, [(0, 1), (1, 0)])  28.1 us
    ppermute x6, starting transfers between devices, over_x(): lax.ppermute(value, 'x', [(i, (i + step) % NX) for i in range(NX)])  19.9 us
    all_gather x1, blocking collectives, on_device(): grad_z = lax.all_gather(test_grad, 'z', axis=0, tiled=True)  15.8 us
    all_gather x1, blocking collectives, on_device(): act_z = lax.all_gather(test_act, 'z', axis=0, tiled=True)  15.3 us
    ppermute x6, waiting for transfers between devices, over_x(): lax.ppermute(value, 'x', [(i, (i + step) % NX) for i in range(NX)])  12.9 us
  transfers between devices with their start and end apart: 13, of which 7 were waited for; matrix products, arithmetic and copies ran while one was open for 5% of the time, Pallas kernels for 0%

profile of v1, /device:TPU:6, one launch (start us, length us, event | category | flops | bytes accessed | tf_op | source)
XLA Modules:
  0.0 210.1 jit_solution(5642928262486471949)
XLA Ops:
  6.5 1.9 collective-permute-start.5
  8.5 15.8 %all_gather.7 = bf16[128,320]{1,0:T(8,128)(2,1)S(1)} all-gather(bf16[32,320]{1,0:T(8,128)(2,1)} %param.13), channel_id=1, replica_groups=mesh['x'=4,'z'=4,'c'=2,'y'=8,'h'=2] {'z'}, dimensions={0}, use_global_device_ids=true | all-gather | bytes 102400 | tf_op jit(solution)/shard_map/all_gather | solution.py:38
  24.2 3.3 %collective-permute-start.8 = (bf16[128,320]{1,0:T(8,128)(2,1)S(1)}, bf16[128,320]{1,0:T(8,128)(2,1)S(1)}, u32[]{:S(2)}, u32[]{:S(2)}) collective-permute-start(bf16[128,320]{1,0:T(8,128)(2,1)S(1)} %all_gather.7), channel_id=1, source_target_pairs={{0,256},{128,384},{256,0},{384,128},{1,257},{129,385},{257,1},{385... | collective-permute-start | bytes 245768 | tf_op jit(solution)/shard_map/ppermute | solution.py:30
  27.5 5.1 %collective-permute-start.7 = (bf16[128,320]{1,0:T(8,128)(2,1)S(1)}, bf16[128,320]{1,0:T(8,128)(2,1)S(1)}, u32[]{:S(2)}, u32[]{:S(2)}) collective-permute-start(bf16[128,320]{1,0:T(8,128)(2,1)S(1)} %all_gather.7), channel_id=1, source_target_pairs={{0,384},{128,0},{256,128},{384,256},{1,385},{129,1},{257,129},{385... | collective-permute-start | bytes 245768 | tf_op jit(solution)/shard_map/ppermute | solution.py:30
  32.6 2.0 collective-permute-start.6
  36.6 2.5 %collective-permute-done.6 = bf16[128,320]{1,0:T(8,128)(2,1)S(1)} collective-permute-done((bf16[128,320]{1,0:T(8,128)(2,1)S(1)}, bf16[128,320]{1,0:T(8,128)(2,1)S(1)}, u32[]{:S(2)}, u32[]{:S(2)}) %collective-permute-start.6) | collective-permute-done | bytes 81952 | tf_op jit(solution)/shard_map/ppermute | solution.py:30
  39.5 1.6 pad_maximum_fusion.1
  41.1 1.4 copy-done
  42.5 1.9 collective-permute-start
  44.4 15.3 %all_gather.6 = bf16[128,1600]{1,0:T(8,128)(2,1)S(1)} all-gather(bf16[32,1600]{1,0:T(8,128)(2,1)S(1)} %copy-done.1), channel_id=1, replica_groups=mesh['x'=4,'z'=4,'c'=2,'y'=8,'h'=2] {'z'}, dimensions={0}, use_global_device_ids=true | all-gather | bytes 512000 | tf_op jit(solution)/shard_map/all_gather | solution.py:39
  59.7 2.5 %collective-permute-start.3 = (bf16[128,1600]{1,0:T(8,128)(2,1)S(1)}, bf16[128,1600]{1,0:T(8,128)(2,1)S(1)}, u32[]{:S(2)}, u32[]{:S(2)}) collective-permute-start(bf16[128,1600]{1,0:T(8,128)(2,1)S(1)} %all_gather.6), channel_id=1, source_target_pairs={{0,256},{128,384},{256,0},{384,128},{1,257},{129,385},{257,1},{385... | collective-permute-start | bytes 1228808 | tf_op jit(solution)/shard_map/ppermute | solution.py:30
  62.2 3.6 %collective-permute-start.2 = (bf16[128,1600]{1,0:T(8,128)(2,1)S(1)}, bf16[128,1600]{1,0:T(8,128)(2,1)S(1)}, u32[]{:S(2)}, u32[]{:S(2)}) collective-permute-start(bf16[128,1600]{1,0:T(8,128)(2,1)S(1)} %all_gather.6), channel_id=1, source_target_pairs={{0,384},{128,0},{256,128},{384,256},{1,385},{129,1},{257,129},{385... | collective-permute-start | bytes 1228808 | tf_op jit(solution)/shard_map/ppermute | solution.py:30
  65.9 3.4 %collective-permute-start.1 = (bf16[128,1600]{1,0:T(8,128)(2,1)S(1)}, bf16[128,1600]{1,0:T(8,128)(2,1)S(1)}, u32[]{:S(2)}, u32[]{:S(2)}) collective-permute-start(bf16[128,1600]{1,0:T(8,128)(2,1)S(1)} %all_gather.6), channel_id=1, source_target_pairs={{0,128},{128,256},{256,384},{384,0},{1,129},{129,257},{257,385},{3... | collective-permute-start | bytes 1228808 | tf_op jit(solution)/shard_map/ppermute | solution.py:30
  70.5 5.4 %collective-permute-done.3 = bf16[128,1600]{1,0:T(8,128)(2,1)S(1)} collective-permute-done((bf16[128,1600]{1,0:T(8,128)(2,1)S(1)}, bf16[128,1600]{1,0:T(8,128)(2,1)S(1)}, u32[]{:S(2)}, u32[]{:S(2)}) %collective-permute-start.3) | collective-permute-done | bytes 409632 | tf_op jit(solution)/shard_map/ppermute | solution.py:30
  76.6 4.9 %collective-permute-done.2 = bf16[128,1600]{1,0:T(8,128)(2,1)S(1)} collective-permute-done((bf16[128,1600]{1,0:T(8,128)(2,1)S(1)}, bf16[128,1600]{1,0:T(8,128)(2,1)S(1)}, u32[]{:S(2)}, u32[]{:S(2)}) %collective-permute-start.2) | collective-permute-done | bytes 409632 | tf_op jit(solution)/shard_map/ppermute | solution.py:30
  82.8 1.5 pad_maximum_fusion
  84.3 1.9 reduce-scatter.5.cloned.1.call-done
  87.2 7.9 %collective-permute-start.9 = (f32[32,1024]{1,0:T(8,128)S(1)}, f32[32,1024]{1,0:T(8,128)S(1)}, u32[]{:S(2)}, u32[]{:S(2)}) collective-permute-start(f32[32,1024]{1,0:T(8,128)S(1)} %constant_dynamic-slice_fusion), channel_id=1, source_target_pairs={{0,1},{1,0},{2,3},{3,2},{4,5},{5,4},{6,7},{7,6},{8,9},{9,8},{10,11... | collective-permute-start | bytes 393224 | tf_op jit(solution)/shard_map/ppermute | solution.py:25
  95.1 37.7 %reduce-scatter.3.cloned.1.call-done = f32[64,1024]{1,0:T(8,128)} async-done(((f32[512,1024]{1,0:T(8,128)}), f32[64,1024]{1,0:T(8,128)}) %reduce-scatter.3.cloned.1.call-update) | async-done | bytes 262160 | tf_op jit(solution)/shard_map/reduce_scatter | solution.py:51
  133.8 8.1 %collective-permute-start.4 = (f32[32,1024]{1,0:T(8,128)S(1)}, f32[32,1024]{1,0:T(8,128)S(1)}, u32[]{:S(2)}, u32[]{:S(2)}) collective-permute-start(f32[32,1024]{1,0:T(8,128)S(1)} %constant_dynamic-slice_fusion.1), channel_id=1, source_target_pairs={{0,1},{1,0},{2,3},{3,2},{4,5},{5,4},{6,7},{7,6},{8,9},{9,8},{10,11... | collective-permute-start | bytes 393224 | tf_op jit(solution)/shard_map/ppermute | solution.py:25
  143.4 2.3 %collective-permute-done.4 = f32[32,1024]{1,0:T(8,128)S(1)} collective-permute-done((f32[32,1024]{1,0:T(8,128)S(1)}, f32[32,1024]{1,0:T(8,128)S(1)}, u32[]{:S(2)}, u32[]{:S(2)}) %collective-permute-start.4) | collective-permute-done | bytes 131104 | tf_op jit(solution)/shard_map/ppermute | solution.py:25
  146.9 45.7 %psum.7 = f32[8,1024]{1,0:T(8,128)S(1)} all-reduce(f32[8,1024]{1,0:T(8,128)S(1)} %maximum_select_fusion), channel_id=1, replica_groups=mesh['x'=4,'z'=4,'c'=2,'y'=8,'h'=2] {'y','c'}, use_global_device_ids=true, to_apply=%region_2.3 | all-reduce | flops 8192 | bytes 65536 | tf_op jit(solution)/shard_map/psum | solution.py:74
  192.6 8.2 %collective-permute-start.10 = (f32[8,512]{1,0:T(8,128)S(1)}, f32[8,512]{1,0:T(8,128)S(1)}, u32[]{:S(2)}, u32[]{:S(2)}) collective-permute-start(f32[8,512]{1,0:T(8,128)S(1)} %constant_dynamic-slice_fusion.2), channel_id=1, source_target_pairs={{0,1},{1,0},{2,3},{3,2},{4,5},{5,4},{6,7},{7,6},{8,9},{9,8},{10,11... | collective-permute-start | bytes 49160 | tf_op jit(solution)/shard_map/ppermute | solution.py:25
  200.9 1.7 collective-permute-done.10
  (39 shorter events, 10.6 us)
Async XLA Ops:
  6.5 79.7 %reduce-scatter.5.cloned.1.call-start = ((), (), s32[]{:S(2)}) async-start(), calls=%async_computation.3 | async-start | bytes 2359296 | tf_op jit(solution)/shard_map/reduce_scatter | solution.py:49
  6.5 29.1 %collective-permute-start.5 = (bf16[512,320]{0,1:T(8,128)(2,1)}, bf16[512,320]{0,1:T(8,128)(2,1)S(1)}, u32[]{:S(2)}, u32[]{:S(2)}) collective-permute-start(bf16[512,320]{0,1:T(8,128)(2,1)} %param.9), channel_id=1, source_target_pairs={{0,16},{16,0},{1,17},{17,1},{2,18},{18,2},{3,19},{19,3},{4,20},{20... | collective-permute-start | bytes 983048 | tf_op jit(solution)/shard_map/ppermute | solution.py:25
  24.2 11.8 %collective-permute-start.8 = (bf16[128,320]{1,0:T(8,128)(2,1)S(1)}, bf16[128,320]{1,0:T(8,128)(2,1)S(1)}, u32[]{:S(2)}, u32[]{:S(2)}) collective-permute-start(bf16[128,320]{1,0:T(8,128)(2,1)S(1)} %all_gather.7), channel_id=1, source_target_pairs={{0,256},{128,384},{256,0},{384,128},{1,257},{129,385},{257,1},{385... | collective-permute-start | bytes 245768 | tf_op jit(solution)/shard_map/ppermute | solution.py:30
  27.5 8.8 %collective-permute-start.7 = (bf16[128,320]{1,0:T(8,128)(2,1)S(1)}, bf16[128,320]{1,0:T(8,128)(2,1)S(1)}, u32[]{:S(2)}, u32[]{:S(2)}) collective-permute-start(bf16[128,320]{1,0:T(8,128)(2,1)S(1)} %all_gather.7), channel_id=1, source_target_pairs={{0,384},{128,0},{256,128},{384,256},{1,385},{129,1},{257,129},{385... | collective-permute-start | bytes 245768 | tf_op jit(solution)/shard_map/ppermute | solution.py:30
  32.6 6.5 %collective-permute-start.6 = (bf16[128,320]{1,0:T(8,128)(2,1)S(1)}, bf16[128,320]{1,0:T(8,128)(2,1)S(1)}, u32[]{:S(2)}, u32[]{:S(2)}) collective-permute-start(bf16[128,320]{1,0:T(8,128)(2,1)S(1)} %all_gather.7), channel_id=1, source_target_pairs={{0,128},{128,256},{256,384},{384,0},{1,129},{129,257},{257,385},{3... | collective-permute-start | bytes 245768 | tf_op jit(solution)/shard_map/ppermute | solution.py:30
  41.0 1.4 copy-start
  41.0 3.3 %copy-start.1 = (bf16[32,1600]{1,0:T(8,128)(2,1)S(1)}, bf16[32,1600]{1,0:T(8,128)(2,1)}, u32[]{:S(2)}) copy-start(bf16[32,1600]{1,0:T(8,128)(2,1)} %param.12) | copy-start | bytes 307204
  41.1 91.8 %reduce-scatter.3.cloned.1.call-start = ((), (), s32[]{:S(2)}) async-start(), calls=%async_computation.2 | async-start | bytes 2359296 | tf_op jit(solution)/shard_map/reduce_scatter | solution.py:51
  42.5 27.1 %collective-permute-start = (bf16[512,1600]{0,1:T(8,128)(2,1)S(1)}, bf16[512,1600]{0,1:T(8,128)(2,1)S(1)}, u32[]{:S(2)}, u32[]{:S(2)}) collective-permute-start(bf16[512,1600]{0,1:T(8,128)(2,1)S(1)} %copy-done), channel_id=1, source_target_pairs={{0,16},{16,0},{1,17},{17,1},{2,18},{18,2},{3,19},{19,3},{4,20},{20... | collective-permute-start | bytes 4915208 | tf_op jit(solution)/shard_map/ppermute | solution.py:25
  59.7 16.2 %collective-permute-start.3 = (bf16[128,1600]{1,0:T(8,128)(2,1)S(1)}, bf16[128,1600]{1,0:T(8,128)(2,1)S(1)}, u32[]{:S(2)}, u32[]{:S(2)}) collective-permute-start(bf16[128,1600]{1,0:T(8,128)(2,1)S(1)} %all_gather.6), channel_id=1, source_target_pairs={{0,256},{128,384},{256,0},{384,128},{1,257},{129,385},{257,1},{385... | collective-permute-start | bytes 1228808 | tf_op jit(solution)/shard_map/ppermute | solution.py:30
  62.2 19.3 %collective-permute-start.2 = (bf16[128,1600]{1,0:T(8,128)(2,1)S(1)}, bf16[128,1600]{1,0:T(8,128)(2,1)S(1)}, u32[]{:S(2)}, u32[]{:S(2)}) collective-permute-start(bf16[128,1600]{1,0:T(8,128)(2,1)S(1)} %all_gather.6), channel_id=1, source_target_pairs={{0,384},{128,0},{256,128},{384,256},{1,385},{129,1},{257,129},{385... | collective-permute-start | bytes 1228808 | tf_op jit(solution)/shard_map/ppermute | solution.py:30
  65.9 16.3 %collective-permute-start.1 = (bf16[128,1600]{1,0:T(8,128)(2,1)S(1)}, bf16[128,1600]{1,0:T(8,128)(2,1)S(1)}, u32[]{:S(2)}, u32[]{:S(2)}) collective-permute-start(bf16[128,1600]{1,0:T(8,128)(2,1)S(1)} %all_gather.6), channel_id=1, source_target_pairs={{0,128},{128,256},{256,384},{384,0},{1,129},{129,257},{257,385},{3... | collective-permute-start | bytes 1228808 | tf_op jit(solution)/shard_map/ppermute | solution.py:30
  84.3 116.5 %copy-start.3 = (s32[1,512]{1,0:T(1,128)S(1)}, s32[1,512]{1,0:T(1,128)}, u32[]{:S(2)}) copy-start(s32[1,512]{1,0:T(1,128)} %param.11) | copy-start | bytes 6148
  84.3 118.3 %copy-start.2 = (s32[1,512]{1,0:T(1,128)S(1)}, s32[1,512]{1,0:T(1,128)}, u32[]{:S(2)}) copy-start(s32[1,512]{1,0:T(1,128)} %param.10) | copy-start | bytes 6148
  87.2 56.2 %collective-permute-start.9 = (f32[32,1024]{1,0:T(8,128)S(1)}, f32[32,1024]{1,0:T(8,128)S(1)}, u32[]{:S(2)}, u32[]{:S(2)}) collective-permute-start(f32[32,1024]{1,0:T(8,128)S(1)} %constant_dynamic-slice_fusion), channel_id=1, source_target_pairs={{0,1},{1,0},{2,3},{3,2},{4,5},{5,4},{6,7},{7,6},{8,9},{9,8},{10,11... | collective-permute-start | bytes 393224 | tf_op jit(solution)/shard_map/ppermute | solution.py:25
  133.8 12.0 %collective-permute-start.4 = (f32[32,1024]{1,0:T(8,128)S(1)}, f32[32,1024]{1,0:T(8,128)S(1)}, u32[]{:S(2)}, u32[]{:S(2)}) collective-permute-start(f32[32,1024]{1,0:T(8,128)S(1)} %constant_dynamic-slice_fusion.1), channel_id=1, source_target_pairs={{0,1},{1,0},{2,3},{3,2},{4,5},{5,4},{6,7},{7,6},{8,9},{9,8},{10,11... | collective-permute-start | bytes 393224 | tf_op jit(solution)/shard_map/ppermute | solution.py:25
  192.6 10.0 %collective-permute-start.10 = (f32[8,512]{1,0:T(8,128)S(1)}, f32[8,512]{1,0:T(8,128)S(1)}, u32[]{:S(2)}, u32[]{:S(2)}) collective-permute-start(f32[8,512]{1,0:T(8,128)S(1)} %constant_dynamic-slice_fusion.2), channel_id=1, source_target_pairs={{0,1},{1,0},{2,3},{3,2},{4,5},{5,4},{6,7},{7,6},{8,9},{9,8},{10,11... | collective-permute-start | bytes 49160 | tf_op jit(solution)/shard_map/ppermute | solution.py:25
Sparse Core Ops, SparseCore 0:
  41.2 45.0 reduce-scatter.4
  89.1 43.6 reduce-scatter.2

commit v2 on v1

--- a/solution.py
+++ b/solution.py
@@ -35,8 +35,9 @@
     train_act, train_grad, train_seg, train_mask, test_act, test_grad, test_seg, test_mask
 ):
     x, y, h, c = (lax.axis_index(a) for a in ("x", "y", "h", "c"))
-    grad_z = lax.all_gather(test_grad, "z", axis=0, tiled=True)
-    act_z = lax.all_gather(test_act, "z", axis=0, tiled=True)
+    wide = test_act.shape[1]
+    both_z = lax.all_gather(jnp.concatenate([test_act, test_grad], 1), "z", axis=0, tiled=True)
+    act_z, grad_z = both_z[:, :wide], both_z[:, wide:]
     other_grad, other_act = swap(train_grad, "c"), swap(train_act, "c")
     grads = over_x(grad_z)
     acts = over_x(act_z)
@@ -68,18 +69,15 @@
     rows = jnp.dot(test_onehot, joint, precision=lax.Precision.HIGHEST)
     n = train_act.shape[0]
     mine, theirs = rows[:, :n], rows[:, n:]
-    ordered = jnp.where(
-        c == 0, jnp.concatenate([mine, theirs], 1), jnp.concatenate([theirs, mine], 1)
-    )
-    total = lax.psum(ordered, ("y", "c"))
-    total = lax.dynamic_slice_in_dim(total, c * n, n, 1)
-    total = total + swap(total, "h")
+    total = mine + swap(theirs, "c")
     train_onehot = (
         (train_seg == jnp.arange(SEQ_PACK, dtype=jnp.int32)[:, None]) & (train_mask != 0)
     ).astype(jnp.float32)
     scores = lax.dot_general(
         train_onehot, total, (((1,), (1,)), ((), ())), precision=lax.Precision.HIGHEST
     )
+    scores = lax.psum(scores, "y")
+    scores = scores + swap(scores, "h")
     return scores * (1.0 / (SEG_LEN * math.sqrt(FF * D)))
 
 

time: 211 us -> 188 us (0.89)
  blocking collectives: 76.8 us -> 34.5 us
  waiting for transfers between devices: 56.6 us -> 72.2 us
  starting transfers between devices: 48 us -> 51 us
    psum x1, blocking collectives: 45.7 us -> 16 us  [on_device(): scores = lax.psum(scores, 'y')]
    all_gather x2 -> x1, blocking collectives: 31.1 us -> 18.5 us  [on_device(): lax.all_gather(jnp.concatenate([test_act, test_grad], 1), 'z', axis=0, ti...]
    reduce_scatter x1, waiting for transfers between devices: 1.93 us -> 9.83 us  [on_device(): lax.psum_scatter(grad_gram, 'y', scatter_dimension=0, tiled=True)]
    ppermute x6, waiting for transfers between devices: 12.9 us -> 19.6 us  [over_x(): lax.ppermute(value, 'x', [(i, (i + step) % NX) for i in range(NX)])]
    ppermute x5 -> x6, starting transfers between devices: 28.1 us -> 30.1 us  [swap(): return lax.ppermute(value, axis, [(0, 1), (1, 0)])]
    ppermute x5 -> x6, waiting for transfers between devices: 3.98 us -> 4.95 us  [swap(): return lax.ppermute(value, axis, [(0, 1), (1, 0)])]
  transfers between devices with their start and end apart: 13 -> 14, of which waited for: 7 -> 9; matrix products, arithmetic and copies ran while one was open for 5% -> 6% of each run, Pallas kernels for 0% -> 0%
where the time goes in v2:
time: 188 us
  waiting for transfers between devices  72.2 us (38%)
  starting transfers between devices  51 us (27%)
  blocking collectives  34.5 us (18%)
  between operations  13.7 us (7%)
  local copies, waits for them, and re-layouts  5.6 us (3%)
  other arithmetic  5.41 us (3%)
  matrix products  5.11 us (3%)
    reduce_scatter x1, waiting for transfers between devices, on_device(): act_part = lax.psum_scatter(act_gram, 'y', scatter_dimension=0, tiled=True)  37.8 us
    ppermute x6, starting transfers between devices, swap(): return lax.ppermute(value, axis, [(0, 1), (1, 0)])  30.1 us
    ppermute x6, starting transfers between devices, over_x(): lax.ppermute(value, 'x', [(i, (i + step) % NX) for i in range(NX)])  20.9 us
    ppermute x6, waiting for transfers between devices, over_x(): lax.ppermute(value, 'x', [(i, (i + step) % NX) for i in range(NX)])  19.6 us
    all_gather x1, blocking collectives, on_device(): lax.all_gather(jnp.concatenate([test_act, test_grad], 1), 'z', axis=0, ti...  18.5 us
    psum x1, blocking collectives, on_device(): scores = lax.psum(scores, 'y')  16 us
    reduce_scatter x1, waiting for transfers between devices, on_device(): lax.psum_scatter(grad_gram, 'y', scatter_dimension=0, tiled=True)  9.83 us
    ppermute x6, waiting for transfers between devices, swap(): return lax.ppermute(value, axis, [(0, 1), (1, 0)])  4.95 us
  transfers between devices with their start and end apart: 14, of which 9 were waited for; matrix products, arithmetic and copies ran while one was open for 6% of the time, Pallas kernels for 0%

profile of v2, /device:TPU:6, one launch (start us, length us, event | category | flops | bytes accessed | tf_op | source)
XLA Modules:
  0.0 187.5 jit_solution(8072992891867748963)
XLA Ops:
  6.5 1.9 %collective-permute-start.5 = (bf16[512,320]{0,1:T(8,128)(2,1)}, bf16[512,320]{0,1:T(8,128)(2,1)S(1)}, u32[]{:S(2)}, u32[]{:S(2)}) collective-permute-start(bf16[512,320]{0,1:T(8,128)(2,1)} %param.9), channel_id=1, source_target_pairs={{0,16},{16,0},{1,17},{17,1},{2,18},{18,2},{3,19},{19,3},{4,20},{20... | collective-permute-start | bytes 983048 | tf_op jit(solution)/shard_map/ppermute | solution.py:25
  9.5 18.5 %all_gather.3 = bf16[128,1920]{1,0:T(8,128)(2,1)S(1)} all-gather(bf16[32,1920]{1,0:T(8,128)(2,1)S(1)} %pad_maximum_fusion.2), channel_id=1, replica_groups=mesh['x'=4,'z'=4,'c'=2,'y'=8,'h'=2] {'z'}, dimensions={0}, use_global_device_ids=true | all-gather | bytes 614400 | tf_op jit(solution)/shard_map/all_gather | solution.py:39
  28.0 5.2 %collective-permute-start.6 = (bf16[128,320]{1,0:T(8,128)(2,1)S(1)}, bf16[128,320]{1,0:T(8,128)(2,1)S(1)}, u32[]{:S(2)}, u32[]{:S(2)}) collective-permute-start(bf16[128,320]{1,0:T(8,128)(2,1)S(1)} %slice.17), channel_id=1, source_target_pairs={{0,128},{128,256},{256,384},{384,0},{1,129},{129,257},{257,385},{3... | collective-permute-start | bytes 245768 | tf_op jit(solution)/shard_map/ppermute | solution.py:30
  33.2 1.9 %collective-permute-start.7 = (bf16[128,320]{1,0:T(8,128)(2,1)S(1)}, bf16[128,320]{1,0:T(8,128)(2,1)S(1)}, u32[]{:S(2)}, u32[]{:S(2)}) collective-permute-start(bf16[128,320]{1,0:T(8,128)(2,1)S(1)} %slice.17), channel_id=1, source_target_pairs={{0,384},{128,0},{256,128},{384,256},{1,385},{129,1},{257,129},{385... | collective-permute-start | bytes 245768 | tf_op jit(solution)/shard_map/ppermute | solution.py:30
  35.2 3.4 %collective-permute-start.8 = (bf16[128,320]{1,0:T(8,128)(2,1)S(1)}, bf16[128,320]{1,0:T(8,128)(2,1)S(1)}, u32[]{:S(2)}, u32[]{:S(2)}) collective-permute-start(bf16[128,320]{1,0:T(8,128)(2,1)S(1)} %slice.17), channel_id=1, source_target_pairs={{0,256},{128,384},{256,0},{384,128},{1,257},{129,385},{257,1},{385... | collective-permute-start | bytes 245768 | tf_op jit(solution)/shard_map/ppermute | solution.py:30
  41.6 1.6 collective-permute-done.8
  43.5 1.6 pad_maximum_fusion.1
  45.1 1.4 copy-done
  46.5 1.9 %collective-permute-start = (bf16[512,1600]{0,1:T(8,128)(2,1)S(1)}, bf16[512,1600]{0,1:T(8,128)(2,1)S(1)}, u32[]{:S(2)}, u32[]{:S(2)}) collective-permute-start(bf16[512,1600]{0,1:T(8,128)(2,1)S(1)} %copy-done), channel_id=1, source_target_pairs={{0,16},{16,0},{1,17},{17,1},{2,18},{18,2},{3,19},{19,3},{4,20},{20... | collective-permute-start | bytes 4915208 | tf_op jit(solution)/shard_map/ppermute | solution.py:25
  48.5 5.1 %collective-permute-start.1 = (bf16[128,1600]{1,0:T(8,128)(2,1)S(1)}, bf16[128,1600]{1,0:T(8,128)(2,1)S(1)}, u32[]{:S(2)}, u32[]{:S(2)}) collective-permute-start(bf16[128,1600]{1,0:T(8,128)(2,1)S(1)} %slice.16), channel_id=1, source_target_pairs={{0,128},{128,256},{256,384},{384,0},{1,129},{129,257},{257,385},{3... | collective-permute-start | bytes 1228808 | tf_op jit(solution)/shard_map/ppermute | solution.py:30
  53.6 1.9 %collective-permute-start.2 = (bf16[128,1600]{1,0:T(8,128)(2,1)S(1)}, bf16[128,1600]{1,0:T(8,128)(2,1)S(1)}, u32[]{:S(2)}, u32[]{:S(2)}) collective-permute-start(bf16[128,1600]{1,0:T(8,128)(2,1)S(1)} %slice.16), channel_id=1, source_target_pairs={{0,384},{128,0},{256,128},{384,256},{1,385},{129,1},{257,129},{385... | collective-permute-start | bytes 1228808 | tf_op jit(solution)/shard_map/ppermute | solution.py:30
  55.5 3.4 %collective-permute-start.3 = (bf16[128,1600]{1,0:T(8,128)(2,1)S(1)}, bf16[128,1600]{1,0:T(8,128)(2,1)S(1)}, u32[]{:S(2)}, u32[]{:S(2)}) collective-permute-start(bf16[128,1600]{1,0:T(8,128)(2,1)S(1)} %slice.16), channel_id=1, source_target_pairs={{0,256},{128,384},{256,0},{384,128},{1,257},{129,385},{257,1},{385... | collective-permute-start | bytes 1228808 | tf_op jit(solution)/shard_map/ppermute | solution.py:30
  60.1 12.3 %collective-permute-done.1 = bf16[128,1600]{1,0:T(8,128)(2,1)S(1)} collective-permute-done((bf16[128,1600]{1,0:T(8,128)(2,1)S(1)}, bf16[128,1600]{1,0:T(8,128)(2,1)S(1)}, u32[]{:S(2)}, u32[]{:S(2)}) %collective-permute-start.1) | collective-permute-done | bytes 409632 | tf_op jit(solution)/shard_map/ppermute | solution.py:30
  73.1 4.7 %collective-permute-done.2 = bf16[128,1600]{1,0:T(8,128)(2,1)S(1)} collective-permute-done((bf16[128,1600]{1,0:T(8,128)(2,1)S(1)}, bf16[128,1600]{1,0:T(8,128)(2,1)S(1)}, u32[]{:S(2)}, u32[]{:S(2)}) %collective-permute-start.2) | collective-permute-done | bytes 409632 | tf_op jit(solution)/shard_map/ppermute | solution.py:30
  79.1 1.5 pad_maximum_fusion
  80.6 9.8 %reduce-scatter.5.cloned.1.call-done = f32[64,1024]{1,0:T(8,128)} async-done(((f32[512,1024]{1,0:T(8,128)}), f32[64,1024]{1,0:T(8,128)}) %reduce-scatter.5.cloned.1.call-update) | async-done | bytes 262160 | tf_op jit(solution)/shard_map/reduce_scatter | solution.py:50
  91.3 8.1 %collective-permute-start.9 = (f32[32,1024]{1,0:T(8,128)S(1)}, f32[32,1024]{1,0:T(8,128)S(1)}, u32[]{:S(2)}, u32[]{:S(2)}) collective-permute-start(f32[32,1024]{1,0:T(8,128)S(1)} %constant_dynamic-slice_fusion.1), channel_id=1, source_target_pairs={{0,1},{1,0},{2,3},{3,2},{4,5},{5,4},{6,7},{7,6},{8,9},{9,8},{10,11... | collective-permute-start | bytes 393224 | tf_op jit(solution)/shard_map/ppermute | solution.py:25
  99.4 37.8 %reduce-scatter.3.cloned.1.call-done = f32[64,1024]{1,0:T(8,128)} async-done(((f32[512,1024]{1,0:T(8,128)}), f32[64,1024]{1,0:T(8,128)}) %reduce-scatter.3.cloned.1.call-update) | async-done | bytes 262160 | tf_op jit(solution)/shard_map/reduce_scatter | solution.py:52
  138.1 8.0 %collective-permute-start.4 = (f32[32,1024]{1,0:T(8,128)S(1)}, f32[32,1024]{1,0:T(8,128)S(1)}, u32[]{:S(2)}, u32[]{:S(2)}) collective-permute-start(f32[32,1024]{1,0:T(8,128)S(1)} %constant_dynamic-slice_fusion), channel_id=1, source_target_pairs={{0,1},{1,0},{2,3},{3,2},{4,5},{5,4},{6,7},{7,6},{8,9},{9,8},{10,11... | collective-permute-start | bytes 393224 | tf_op jit(solution)/shard_map/ppermute | solution.py:25
  147.7 2.3 %collective-permute-done.4 = f32[32,1024]{1,0:T(8,128)S(1)} collective-permute-done((f32[32,1024]{1,0:T(8,128)S(1)}, f32[32,1024]{1,0:T(8,128)S(1)}, u32[]{:S(2)}, u32[]{:S(2)}) %collective-permute-start.4) | collective-permute-done | bytes 131104 | tf_op jit(solution)/shard_map/ppermute | solution.py:25
  151.1 1.9 %collective-permute-start.10 = (f32[8,512]{1,0:T(8,128)S(1)}, f32[8,512]{1,0:T(8,128)S(1)}, u32[]{:S(2)}, u32[]{:S(2)}) collective-permute-start(f32[8,512]{1,0:T(8,128)S(1)} %slice.19), channel_id=1, source_target_pairs={{0,16},{16,0},{1,17},{17,1},{2,18},{18,2},{3,19},{19,3},{4,20},{20... | collective-permute-start | bytes 49160 | tf_op jit(solution)/shard_map/ppermute | solution.py:25
  154.3 16.0 %psum.7 = f32[4,8]{1,0:T(4,128)S(1)} all-reduce(f32[4,8]{1,0:T(4,128)S(1)} %fusion.6), channel_id=1, replica_groups=mesh['x'=4,'z'=4,'c'=2,'y'=8,'h'=2] {'y'}, use_global_device_ids=true, to_apply=%region_2.3 | all-reduce | flops 32 | bytes 256 | tf_op jit(solution)/shard_map/psum | solution.py:79
  170.3 8.3 %collective-permute-start.11 = (f32[4,8]{1,0:T(4,128)S(1)}, f32[4,8]{1,0:T(4,128)S(1)}, u32[]{:S(2)}, u32[]{:S(2)}) collective-permute-start(f32[4,8]{1,0:T(4,128)S(1)} %psum.7), channel_id=1, source_target_pairs={{0,1},{1,0},{2,3},{3,2},{4,5},{5,4},{6,7},{7,6},{8,9},{9,8},{10,11... | collective-permute-start | bytes 392 | tf_op jit(solution)/shard_map/ppermute | solution.py:25
  178.6 1.5 collective-permute-done.11
  (40 shorter events, 14.0 us)
Async XLA Ops:
  6.5 83.9 %reduce-scatter.5.cloned.1.call-start = ((), (), s32[]{:S(2)}) async-start(), calls=%async_computation.3 | async-start | bytes 2359296 | tf_op jit(solution)/shard_map/reduce_scatter | solution.py:50
  6.5 33.0 %collective-permute-start.5 = (bf16[512,320]{0,1:T(8,128)(2,1)}, bf16[512,320]{0,1:T(8,128)(2,1)S(1)}, u32[]{:S(2)}, u32[]{:S(2)}) collective-permute-start(bf16[512,320]{0,1:T(8,128)(2,1)} %param.9), channel_id=1, source_target_pairs={{0,16},{16,0},{1,17},{17,1},{2,18},{18,2},{3,19},{19,3},{4,20},{20... | collective-permute-start | bytes 983048 | tf_op jit(solution)/shard_map/ppermute | solution.py:25
  28.0 11.9 %collective-permute-start.6 = (bf16[128,320]{1,0:T(8,128)(2,1)S(1)}, bf16[128,320]{1,0:T(8,128)(2,1)S(1)}, u32[]{:S(2)}, u32[]{:S(2)}) collective-permute-start(bf16[128,320]{1,0:T(8,128)(2,1)S(1)} %slice.17), channel_id=1, source_target_pairs={{0,128},{128,256},{256,384},{384,0},{1,129},{129,257},{257,385},{3... | collective-permute-start | bytes 245768 | tf_op jit(solution)/shard_map/ppermute | solution.py:30
  33.2 8.1 %collective-permute-start.7 = (bf16[128,320]{1,0:T(8,128)(2,1)S(1)}, bf16[128,320]{1,0:T(8,128)(2,1)S(1)}, u32[]{:S(2)}, u32[]{:S(2)}) collective-permute-start(bf16[128,320]{1,0:T(8,128)(2,1)S(1)} %slice.17), channel_id=1, source_target_pairs={{0,384},{128,0},{256,128},{384,256},{1,385},{129,1},{257,129},{385... | collective-permute-start | bytes 245768 | tf_op jit(solution)/shard_map/ppermute | solution.py:30
  35.2 8.0 %collective-permute-start.8 = (bf16[128,320]{1,0:T(8,128)(2,1)S(1)}, bf16[128,320]{1,0:T(8,128)(2,1)S(1)}, u32[]{:S(2)}, u32[]{:S(2)}) collective-permute-start(bf16[128,320]{1,0:T(8,128)(2,1)S(1)} %slice.17), channel_id=1, source_target_pairs={{0,256},{128,384},{256,0},{384,128},{1,257},{129,385},{257,1},{385... | collective-permute-start | bytes 245768 | tf_op jit(solution)/shard_map/ppermute | solution.py:30
  45.1 1.4 copy-start
  45.1 92.1 %reduce-scatter.3.cloned.1.call-start = ((), (), s32[]{:S(2)}) async-start(), calls=%async_computation.2 | async-start | bytes 2359296 | tf_op jit(solution)/shard_map/reduce_scatter | solution.py:52
  46.5 12.7 %collective-permute-start = (bf16[512,1600]{0,1:T(8,128)(2,1)S(1)}, bf16[512,1600]{0,1:T(8,128)(2,1)S(1)}, u32[]{:S(2)}, u32[]{:S(2)}) collective-permute-start(bf16[512,1600]{0,1:T(8,128)(2,1)S(1)} %copy-done), channel_id=1, source_target_pairs={{0,16},{16,0},{1,17},{17,1},{2,18},{18,2},{3,19},{19,3},{4,20},{20... | collective-permute-start | bytes 4915208 | tf_op jit(solution)/shard_map/ppermute | solution.py:25
  48.5 24.0 %collective-permute-start.1 = (bf16[128,1600]{1,0:T(8,128)(2,1)S(1)}, bf16[128,1600]{1,0:T(8,128)(2,1)S(1)}, u32[]{:S(2)}, u32[]{:S(2)}) collective-permute-start(bf16[128,1600]{1,0:T(8,128)(2,1)S(1)} %slice.16), channel_id=1, source_target_pairs={{0,128},{128,256},{256,384},{384,0},{1,129},{129,257},{257,385},{3... | collective-permute-start | bytes 1228808 | tf_op jit(solution)/shard_map/ppermute | solution.py:30
  53.6 24.2 %collective-permute-start.2 = (bf16[128,1600]{1,0:T(8,128)(2,1)S(1)}, bf16[128,1600]{1,0:T(8,128)(2,1)S(1)}, u32[]{:S(2)}, u32[]{:S(2)}) collective-permute-start(bf16[128,1600]{1,0:T(8,128)(2,1)S(1)} %slice.16), channel_id=1, source_target_pairs={{0,384},{128,0},{256,128},{384,256},{1,385},{129,1},{257,129},{385... | collective-permute-start | bytes 1228808 | tf_op jit(solution)/shard_map/ppermute | solution.py:30
  55.5 22.9 %collective-permute-start.3 = (bf16[128,1600]{1,0:T(8,128)(2,1)S(1)}, bf16[128,1600]{1,0:T(8,128)(2,1)S(1)}, u32[]{:S(2)}, u32[]{:S(2)}) collective-permute-start(bf16[128,1600]{1,0:T(8,128)(2,1)S(1)} %slice.16), channel_id=1, source_target_pairs={{0,256},{128,384},{256,0},{384,128},{1,257},{129,385},{257,1},{385... | collective-permute-start | bytes 1228808 | tf_op jit(solution)/shard_map/ppermute | solution.py:30
  80.5 72.5 %copy-start.2 = (s32[1,512]{1,0:T(1,128)S(1)}, s32[1,512]{1,0:T(1,128)}, u32[]{:S(2)}) copy-start(s32[1,512]{1,0:T(1,128)} %param.11) | copy-start | bytes 6148
  80.5 73.7 %copy-start.1 = (s32[1,512]{1,0:T(1,128)S(1)}, s32[1,512]{1,0:T(1,128)}, u32[]{:S(2)}) copy-start(s32[1,512]{1,0:T(1,128)} %param.10) | copy-start | bytes 6148
  91.3 56.4 %collective-permute-start.9 = (f32[32,1024]{1,0:T(8,128)S(1)}, f32[32,1024]{1,0:T(8,128)S(1)}, u32[]{:S(2)}, u32[]{:S(2)}) collective-permute-start(f32[32,1024]{1,0:T(8,128)S(1)} %constant_dynamic-slice_fusion.1), channel_id=1, source_target_pairs={{0,1},{1,0},{2,3},{3,2},{4,5},{5,4},{6,7},{7,6},{8,9},{9,8},{10,11... | collective-permute-start | bytes 393224 | tf_op jit(solution)/shard_map/ppermute | solution.py:25
  138.1 11.8 %collective-permute-start.4 = (f32[32,1024]{1,0:T(8,128)S(1)}, f32[32,1024]{1,0:T(8,128)S(1)}, u32[]{:S(2)}, u32[]{:S(2)}) collective-permute-start(f32[32,1024]{1,0:T(8,128)S(1)} %constant_dynamic-slice_fusion), channel_id=1, source_target_pairs={{0,1},{1,0},{2,3},{3,2},{4,5},{5,4},{6,7},{7,6},{8,9},{9,8},{10,11... | collective-permute-start | bytes 393224 | tf_op jit(solution)/shard_map/ppermute | solution.py:25
  151.1 3.1 %collective-permute-start.10 = (f32[8,512]{1,0:T(8,128)S(1)}, f32[8,512]{1,0:T(8,128)S(1)}, u32[]{:S(2)}, u32[]{:S(2)}) collective-permute-start(f32[8,512]{1,0:T(8,128)S(1)} %slice.19), channel_id=1, source_target_pairs={{0,16},{16,0},{1,17},{17,1},{2,18},{18,2},{3,19},{19,3},{4,20},{20... | collective-permute-start | bytes 49160 | tf_op jit(solution)/shard_map/ppermute | solution.py:25
  170.3 9.8 %collective-permute-start.11 = (f32[4,8]{1,0:T(4,128)S(1)}, f32[4,8]{1,0:T(4,128)S(1)}, u32[]{:S(2)}, u32[]{:S(2)}) collective-permute-start(f32[4,8]{1,0:T(4,128)S(1)} %psum.7), channel_id=1, source_target_pairs={{0,1},{1,0},{2,3},{3,2},{4,5},{5,4},{6,7},{7,6},{8,9},{9,8},{10,11... | collective-permute-start | bytes 392 | tf_op jit(solution)/shard_map/ppermute | solution.py:25
Sparse Core Ops, SparseCore 0:
  45.2 45.1 reduce-scatter.4
  93.2 43.9 reduce-scatter.2

commit v3 on v2

--- a/solution.py
+++ b/solution.py
@@ -3,6 +3,8 @@
 import jax
 import jax.numpy as jnp
 from jax import lax
+from jax.experimental import pallas as pl
+from jax.experimental.pallas import tpu as pltpu
 from jax.sharding import Mesh, PartitionSpec as P
 
 D = 5120
@@ -13,6 +15,10 @@
 NX, NZ, NC, NY, NH = 4, 4, 2, 8, 2
 DP = ("x", "z", "c")
 FFN = ("y", "h")
+LANES = 128
+SCALE_ROWS = 16
+STEPS = 128.0
+TOP = 32000.0
 
 
 def cross_rows(left, right):
@@ -31,6 +37,77 @@
     ]
 
 
+def pack_kernel(*refs):
+    chunks, out = refs[:-1], refs[-1]
+    rows = chunks[0].shape[0] * len(chunks) // NY
+    blocks = chunks[0].shape[1] // LANES
+    exponents = []
+    for b in range(blocks):
+        cols = slice(b * LANES, (b + 1) * LANES)
+        parts = [r[:, cols] for r in chunks]
+        most = jnp.max(jnp.abs(parts[0]), axis=0, keepdims=True)
+        for p in parts[1:]:
+            most = jnp.maximum(most, jnp.max(jnp.abs(p), axis=0, keepdims=True))
+        e = jnp.ceil(jnp.log(jnp.maximum(most, 1e-30)) * STEPS)
+        factor = jnp.exp(e * (-1.0 / STEPS)) * TOP
+        exponents.append(e)
+        for d in range(NY):
+            per = chunks[0].shape[0] // rows
+            p = parts[d // per][(d % per) * rows : (d % per + 1) * rows]
+            q = jnp.round(p * factor).astype(jnp.int32).astype(jnp.int16)
+            out[d, b * rows : (b + 1) * rows, :] = q
+    pad = [jnp.zeros((SCALE_ROWS - blocks, LANES), jnp.float32)]
+    tail = jnp.concatenate(exponents + pad, 0).astype(jnp.int32).astype(jnp.int16)
+    for d in range(NY):
+        out[d, blocks * rows : blocks * rows + SCALE_ROWS, :] = tail
+
+
+def unpack_kernel(h_ref, got, keep, send):
+    half = keep.shape[0]
+    rows = 2 * half
+    blocks = keep.shape[1] // LANES
+    mine = h_ref[0] == 0
+    factors = []
+    for s in range(NY):
+        e = got[s, blocks * rows : blocks * rows + SCALE_ROWS, :].astype(jnp.float32)
+        factors.append(jnp.exp(e * (1.0 / STEPS)) * (1.0 / TOP))
+    for b in range(blocks):
+        cols = slice(b * LANES, (b + 1) * LANES)
+        total = jnp.zeros((rows, LANES), jnp.float32)
+        for s in range(NY):
+            block = got[s, b * rows : (b + 1) * rows, :].astype(jnp.float32)
+            total = total + block * factors[s][b : b + 1]
+        low, high = total[:half], total[half:]
+        keep[:, cols] = jnp.where(mine, low, high)
+        send[:, cols] = jnp.where(mine, high, low)
+
+
+def sum_over_y(chunks, h):
+    tokens = chunks[0].shape[1]
+    rows = chunks[0].shape[0] * len(chunks) // NY
+    packed = pl.pallas_call(
+        pack_kernel,
+        out_shape=jax.ShapeDtypeStruct(
+            (NY, tokens // LANES * rows + SCALE_ROWS, LANES), jnp.int16
+        ),
+        in_specs=[pl.BlockSpec(memory_space=pltpu.VMEM)] * len(chunks),
+        out_specs=pl.BlockSpec(memory_space=pltpu.VMEM),
+        compiler_params=pltpu.CompilerParams(vmem_limit_bytes=24 << 20),
+    )(*chunks)
+    got = lax.all_to_all(packed, "y", 0, 0, tiled=True)
+    half = jax.ShapeDtypeStruct((rows // 2, tokens), jnp.float32)
+    return pl.pallas_call(
+        unpack_kernel,
+        out_shape=(half, half),
+        in_specs=[
+            pl.BlockSpec(memory_space=pltpu.SMEM),
+            pl.BlockSpec(memory_space=pltpu.VMEM),
+        ],
+        out_specs=(pl.BlockSpec(memory_space=pltpu.VMEM),) * 2,
+        compiler_params=pltpu.CompilerParams(vmem_limit_bytes=24 << 20),
+    )(h.reshape(1), got)
+
+
 def on_device(
     train_act, train_grad, train_seg, train_mask, test_act, test_grad, test_seg, test_mask
 ):
@@ -42,23 +119,18 @@
     grads = over_x(grad_z)
     acts = over_x(act_z)
 
-    def gram(chunks, own, other):
+    def grams(chunks, own, other):
         both = jnp.concatenate([own, other], 0)
-        return jnp.concatenate([cross_rows(t, both) for t in chunks], 0)
+        return [cross_rows(t, both) for t in chunks]
 
-    grad_gram = gram(grads, train_grad, other_grad)
+    grad_gram = jnp.concatenate(grams(grads, train_grad, other_grad), 0)
     grad_part = lax.psum_scatter(grad_gram, "y", scatter_dimension=0, tiled=True)
-    act_gram = gram(acts, train_act, other_act)
-    act_part = lax.psum_scatter(act_gram, "y", scatter_dimension=0, tiled=True)
+    act_keep, act_send = sum_over_y(grams(acts, train_act, other_act), h)
 
-    half = act_part.shape[0] // 2
-
-    def over_h(part):
-        keep = lax.dynamic_slice_in_dim(part, h * half, half, 0)
-        send = lax.dynamic_slice_in_dim(part, (1 - h) * half, half, 0)
-        return keep + swap(send, "h")
-
-    joint = over_h(act_part) * over_h(grad_part)
+    half = act_keep.shape[0]
+    grad_keep = lax.dynamic_slice_in_dim(grad_part, h * half, half, 0)
+    grad_send = lax.dynamic_slice_in_dim(grad_part, (1 - h) * half, half, 0)
+    joint = (act_keep + swap(act_send, "h")) * (grad_keep + swap(grad_send, "h"))
     behind = (y // 2) ^ (y // 4)
     first = (((x - behind) % NX * NZ + 2 * (y % 2) + h) * NC + c) * half
     seg = lax.dynamic_slice_in_dim(test_seg, first, half, 0)

time: 188 us -> 172 us (0.915)
  waiting for transfers between devices: 72.2 us -> 60.1 us
  starting transfers between devices: 51 us -> 46.1 us
    reduce_scatter x1 -> x0, waiting for transfers between devices: 37.8 us -> none  [on_device(): act_part = lax.psum_scatter(act_gram, 'y', scatter_dimension=0, tiled=True)]
    all_to_all x0 -> x1, waiting for transfers between devices: none -> 30.1 us  [sum_over_y(): got = lax.all_to_all(packed, 'y', 0, 0, tiled=True)]
    ppermute x6, starting transfers between devices: 30.1 us -> 19.4 us  [swap(): return lax.ppermute(value, axis, [(0, 1), (1, 0)])]
    ppermute x6, waiting for transfers between devices: 4.95 us -> 15.5 us  [swap(): return lax.ppermute(value, axis, [(0, 1), (1, 0)])]
    reduce_scatter x1, waiting for transfers between devices: 9.83 us -> 0.02 us  [on_device(): lax.psum_scatter(grad_gram, 'y', scatter_dimension=0, tiled=True)]
    all_to_all x0 -> x1, starting transfers between devices: none -> 7.11 us  [sum_over_y(): got = lax.all_to_all(packed, 'y', 0, 0, tiled=True)]
    ppermute x6, waiting for transfers between devices: 19.6 us -> 14.5 us  [over_x(): lax.ppermute(value, 'x', [(i, (i + step) % NX) for i in range(NX)])]
  transfers between devices with their start and end apart: 14 -> 14, of which waited for: 9 -> 8; matrix products, arithmetic and copies ran while one was open for 6% -> 7% of each run, Pallas kernels for 0% -> 1%
where the time goes in v3:
time: 172 us; the launch traced here: 170 us
  waiting for transfers between devices  60.1 us (35%)
  starting transfers between devices  46.1 us (27%)
  blocking collectives  34.5 us (20%)
  between operations  13.8 us (8%)
  matrix products  5.05 us (3%)
  local copies, waits for them, and re-layouts  4.78 us (3%)
  other arithmetic  3.94 us (2%)
  Pallas kernels  1.76 us (1%)
    all_to_all x1, waiting for transfers between devices, sum_over_y(): got = lax.all_to_all(packed, 'y', 0, 0, tiled=True)  30.1 us
    ppermute x6, starting transfers between devices, over_x(): lax.ppermute(value, 'x', [(i, (i + step) % NX) for i in range(NX)])  19.6 us
    ppermute x6, starting transfers between devices, swap(): return lax.ppermute(value, axis, [(0, 1), (1, 0)])  19.4 us
    all_gather x1, blocking collectives, on_device(): lax.all_gather(jnp.concatenate([test_act, test_grad], 1), 'z', axis=0, ti...  18.5 us
    psum x1, blocking collectives, on_device(): scores = lax.psum(scores, 'y')  16 us
    ppermute x6, waiting for transfers between devices, swap(): return lax.ppermute(value, axis, [(0, 1), (1, 0)])  15.5 us
    ppermute x6, waiting for transfers between devices, over_x(): lax.ppermute(value, 'x', [(i, (i + step) % NX) for i in range(NX)])  14.5 us
    all_to_all x1, starting transfers between devices, sum_over_y(): got = lax.all_to_all(packed, 'y', 0, 0, tiled=True)  7.11 us
  transfers between devices with their start and end apart: 14, of which 8 were waited for; matrix products, arithmetic and copies ran while one was open for 7% of the time, Pallas kernels for 1%

profile of v3, /device:TPU:6, one launch (start us, length us, event | category | flops | bytes accessed | tf_op | source)
XLA Modules:
  0.0 170.0 jit_solution(11992895369944676700)
XLA Ops:
  6.5 1.9 %collective-permute-start.5 = (bf16[512,320]{0,1:T(8,128)(2,1)}, bf16[512,320]{0,1:T(8,128)(2,1)S(1)}, u32[]{:S(2)}, u32[]{:S(2)}) collective-permute-start(bf16[512,320]{0,1:T(8,128)(2,1)} %param.9), channel_id=1, source_target_pairs={{0,16},{16,0},{1,17},{17,1},{2,18},{18,2},{3,19},{19,3},{4,20},{20... | collective-permute-start | bytes 983048 | tf_op jit(solution)/shard_map/ppermute | solution.py:31
  9.5 18.5 %all_gather.3 = bf16[128,1920]{1,0:T(8,128)(2,1)S(1)} all-gather(bf16[32,1920]{1,0:T(8,128)(2,1)S(1)} %pad_maximum_fusion.1), channel_id=1, replica_groups=mesh['x'=4,'z'=4,'c'=2,'y'=8,'h'=2] {'z'}, dimensions={0}, use_global_device_ids=true | all-gather | bytes 614400 | tf_op jit(solution)/shard_map/all_gather | solution.py:116
  28.0 3.3 %collective-permute-start.8 = (bf16[128,320]{1,0:T(8,128)(2,1)S(1)}, bf16[128,320]{1,0:T(8,128)(2,1)S(1)}, u32[]{:S(2)}, u32[]{:S(2)}) collective-permute-start(bf16[128,320]{1,0:T(8,128)(2,1)S(1)} %slice.17), channel_id=1, source_target_pairs={{0,256},{128,384},{256,0},{384,128},{1,257},{129,385},{257,1},{385... | collective-permute-start | bytes 245768 | tf_op jit(solution)/shard_map/ppermute | solution.py:36
  31.4 4.6 %collective-permute-start.7 = (bf16[128,320]{1,0:T(8,128)(2,1)S(1)}, bf16[128,320]{1,0:T(8,128)(2,1)S(1)}, u32[]{:S(2)}, u32[]{:S(2)}) collective-permute-start(bf16[128,320]{1,0:T(8,128)(2,1)S(1)} %slice.17), channel_id=1, source_target_pairs={{0,384},{128,0},{256,128},{384,256},{1,385},{129,1},{257,129},{385... | collective-permute-start | bytes 245768 | tf_op jit(solution)/shard_map/ppermute | solution.py:36
  36.0 2.4 %collective-permute-start.6 = (bf16[128,320]{1,0:T(8,128)(2,1)S(1)}, bf16[128,320]{1,0:T(8,128)(2,1)S(1)}, u32[]{:S(2)}, u32[]{:S(2)}) collective-permute-start(bf16[128,320]{1,0:T(8,128)(2,1)S(1)} %slice.17), channel_id=1, source_target_pairs={{0,128},{128,256},{256,384},{384,0},{1,129},{129,257},{257,385},{3... | collective-permute-start | bytes 245768 | tf_op jit(solution)/shard_map/ppermute | solution.py:36
  38.4 1.9 %collective-permute-start = (bf16[512,1600]{0,1:T(8,128)(2,1)}, bf16[512,1600]{0,1:T(8,128)(2,1)}, u32[]{:S(2)}, u32[]{:S(2)}) collective-permute-start(bf16[512,1600]{0,1:T(8,128)(2,1)} %param.8), channel_id=1, source_target_pairs={{0,16},{16,0},{1,17},{17,1},{2,18},{18,2},{3,19},{19,3},{4,20},{20... | collective-permute-start | bytes 4915208 | tf_op jit(solution)/shard_map/ppermute | solution.py:31
  42.8 1.6 pad_maximum_fusion
  44.5 3.6 %collective-permute-start.1 = (bf16[128,1600]{1,0:T(8,128)(2,1)S(1)}, bf16[128,1600]{1,0:T(8,128)(2,1)S(1)}, u32[]{:S(2)}, u32[]{:S(2)}) collective-permute-start(bf16[128,1600]{1,0:T(8,128)(2,1)S(1)} %slice.16), channel_id=1, source_target_pairs={{0,128},{128,256},{256,384},{384,0},{1,129},{129,257},{257,385},{3... | collective-permute-start | bytes 1228808 | tf_op jit(solution)/shard_map/ppermute | solution.py:36
  48.1 2.2 %collective-permute-start.2 = (bf16[128,1600]{1,0:T(8,128)(2,1)S(1)}, bf16[128,1600]{1,0:T(8,128)(2,1)S(1)}, u32[]{:S(2)}, u32[]{:S(2)}) collective-permute-start(bf16[128,1600]{1,0:T(8,128)(2,1)S(1)} %slice.16), channel_id=1, source_target_pairs={{0,384},{128,0},{256,128},{384,256},{1,385},{129,1},{257,129},{385... | collective-permute-start | bytes 1228808 | tf_op jit(solution)/shard_map/ppermute | solution.py:36
  50.3 3.4 %collective-permute-start.3 = (bf16[128,1600]{1,0:T(8,128)(2,1)S(1)}, bf16[128,1600]{1,0:T(8,128)(2,1)S(1)}, u32[]{:S(2)}, u32[]{:S(2)}) collective-permute-start(bf16[128,1600]{1,0:T(8,128)(2,1)S(1)} %slice.16), channel_id=1, source_target_pairs={{0,256},{128,384},{256,0},{384,128},{1,257},{129,385},{257,1},{385... | collective-permute-start | bytes 1228808 | tf_op jit(solution)/shard_map/ppermute | solution.py:36
  54.0 1.7 constant_dynamic-update-slice_fusion
  56.4 2.6 %collective-permute-done.1 = bf16[128,1600]{1,0:T(8,128)(2,1)S(1)} collective-permute-done((bf16[128,1600]{1,0:T(8,128)(2,1)S(1)}, bf16[128,1600]{1,0:T(8,128)(2,1)S(1)}, u32[]{:S(2)}, u32[]{:S(2)}) %collective-permute-start.1) | collective-permute-done | bytes 409632 | tf_op jit(solution)/shard_map/ppermute | solution.py:36
  59.6 11.7 %collective-permute-done.2 = bf16[128,1600]{1,0:T(8,128)(2,1)S(1)} collective-permute-done((bf16[128,1600]{1,0:T(8,128)(2,1)S(1)}, bf16[128,1600]{1,0:T(8,128)(2,1)S(1)}, u32[]{:S(2)}, u32[]{:S(2)}) %collective-permute-start.2) | collective-permute-done | bytes 409632 | tf_op jit(solution)/shard_map/ppermute | solution.py:36
  72.7 1.5 shard_map.82
  74.2 7.1 %all-to-all-start = ((s16[8,528,128]{2,1,0:T(8,128)(2,1)}), s16[8,528,128]{2,1,0:T(8,128)(2,1)S(1)}, u32[]{:S(2)}, u32[]{:S(2)}) async-start(s16[8,528,128]{2,1,0:T(8,128)(2,1)} %shard_map.82), calls=%async_computation | async-start | bytes 2162688 | tf_op jit(solution)/shard_map/all_to_all | solution.py:97
  81.3 30.1 %all-to-all-done.got = s16[8,528,128]{2,1,0:T(8,128)(2,1)S(1)} async-done(((s16[8,528,128]{2,1,0:T(8,128)(2,1)}), s16[8,528,128]{2,1,0:T(8,128)(2,1)S(1)}, u32[]{:S(2)}, u32[]{:S(2)}) %all-to-all-start) | async-done | bytes 1081376 | tf_op jit(solution)/shard_map/all_to_all | solution.py:97
  111.7 8.0 %collective-permute-start.4 = (f32[32,1024]{1,0:T(8,128)S(1)}, f32[32,1024]{1,0:T(8,128)S(1)}, u32[]{:S(2)}, u32[]{:S(2)}) collective-permute-start(f32[32,1024]{1,0:T(8,128)S(1)} %get-tuple-element.8), channel_id=1, source_target_pairs={{0,1},{1,0},{2,3},{3,2},{4,5},{5,4},{6,7},{7,6},{8,9},{9,8},{10,11... | collective-permute-start | bytes 393224 | tf_op jit(solution)/shard_map/ppermute | solution.py:31
  120.7 1.9 %collective-permute-start.9 = (f32[32,1024]{1,0:T(8,128)S(1)}, f32[32,1024]{1,0:T(8,128)S(1)}, u32[]{:S(2)}, u32[]{:S(2)}) collective-permute-start(f32[32,1024]{1,0:T(8,128)S(1)} %constant_dynamic-slice_fusion), channel_id=1, source_target_pairs={{0,1},{1,0},{2,3},{3,2},{4,5},{5,4},{6,7},{7,6},{8,9},{9,8},{10,11... | collective-permute-start | bytes 393224 | tf_op jit(solution)/shard_map/ppermute | solution.py:31
  124.4 8.4 %collective-permute-done.9 = f32[32,1024]{1,0:T(8,128)S(1)} collective-permute-done((f32[32,1024]{1,0:T(8,128)S(1)}, f32[32,1024]{1,0:T(8,128)S(1)}, u32[]{:S(2)}, u32[]{:S(2)}) %collective-permute-start.9) | collective-permute-done | bytes 131104 | tf_op jit(solution)/shard_map/ppermute | solution.py:31
  134.0 1.9 %collective-permute-start.10 = (f32[8,512]{1,0:T(8,128)S(1)}, f32[8,512]{1,0:T(8,128)S(1)}, u32[]{:S(2)}, u32[]{:S(2)}) collective-permute-start(f32[8,512]{1,0:T(8,128)S(1)} %slice.19), channel_id=1, source_target_pairs={{0,16},{16,0},{1,17},{17,1},{2,18},{18,2},{3,19},{19,3},{4,20},{20... | collective-permute-start | bytes 49160 | tf_op jit(solution)/shard_map/ppermute | solution.py:31
  135.9 1.1 collective-permute-done.10
  137.2 16.0 %psum.7 = f32[4,8]{1,0:T(4,128)S(1)} all-reduce(f32[4,8]{1,0:T(4,128)S(1)} %fusion.5), channel_id=1, replica_groups=mesh['x'=4,'z'=4,'c'=2,'y'=8,'h'=2] {'y'}, use_global_device_ids=true, to_apply=%region_1.2 | all-reduce | flops 32 | bytes 256 | tf_op jit(solution)/shard_map/psum | solution.py:151
  153.2 3.7 %collective-permute-start.11 = (f32[4,8]{1,0:T(4,128)S(1)}, f32[4,8]{1,0:T(4,128)S(1)}, u32[]{:S(2)}, u32[]{:S(2)}) collective-permute-start(f32[4,8]{1,0:T(4,128)S(1)} %psum.7), channel_id=1, source_target_pairs={{0,1},{1,0},{2,3},{3,2},{4,5},{5,4},{6,7},{7,6},{8,9},{9,8},{10,11... | collective-permute-start | bytes 392 | tf_op jit(solution)/shard_map/ppermute | solution.py:31
  156.9 5.7 %collective-permute-done.11 = f32[4,8]{1,0:T(4,128)S(1)} collective-permute-done((f32[4,8]{1,0:T(4,128)S(1)}, f32[4,8]{1,0:T(4,128)S(1)}, u32[]{:S(2)}, u32[]{:S(2)}) %collective-permute-start.11) | collective-permute-done | bytes 160 | tf_op jit(solution)/shard_map/ppermute | solution.py:31
  (39 shorter events, 11.2 us)
Async XLA Ops:
  6.5 113.2 %reduce-scatter.2.cloned.1.call-start = ((), (), s32[]{:S(2)}) async-start(), calls=%async_computation.2 | async-start | bytes 2359296 | tf_op jit(solution)/shard_map/reduce_scatter | solution.py:127
  6.5 34.8 %collective-permute-start.5 = (bf16[512,320]{0,1:T(8,128)(2,1)}, bf16[512,320]{0,1:T(8,128)(2,1)S(1)}, u32[]{:S(2)}, u32[]{:S(2)}) collective-permute-start(bf16[512,320]{0,1:T(8,128)(2,1)} %param.9), channel_id=1, source_target_pairs={{0,16},{16,0},{1,17},{17,1},{2,18},{18,2},{3,19},{19,3},{4,20},{20... | collective-permute-start | bytes 983048 | tf_op jit(solution)/shard_map/ppermute | solution.py:31
  28.0 13.7 %collective-permute-start.8 = (bf16[128,320]{1,0:T(8,128)(2,1)S(1)}, bf16[128,320]{1,0:T(8,128)(2,1)S(1)}, u32[]{:S(2)}, u32[]{:S(2)}) collective-permute-start(bf16[128,320]{1,0:T(8,128)(2,1)S(1)} %slice.17), channel_id=1, source_target_pairs={{0,256},{128,384},{256,0},{384,128},{1,257},{129,385},{257,1},{385... | collective-permute-start | bytes 245768 | tf_op jit(solution)/shard_map/ppermute | solution.py:36
  31.4 10.7 %collective-permute-start.7 = (bf16[128,320]{1,0:T(8,128)(2,1)S(1)}, bf16[128,320]{1,0:T(8,128)(2,1)S(1)}, u32[]{:S(2)}, u32[]{:S(2)}) collective-permute-start(bf16[128,320]{1,0:T(8,128)(2,1)S(1)} %slice.17), channel_id=1, source_target_pairs={{0,384},{128,0},{256,128},{384,256},{1,385},{129,1},{257,129},{385... | collective-permute-start | bytes 245768 | tf_op jit(solution)/shard_map/ppermute | solution.py:36
  36.0 6.5 %collective-permute-start.6 = (bf16[128,320]{1,0:T(8,128)(2,1)S(1)}, bf16[128,320]{1,0:T(8,128)(2,1)S(1)}, u32[]{:S(2)}, u32[]{:S(2)}) collective-permute-start(bf16[128,320]{1,0:T(8,128)(2,1)S(1)} %slice.17), channel_id=1, source_target_pairs={{0,128},{128,256},{256,384},{384,0},{1,129},{129,257},{257,385},{3... | collective-permute-start | bytes 245768 | tf_op jit(solution)/shard_map/ppermute | solution.py:36
  38.4 15.6 %collective-permute-start = (bf16[512,1600]{0,1:T(8,128)(2,1)}, bf16[512,1600]{0,1:T(8,128)(2,1)}, u32[]{:S(2)}, u32[]{:S(2)}) collective-permute-start(bf16[512,1600]{0,1:T(8,128)(2,1)} %param.8), channel_id=1, source_target_pairs={{0,16},{16,0},{1,17},{17,1},{2,18},{18,2},{3,19},{19,3},{4,20},{20... | collective-permute-start | bytes 4915208 | tf_op jit(solution)/shard_map/ppermute | solution.py:31
  42.8 10.9 %copy-start = (bf16[512,1600]{0,1:T(8,128)(2,1)S(1)}, bf16[512,1600]{0,1:T(8,128)(2,1)}, u32[]{:S(2)}) copy-start(bf16[512,1600]{0,1:T(8,128)(2,1)} %param.8) | copy-start | bytes 4915204
  44.5 14.5 %collective-permute-start.1 = (bf16[128,1600]{1,0:T(8,128)(2,1)S(1)}, bf16[128,1600]{1,0:T(8,128)(2,1)S(1)}, u32[]{:S(2)}, u32[]{:S(2)}) collective-permute-start(bf16[128,1600]{1,0:T(8,128)(2,1)S(1)} %slice.16), channel_id=1, source_target_pairs={{0,128},{128,256},{256,384},{384,0},{1,129},{129,257},{257,385},{3... | collective-permute-start | bytes 1228808 | tf_op jit(solution)/shard_map/ppermute | solution.py:36
  48.1 23.2 %collective-permute-start.2 = (bf16[128,1600]{1,0:T(8,128)(2,1)S(1)}, bf16[128,1600]{1,0:T(8,128)(2,1)S(1)}, u32[]{:S(2)}, u32[]{:S(2)}) collective-permute-start(bf16[128,1600]{1,0:T(8,128)(2,1)S(1)} %slice.16), channel_id=1, source_target_pairs={{0,384},{128,0},{256,128},{384,256},{1,385},{129,1},{257,129},{385... | collective-permute-start | bytes 1228808 | tf_op jit(solution)/shard_map/ppermute | solution.py:36
  50.3 21.7 %collective-permute-start.3 = (bf16[128,1600]{1,0:T(8,128)(2,1)S(1)}, bf16[128,1600]{1,0:T(8,128)(2,1)S(1)}, u32[]{:S(2)}, u32[]{:S(2)}) collective-permute-start(bf16[128,1600]{1,0:T(8,128)(2,1)S(1)} %slice.16), channel_id=1, source_target_pairs={{0,256},{128,384},{256,0},{384,128},{1,257},{129,385},{257,1},{385... | collective-permute-start | bytes 1228808 | tf_op jit(solution)/shard_map/ppermute | solution.py:36
  72.7 63.2 %copy-start.2 = (s32[1,512]{1,0:T(1,128)S(1)}, s32[1,512]{1,0:T(1,128)}, u32[]{:S(2)}) copy-start(s32[1,512]{1,0:T(1,128)} %param.11) | copy-start | bytes 6148
  72.7 64.4 %copy-start.1 = (s32[1,512]{1,0:T(1,128)S(1)}, s32[1,512]{1,0:T(1,128)}, u32[]{:S(2)}) copy-start(s32[1,512]{1,0:T(1,128)} %param.10) | copy-start | bytes 6148
  74.2 37.2 %all-to-all-start = ((s16[8,528,128]{2,1,0:T(8,128)(2,1)}), s16[8,528,128]{2,1,0:T(8,128)(2,1)S(1)}, u32[]{:S(2)}, u32[]{:S(2)}) async-start(s16[8,528,128]{2,1,0:T(8,128)(2,1)} %shard_map.82), calls=%async_computation | async-start | bytes 2162688 | tf_op jit(solution)/shard_map/all_to_all | solution.py:97
  111.7 12.8 %collective-permute-start.4 = (f32[32,1024]{1,0:T(8,128)S(1)}, f32[32,1024]{1,0:T(8,128)S(1)}, u32[]{:S(2)}, u32[]{:S(2)}) collective-permute-start(f32[32,1024]{1,0:T(8,128)S(1)} %get-tuple-element.8), channel_id=1, source_target_pairs={{0,1},{1,0},{2,3},{3,2},{4,5},{5,4},{6,7},{7,6},{8,9},{9,8},{10,11... | collective-permute-start | bytes 393224 | tf_op jit(solution)/shard_map/ppermute | solution.py:31
  120.7 12.2 %collective-permute-start.9 = (f32[32,1024]{1,0:T(8,128)S(1)}, f32[32,1024]{1,0:T(8,128)S(1)}, u32[]{:S(2)}, u32[]{:S(2)}) collective-permute-start(f32[32,1024]{1,0:T(8,128)S(1)} %constant_dynamic-slice_fusion), channel_id=1, source_target_pairs={{0,1},{1,0},{2,3},{3,2},{4,5},{5,4},{6,7},{7,6},{8,9},{9,8},{10,11... | collective-permute-start | bytes 393224 | tf_op jit(solution)/shard_map/ppermute | solution.py:31
  134.0 3.1 %collective-permute-start.10 = (f32[8,512]{1,0:T(8,128)S(1)}, f32[8,512]{1,0:T(8,128)S(1)}, u32[]{:S(2)}, u32[]{:S(2)}) collective-permute-start(f32[8,512]{1,0:T(8,128)S(1)} %slice.19), channel_id=1, source_target_pairs={{0,16},{16,0},{1,17},{17,1},{2,18},{18,2},{3,19},{19,3},{4,20},{20... | collective-permute-start | bytes 49160 | tf_op jit(solution)/shard_map/ppermute | solution.py:31
  153.2 9.4 %collective-permute-start.11 = (f32[4,8]{1,0:T(4,128)S(1)}, f32[4,8]{1,0:T(4,128)S(1)}, u32[]{:S(2)}, u32[]{:S(2)}) collective-permute-start(f32[4,8]{1,0:T(4,128)S(1)} %psum.7), channel_id=1, source_target_pairs={{0,1},{1,0},{2,3},{3,2},{4,5},{5,4},{6,7},{7,6},{8,9},{9,8},{10,11... | collective-permute-start | bytes 392 | tf_op jit(solution)/shard_map/ppermute | solution.py:31
Sparse Core Ops, SparseCore 0:
  44.6 56.0 reduce-scatter.1

commit v4 on v2

v4 whole, which is shorter than its diff:
```python
import math

import jax
import jax.numpy as jnp
from jax import lax
from jax.experimental import pallas as pl
from jax.experimental.pallas import tpu as pltpu
from jax.sharding import Mesh, PartitionSpec as P

D = 5120
FF = 25600
SEG_LEN = 256
SEQ_PACK = 4
TEST_SEQS = 8
NX, NZ, NC, NY, NH = 4, 4, 2, 8, 2
DP = ("x", "z", "c")
FFN = ("y", "h")
LANES = 128
BLOCKS = 8
SCALE_ROWS = 16
STEPS = 128.0
TOP = 32000.0


def cross_rows(left, right):
    return lax.dot_general(
        left, right, (((1,), (1,)), ((), ())), preferred_element_type=jnp.float32
    )


def swap(value, axis):
    return lax.ppermute(value, axis, [(0, 1), (1, 0)])


def over_x(value):
    return [value] + [
        lax.ppermute(value, "x", [(i, (i + step) % NX) for i in range(NX)]) for step in (1, 3, 2)
    ]


def pack(parts, out, lead):
    blocks = parts.blocks
    exponents = []
    for b in range(blocks):
        pieces = parts(b)
        rows = pieces[0].shape[0]
        most = jnp.max(jnp.abs(pieces[0]), axis=0, keepdims=True)
        for p in pieces[1:]:
            most = jnp.maximum(most, jnp.max(jnp.abs(p), axis=0, keepdims=True))
        e = jnp.ceil(jnp.log(jnp.maximum(most, 1e-30)) * STEPS)
        factor = jnp.exp(e * (-1.0 / STEPS)) * TOP
        exponents.append(e)
        for i, p in enumerate(pieces):
            q = jnp.round(p * factor).astype(jnp.int32).astype(jnp.int16)
            out[lead[i] + (slice(b * rows, (b + 1) * rows), slice(None))] = q
    pad = [jnp.zeros((SCALE_ROWS - blocks, LANES), jnp.float32)]
    tail = jnp.concatenate(exponents + pad, 0).astype(jnp.int32).astype(jnp.int16)
    for at in lead:
        out[at + (slice(blocks * rows, blocks * rows + SCALE_ROWS), slice(None))] = tail


class Pieces:
    def __init__(self, blocks, get):
        self.blocks, self.get = blocks, get

    def __call__(self, b):
        return self.get(b)


def factors_of(tail):
    return jnp.exp(tail.astype(jnp.float32) * (1.0 / STEPS)) * (1.0 / TOP)


def pack_kernel(*refs):
    chunks, out = refs[:-1], refs[-1]
    rows = chunks[0].shape[0] * len(chunks) // NY
    per = chunks[0].shape[0] // rows

    def pieces(b):
        cols = slice(b * LANES, (b + 1) * LANES)
        return [
            chunks[d // per][(d % per) * rows : (d % per + 1) * rows, cols] for d in range(NY)
        ]

    pack(Pieces(chunks[0].shape[1] // LANES, pieces), out, [(d,) for d in range(NY)])


def unpack_kernel(got, out):
    blocks = BLOCKS
    rows = (got.shape[1] - SCALE_ROWS) // blocks
    factors = [factors_of(got[s, blocks * rows :, :]) for s in range(NY)]

    def pieces(b):
        total = jnp.zeros((rows, LANES), jnp.float32)
        for s in range(NY):
            block = got[s, b * rows : (b + 1) * rows, :].astype(jnp.float32)
            total = total + block * factors[s][b : b + 1]
        return [total]

    pack(Pieces(blocks, pieces), out, [()])


def joint_kernel(onehot, act_own, act_other, grad_own, grad_other, out):
    blocks = BLOCKS
    rows = (act_own.shape[0] - SCALE_ROWS) // blocks

    def part(ref, factor, b):
        return ref[b * rows : (b + 1) * rows, :].astype(jnp.float32) * factor[b : b + 1]

    refs = (act_own, act_other, grad_own, grad_other)
    f = [factors_of(r[blocks * rows :, :]) for r in refs]
    for b in range(blocks):
        a0, a1, g0, g1 = (part(r, k, b) for r, k in zip(refs, f))
        joint = (a0 + a1) * (g0 + g1)
        out[:, b * LANES : (b + 1) * LANES] = lax.dot_general(
            onehot[...],
            joint,
            (((1,), (0,)), ((), ())),
            precision=lax.Precision.HIGHEST,
            preferred_element_type=jnp.float32,
        )


VMEM = pl.BlockSpec(memory_space=pltpu.VMEM)


def call(kernel, shape, dtype, *args):
    return pl.pallas_call(
        kernel,
        out_shape=jax.ShapeDtypeStruct(shape, dtype),
        in_specs=[VMEM] * len(args),
        out_specs=VMEM,
        compiler_params=pltpu.CompilerParams(vmem_limit_bytes=24 << 20),
    )(*args)


def sum_over_y(chunks):
    rows = chunks[0].shape[0] * len(chunks) // NY
    height = BLOCKS * rows + SCALE_ROWS
    packed = call(pack_kernel, (NY, height, LANES), jnp.int16, *chunks)
    got = lax.all_to_all(packed, "y", 0, 0, tiled=True)
    return call(unpack_kernel, (height, LANES), jnp.int16, got)


def on_device(
    train_act, train_grad, train_seg, train_mask, test_act, test_grad, test_seg, test_mask
):
    x, y, c = (lax.axis_index(a) for a in ("x", "y", "c"))
    wide = test_act.shape[1]
    both_z = lax.all_gather(jnp.concatenate([test_act, test_grad], 1), "z", axis=0, tiled=True)
    act_z, grad_z = both_z[:, :wide], both_z[:, wide:]
    other_grad, other_act = swap(train_grad, "c"), swap(train_act, "c")
    grads = over_x(grad_z)
    acts = over_x(act_z)

    def grams(chunks, own, other):
        both = jnp.concatenate([own, other], 0)
        return [cross_rows(t, both) for t in chunks]

    grad_y = sum_over_y(grams(grads, train_grad, other_grad))
    act_y = sum_over_y(grams(acts, train_act, other_act))
    behind = (y // 2) ^ (y // 4)
    local = test_act.shape[0]
    seg, mask = (
        lax.dynamic_slice(
            v.reshape(NX, NZ, NC, local), ((x - behind) % NX, 2 * (y % 2), c, 0), (1, 2, 1, local)
        ).reshape(1, -1)
        for v in (test_seg, test_mask)
    )
    test_onehot = (
        (seg == jnp.arange(TEST_SEQS, dtype=jnp.int32)[:, None]) & (mask != 0)
    ).astype(jnp.float32)
    grad_other, act_other = swap(grad_y, "h"), swap(act_y, "h")
    rows = call(
        joint_kernel,
        (TEST_SEQS, BLOCKS * LANES),
        jnp.float32,
        test_onehot,
        act_y,
        act_other,
        grad_y,
        grad_other,
    )
    n = train_act.shape[0]
    mine, theirs = rows[:, :n], rows[:, n:]
    total = mine + swap(theirs, "c")
    train_onehot = (
        (train_seg == jnp.arange(SEQ_PACK, dtype=jnp.int32)[:, None]) & (train_mask != 0)
    ).astype(jnp.float32)
    scores = lax.dot_general(
        train_onehot, total, (((1,), (1,)), ((), ())), precision=lax.Precision.HIGHEST
    )
    scores = lax.psum(scores, "y")
    return scores * (1.0 / (SEG_LEN * math.sqrt(FF * D)))


def solution(mesh):
    fine = Mesh(mesh.devices.reshape(NX, NZ, NC, NY, NH), ("x", "z", "c", "y", "h"))
    return jax.shard_map(
        on_device,
        mesh=fine,
        in_specs=(P(DP, FFN), P(DP, FFN), P(DP, None), P(DP, None), P(DP, FFN), P(DP, FFN), P(), P()),
        out_specs=P(DP, None),
        check_vma=False,
    )
```

time: 188 us -> 135 us (0.72)
  waiting for transfers between devices: 72.2 us -> 33 us
  between operations: 13.7 us -> 0.32 us
  starting transfers between devices: 51 us -> 55.2 us
  Pallas kernels: 0 us -> 4.07 us
  other arithmetic: 5.41 us -> 1.64 us
  local copies, waits for them, and re-layouts: 5.6 us -> 3.46 us
    reduce_scatter x2 -> x0, waiting for transfers between devices: 47.6 us -> none  [the longest x1 37.8 us: on_device(): act_part = lax.psum_scatter(act_gram, 'y', scatter_dimension=0, tiled=True)]
    all_to_all x0 -> x2, waiting for transfers between devices: none -> 15 us  [sum_over_y(): got = lax.all_to_all(packed, 'y', 0, 0, tiled=True)]
    all_to_all x0 -> x2, starting transfers between devices: none -> 12.3 us  [sum_over_y(): got = lax.all_to_all(packed, 'y', 0, 0, tiled=True)]
    ppermute x6 -> x5, starting transfers between devices: 30.1 us -> 22.7 us  [swap(): return lax.ppermute(value, axis, [(0, 1), (1, 0)])]
    ppermute x6, waiting for transfers between devices: 19.6 us -> 13.9 us  [over_x(): lax.ppermute(value, 'x', [(i, (i + step) % NX) for i in range(NX)])]
    pallas_call x0 -> x5, Pallas kernels: none -> 4.07 us  [call(): pl.pallas_call(kernel, out_shape=jax.ShapeDtypeStruct(shape, dtype), in_s...]
    concatenate x2 -> x0, other arithmetic: 3.05 us -> none  [gram(): return jnp.concatenate([cross_rows(t, both) for t in chunks], 0)]
    dynamic_slice x3 -> x1, local copies, waits for them, and re-layouts: 2.59 us -> 0.03 us  [on_device(): lax.dynamic_slice(v.reshape(NX, NZ, NC, local), ((x - behind) % NX, 2 * (...]
  transfers between devices with their start and end apart: 14 -> 13, of which waited for: 9 -> 7; matrix products, arithmetic and copies ran while one was open for 6% -> 6% of each run, Pallas kernels for 0% -> 3%
where the time goes in v4:
time: 135 us; the launch traced here: 134 us
  starting transfers between devices  55.2 us (41%)
  waiting for transfers between devices  33 us (24%)
  blocking collectives  32.7 us (24%)
  Pallas kernels  4.07 us (3%)
  matrix products  4 us (3%)
  local copies, waits for them, and re-layouts  3.46 us (3%)
  other arithmetic  1.64 us (1%)
    ppermute x5, starting transfers between devices, swap(): return lax.ppermute(value, axis, [(0, 1), (1, 0)])  22.7 us
    ppermute x6, starting transfers between devices, over_x(): lax.ppermute(value, 'x', [(i, (i + step) % NX) for i in range(NX)])  20.3 us
    all_gather x1, blocking collectives, on_device(): lax.all_gather(jnp.concatenate([test_act, test_grad], 1), 'z', axis=0, ti...  18 us
    all_to_all x2, waiting for transfers between devices, sum_over_y(): got = lax.all_to_all(packed, 'y', 0, 0, tiled=True)  15 us
    psum x1, blocking collectives, on_device(): scores = lax.psum(scores, 'y')  14.7 us
    ppermute x6, waiting for transfers between devices, over_x(): lax.ppermute(value, 'x', [(i, (i + step) % NX) for i in range(NX)])  13.9 us
    all_to_all x2, starting transfers between devices, sum_over_y(): got = lax.all_to_all(packed, 'y', 0, 0, tiled=True)  12.3 us
    ppermute x5, waiting for transfers between devices, swap(): return lax.ppermute(value, axis, [(0, 1), (1, 0)])  4.08 us
  transfers between devices with their start and end apart: 13, of which 7 were waited for; matrix products, arithmetic and copies ran while one was open for 6% of the time, Pallas kernels for 3%

profile of v4, /device:TPU:6, one launch (start us, length us, event | category | flops | bytes accessed | tf_op | source)
XLA Modules:
  0.0 134.4 jit_solution(4782182407656380176)
XLA Ops:
  0.0 1.9 %collective-permute-start = (bf16[512,1600]{0,1:T(8,128)(2,1)}, bf16[512,1600]{0,1:T(8,128)(2,1)}, u32[]{:S(2)}, u32[]{:S(2)}) collective-permute-start(bf16[512,1600]{0,1:T(8,128)(2,1)} %param.8), channel_id=1, source_target_pairs={{0,16},{16,0},{1,17},{17,1},{2,18},{18,2},{3,19},{19,3},{4,20},{20... | collective-permute-start | bytes 4915208 | tf_op jit(solution)/shard_map/ppermute | solution.py:32
  1.9 2.4 %collective-permute-start.5 = (bf16[512,320]{0,1:T(8,128)(2,1)}, bf16[512,320]{0,1:T(8,128)(2,1)S(1)}, u32[]{:S(2)}, u32[]{:S(2)}) collective-permute-start(bf16[512,320]{0,1:T(8,128)(2,1)} %param.9), channel_id=1, source_target_pairs={{0,16},{16,0},{1,17},{17,1},{2,18},{18,2},{3,19},{19,3},{4,20},{20... | collective-permute-start | bytes 983048 | tf_op jit(solution)/shard_map/ppermute | solution.py:32
  5.3 18.0 %all_gather.3 = bf16[128,1920]{1,0:T(8,128)(2,1)S(1)} all-gather(bf16[32,1920]{1,0:T(8,128)(2,1)S(1)} %pad_maximum_fusion), channel_id=1, replica_groups=mesh['x'=4,'z'=4,'c'=2,'y'=8,'h'=2] {'z'}, dimensions={0}, use_global_device_ids=true | all-gather | bytes 614400 | tf_op jit(solution)/shard_map/all_gather | solution.py:150
  23.5 5.8 %collective-permute-start.6 = (bf16[128,320]{1,0:T(8,128)(2,1)S(1)}, bf16[128,320]{1,0:T(8,128)(2,1)S(1)}, u32[]{:S(2)}, u32[]{:S(2)}) collective-permute-start(bf16[128,320]{1,0:T(8,128)(2,1)S(1)} %slice.17), channel_id=1, source_target_pairs={{0,128},{128,256},{256,384},{384,0},{1,129},{129,257},{257,385},{3... | collective-permute-start | bytes 245768 | tf_op jit(solution)/shard_map/ppermute | solution.py:37
  29.3 1.9 %collective-permute-start.7 = (bf16[128,320]{1,0:T(8,128)(2,1)S(1)}, bf16[128,320]{1,0:T(8,128)(2,1)S(1)}, u32[]{:S(2)}, u32[]{:S(2)}) collective-permute-start(bf16[128,320]{1,0:T(8,128)(2,1)S(1)} %slice.17), channel_id=1, source_target_pairs={{0,384},{128,0},{256,128},{384,256},{1,385},{129,1},{257,129},{385... | collective-permute-start | bytes 245768 | tf_op jit(solution)/shard_map/ppermute | solution.py:37
  31.2 3.4 %collective-permute-start.8 = (bf16[128,320]{1,0:T(8,128)(2,1)S(1)}, bf16[128,320]{1,0:T(8,128)(2,1)S(1)}, u32[]{:S(2)}, u32[]{:S(2)}) collective-permute-start(bf16[128,320]{1,0:T(8,128)(2,1)S(1)} %slice.17), channel_id=1, source_target_pairs={{0,256},{128,384},{256,0},{384,128},{1,257},{129,385},{257,1},{385... | collective-permute-start | bytes 245768 | tf_op jit(solution)/shard_map/ppermute | solution.py:37
  34.6 1.0 constant_dynamic-update-slice_fusion.3
  37.3 1.9 %collective-permute-done.8 = bf16[128,320]{1,0:T(8,128)(2,1)S(1)} collective-permute-done((bf16[128,320]{1,0:T(8,128)(2,1)S(1)}, bf16[128,320]{1,0:T(8,128)(2,1)S(1)}, u32[]{:S(2)}, u32[]{:S(2)}) %collective-permute-start.8) | collective-permute-done | bytes 81952 | tf_op jit(solution)/shard_map/ppermute | solution.py:37
  39.5 1.5 %shard_map.84 = s16[8,528,128]{2,1,0:T(8,128)(2,1)} custom-call(f32[128,1024]{1,0:T(8,128)S(1)} %fusion.7.refs_0_, f32[128,1024]{1,0:T(8,128)S(1)} %fusion.14.refs_1_, f32[128,1024]{1,0:T(8,128)S(1)} %fusion.15.refs_2_, f32[128,1024]{1,0:T(8,128)S(1)} %fusion.16.refs_3_), custom_call_target="tpu_custom_call" | custom-call | tf_op jit(solution)/shard_map/pallas_call | solution.py:128
  41.0 5.2 %all-to-all-start.1 = ((s16[8,528,128]{2,1,0:T(8,128)(2,1)}), s16[8,528,128]{2,1,0:T(8,128)(2,1)S(1)}, u32[]{:S(2)}, u32[]{:S(2)}) async-start(s16[8,528,128]{2,1,0:T(8,128)(2,1)} %shard_map.84), calls=%async_computation.1 | async-start | bytes 2162688 | tf_op jit(solution)/shard_map/all_to_all | solution.py:141
  46.3 3.6 %collective-permute-start.1 = (bf16[128,1600]{1,0:T(8,128)(2,1)S(1)}, bf16[128,1600]{1,0:T(8,128)(2,1)S(1)}, u32[]{:S(2)}, u32[]{:S(2)}) collective-permute-start(bf16[128,1600]{1,0:T(8,128)(2,1)S(1)} %slice.16), channel_id=1, source_target_pairs={{0,128},{128,256},{256,384},{384,0},{1,129},{129,257},{257,385},{3... | collective-permute-start | bytes 1228808 | tf_op jit(solution)/shard_map/ppermute | solution.py:37
  49.9 2.2 %collective-permute-start.2 = (bf16[128,1600]{1,0:T(8,128)(2,1)S(1)}, bf16[128,1600]{1,0:T(8,128)(2,1)S(1)}, u32[]{:S(2)}, u32[]{:S(2)}) collective-permute-start(bf16[128,1600]{1,0:T(8,128)(2,1)S(1)} %slice.16), channel_id=1, source_target_pairs={{0,384},{128,0},{256,128},{384,256},{1,385},{129,1},{257,129},{385... | collective-permute-start | bytes 1228808 | tf_op jit(solution)/shard_map/ppermute | solution.py:37
  52.1 3.3 %collective-permute-start.3 = (bf16[128,1600]{1,0:T(8,128)(2,1)S(1)}, bf16[128,1600]{1,0:T(8,128)(2,1)S(1)}, u32[]{:S(2)}, u32[]{:S(2)}) collective-permute-start(bf16[128,1600]{1,0:T(8,128)(2,1)S(1)} %slice.16), channel_id=1, source_target_pairs={{0,256},{128,384},{256,0},{384,128},{1,257},{129,385},{257,1},{385... | collective-permute-start | bytes 1228808 | tf_op jit(solution)/shard_map/ppermute | solution.py:37
  55.7 1.7 %constant_dynamic-update-slice_fusion = bf16[1024,1600]{0,1:T(8,128)(2,1)S(1)} fusion(bf16[1024,1600]{0,1:T(8,128)(2,1)S(1)} %constant_dynamic-update-slice_fusion.1, bf16[512,1600]{0,1:T(8,128)(2,1)} %collective-permute-done), kind=kLoop, calls=%fused_computation.3 | loop fusion | bytes 3276800 | tf_op jit(solution)/shard_map/concatenate | solution.py:157
  59.4 10.7 %collective-permute-done.2 = bf16[128,1600]{1,0:T(8,128)(2,1)S(1)} collective-permute-done((bf16[128,1600]{1,0:T(8,128)(2,1)S(1)}, bf16[128,1600]{1,0:T(8,128)(2,1)S(1)}, u32[]{:S(2)}, u32[]{:S(2)}) %collective-permute-start.2) | collective-permute-done | bytes 409632 | tf_op jit(solution)/shard_map/ppermute | solution.py:37
  71.4 1.5 %shard_map.82 = s16[8,528,128]{2,1,0:T(8,128)(2,1)} custom-call(f32[128,1024]{1,0:T(8,128)S(1)} %fusion.9.refs_0_, f32[128,1024]{1,0:T(8,128)S(1)} %fusion.11.refs_1_, f32[128,1024]{1,0:T(8,128)S(1)} %fusion.12.refs_2_, f32[128,1024]{1,0:T(8,128)S(1)} %fusion.13.refs_3_), custom_call_target="tpu_custom_call" | custom-call | tf_op jit(solution)/shard_map/pallas_call | solution.py:128
  72.9 7.1 %all-to-all-start = ((s16[8,528,128]{2,1,0:T(8,128)(2,1)}), s16[8,528,128]{2,1,0:T(8,128)(2,1)S(1)}, u32[]{:S(2)}, u32[]{:S(2)}) async-start(s16[8,528,128]{2,1,0:T(8,128)(2,1)} %shard_map.82), calls=%async_computation | async-start | bytes 2162688 | tf_op jit(solution)/shard_map/all_to_all | solution.py:141
  80.8 8.2 %collective-permute-start.9 = (s16[528,128]{1,0:T(8,128)(2,1)S(1)}, s16[528,128]{1,0:T(8,128)(2,1)S(1)}, u32[]{:S(2)}, u32[]{:S(2)}) collective-permute-start(s16[528,128]{1,0:T(8,128)(2,1)S(1)} %shard_map.85.grad_own), channel_id=1, source_target_pairs={{0,1},{1,0},{2,3},{3,2},{4,5},{5,4},{6,7},{7,6},{8,9},{9,8},{10,11... | collective-permute-start | bytes 405512 | tf_op jit(solution)/shard_map/ppermute | solution.py:32
  89.0 15.0 %all-to-all-done.got = s16[8,528,128]{2,1,0:T(8,128)(2,1)S(1)} async-done(((s16[8,528,128]{2,1,0:T(8,128)(2,1)}), s16[8,528,128]{2,1,0:T(8,128)(2,1)S(1)}, u32[]{:S(2)}, u32[]{:S(2)}) %all-to-all-start) | async-done | bytes 1081376 | tf_op jit(solution)/shard_map/all_to_all | solution.py:141
  104.4 8.2 %collective-permute-start.4 = (s16[528,128]{1,0:T(8,128)(2,1)S(1)}, s16[528,128]{1,0:T(8,128)(2,1)S(1)}, u32[]{:S(2)}, u32[]{:S(2)}) collective-permute-start(s16[528,128]{1,0:T(8,128)(2,1)S(1)} %shard_map.83.act_own), channel_id=1, source_target_pairs={{0,1},{1,0},{2,3},{3,2},{4,5},{5,4},{6,7},{7,6},{8,9},{9,8},{10,11... | collective-permute-start | bytes 405512 | tf_op jit(solution)/shard_map/ppermute | solution.py:32
  112.6 3.0 %collective-permute-done.4.act_other = s16[528,128]{1,0:T(8,128)(2,1)S(1)} collective-permute-done((s16[528,128]{1,0:T(8,128)(2,1)S(1)}, s16[528,128]{1,0:T(8,128)(2,1)S(1)}, u32[]{:S(2)}, u32[]{:S(2)}) %collective-permute-start.4) | collective-permute-done | bytes 135200 | tf_op jit(solution)/shard_map/ppermute | solution.py:32
  115.9 1.9 %collective-permute-start.10 = (f32[8,512]{1,0:T(8,128)S(1)}, f32[8,512]{1,0:T(8,128)S(1)}, u32[]{:S(2)}, u32[]{:S(2)}) collective-permute-start(f32[8,512]{1,0:T(8,128)S(1)} %slice.19), channel_id=1, source_target_pairs={{0,16},{16,0},{1,17},{17,1},{2,18},{18,2},{3,19},{19,3},{4,20},{20... | collective-permute-start | bytes 49160 | tf_op jit(solution)/shard_map/ppermute | solution.py:32
  117.9 1.1 collective-permute-done.10
  119.1 14.7 %psum.7 = f32[4,8]{1,0:T(4,128)S(1)} all-reduce(f32[4,8]{1,0:T(4,128)S(1)} %fusion), channel_id=1, replica_groups=mesh['x'=4,'z'=4,'c'=2,'y'=8,'h'=2] {'y'}, use_global_device_ids=true, to_apply=%region_0.1 | all-reduce | flops 32 | bytes 256 | tf_op jit(solution)/shard_map/psum | solution.py:193
  (45 shorter events, 8.8 us)
Async XLA Ops:
  0.0 55.7 %collective-permute-start = (bf16[512,1600]{0,1:T(8,128)(2,1)}, bf16[512,1600]{0,1:T(8,128)(2,1)}, u32[]{:S(2)}, u32[]{:S(2)}) collective-permute-start(bf16[512,1600]{0,1:T(8,128)(2,1)} %param.8), channel_id=1, source_target_pairs={{0,16},{16,0},{1,17},{17,1},{2,18},{18,2},{3,19},{19,3},{4,20},{20... | collective-permute-start | bytes 4915208 | tf_op jit(solution)/shard_map/ppermute | solution.py:32
  1.9 33.7 %collective-permute-start.5 = (bf16[512,320]{0,1:T(8,128)(2,1)}, bf16[512,320]{0,1:T(8,128)(2,1)S(1)}, u32[]{:S(2)}, u32[]{:S(2)}) collective-permute-start(bf16[512,320]{0,1:T(8,128)(2,1)} %param.9), channel_id=1, source_target_pairs={{0,16},{16,0},{1,17},{17,1},{2,18},{18,2},{3,19},{19,3},{4,20},{20... | collective-permute-start | bytes 983048 | tf_op jit(solution)/shard_map/ppermute | solution.py:32
  23.5 12.5 %collective-permute-start.6 = (bf16[128,320]{1,0:T(8,128)(2,1)S(1)}, bf16[128,320]{1,0:T(8,128)(2,1)S(1)}, u32[]{:S(2)}, u32[]{:S(2)}) collective-permute-start(bf16[128,320]{1,0:T(8,128)(2,1)S(1)} %slice.17), channel_id=1, source_target_pairs={{0,128},{128,256},{256,384},{384,0},{1,129},{129,257},{257,385},{3... | collective-permute-start | bytes 245768 | tf_op jit(solution)/shard_map/ppermute | solution.py:37
  29.3 7.7 %collective-permute-start.7 = (bf16[128,320]{1,0:T(8,128)(2,1)S(1)}, bf16[128,320]{1,0:T(8,128)(2,1)S(1)}, u32[]{:S(2)}, u32[]{:S(2)}) collective-permute-start(bf16[128,320]{1,0:T(8,128)(2,1)S(1)} %slice.17), channel_id=1, source_target_pairs={{0,384},{128,0},{256,128},{384,256},{1,385},{129,1},{257,129},{385... | collective-permute-start | bytes 245768 | tf_op jit(solution)/shard_map/ppermute | solution.py:37
  31.2 8.0 %collective-permute-start.8 = (bf16[128,320]{1,0:T(8,128)(2,1)S(1)}, bf16[128,320]{1,0:T(8,128)(2,1)S(1)}, u32[]{:S(2)}, u32[]{:S(2)}) collective-permute-start(bf16[128,320]{1,0:T(8,128)(2,1)S(1)} %slice.17), channel_id=1, source_target_pairs={{0,256},{128,384},{256,0},{384,128},{1,257},{129,385},{257,1},{385... | collective-permute-start | bytes 245768 | tf_op jit(solution)/shard_map/ppermute | solution.py:37
  39.5 15.9 %copy-start = (bf16[512,1600]{0,1:T(8,128)(2,1)S(1)}, bf16[512,1600]{0,1:T(8,128)(2,1)}, u32[]{:S(2)}) copy-start(bf16[512,1600]{0,1:T(8,128)(2,1)} %param.8) | copy-start | bytes 4915204
  41.0 31.9 %all-to-all-start.1 = ((s16[8,528,128]{2,1,0:T(8,128)(2,1)}), s16[8,528,128]{2,1,0:T(8,128)(2,1)S(1)}, u32[]{:S(2)}, u32[]{:S(2)}) async-start(s16[8,528,128]{2,1,0:T(8,128)(2,1)} %shard_map.84), calls=%async_computation.1 | async-start | bytes 2162688 | tf_op jit(solution)/shard_map/all_to_all | solution.py:141
  46.3 12.4 %collective-permute-start.1 = (bf16[128,1600]{1,0:T(8,128)(2,1)S(1)}, bf16[128,1600]{1,0:T(8,128)(2,1)S(1)}, u32[]{:S(2)}, u32[]{:S(2)}) collective-permute-start(bf16[128,1600]{1,0:T(8,128)(2,1)S(1)} %slice.16), channel_id=1, source_target_pairs={{0,128},{128,256},{256,384},{384,0},{1,129},{129,257},{257,385},{3... | collective-permute-start | bytes 1228808 | tf_op jit(solution)/shard_map/ppermute | solution.py:37
  49.9 20.2 %collective-permute-start.2 = (bf16[128,1600]{1,0:T(8,128)(2,1)S(1)}, bf16[128,1600]{1,0:T(8,128)(2,1)S(1)}, u32[]{:S(2)}, u32[]{:S(2)}) collective-permute-start(bf16[128,1600]{1,0:T(8,128)(2,1)S(1)} %slice.16), channel_id=1, source_target_pairs={{0,384},{128,0},{256,128},{384,256},{1,385},{129,1},{257,129},{385... | collective-permute-start | bytes 1228808 | tf_op jit(solution)/shard_map/ppermute | solution.py:37
  52.1 18.6 %collective-permute-start.3 = (bf16[128,1600]{1,0:T(8,128)(2,1)S(1)}, bf16[128,1600]{1,0:T(8,128)(2,1)S(1)}, u32[]{:S(2)}, u32[]{:S(2)}) collective-permute-start(bf16[128,1600]{1,0:T(8,128)(2,1)S(1)} %slice.16), channel_id=1, source_target_pairs={{0,256},{128,384},{256,0},{384,128},{1,257},{129,385},{257,1},{385... | collective-permute-start | bytes 1228808 | tf_op jit(solution)/shard_map/ppermute | solution.py:37
  71.4 8.6 %copy-start.1 = (s32[1024]{0:T(1024)S(1)}, s32[1024]{0:T(1024)}, u32[]{:S(2)}) copy-start(s32[1024]{0:T(1024)} %param.14) | copy-start | bytes 12292
  71.4 8.8 %copy-start.2 = (s32[1024]{0:T(1024)S(1)}, s32[1024]{0:T(1024)}, u32[]{:S(2)}) copy-start(s32[1024]{0:T(1024)} %param.15) | copy-start | bytes 12292
  72.9 44.9 %copy-start.4 = (s32[1,512]{1,0:T(1,128)S(1)}, s32[1,512]{1,0:T(1,128)}, u32[]{:S(2)}) copy-start(s32[1,512]{1,0:T(1,128)} %param.11) | copy-start | bytes 6148
  72.9 46.1 %copy-start.3 = (s32[1,512]{1,0:T(1,128)S(1)}, s32[1,512]{1,0:T(1,128)}, u32[]{:S(2)}) copy-start(s32[1,512]{1,0:T(1,128)} %param.10) | copy-start | bytes 6148
  72.9 31.1 %all-to-all-start = ((s16[8,528,128]{2,1,0:T(8,128)(2,1)}), s16[8,528,128]{2,1,0:T(8,128)(2,1)S(1)}, u32[]{:S(2)}, u32[]{:S(2)}) async-start(s16[8,528,128]{2,1,0:T(8,128)(2,1)} %shard_map.82), calls=%async_computation | async-start | bytes 2162688 | tf_op jit(solution)/shard_map/all_to_all | solution.py:141
  80.8 31.8 %collective-permute-start.9 = (s16[528,128]{1,0:T(8,128)(2,1)S(1)}, s16[528,128]{1,0:T(8,128)(2,1)S(1)}, u32[]{:S(2)}, u32[]{:S(2)}) collective-permute-start(s16[528,128]{1,0:T(8,128)(2,1)S(1)} %shard_map.85.grad_own), channel_id=1, source_target_pairs={{0,1},{1,0},{2,3},{3,2},{4,5},{5,4},{6,7},{7,6},{8,9},{9,8},{10,11... | collective-permute-start | bytes 405512 | tf_op jit(solution)/shard_map/ppermute | solution.py:32
  104.4 11.2 %collective-permute-start.4 = (s16[528,128]{1,0:T(8,128)(2,1)S(1)}, s16[528,128]{1,0:T(8,128)(2,1)S(1)}, u32[]{:S(2)}, u32[]{:S(2)}) collective-permute-start(s16[528,128]{1,0:T(8,128)(2,1)S(1)} %shard_map.83.act_own), channel_id=1, source_target_pairs={{0,1},{1,0},{2,3},{3,2},{4,5},{5,4},{6,7},{7,6},{8,9},{9,8},{10,11... | collective-permute-start | bytes 405512 | tf_op jit(solution)/shard_map/ppermute | solution.py:32
  115.9 3.1 %collective-permute-start.10 = (f32[8,512]{1,0:T(8,128)S(1)}, f32[8,512]{1,0:T(8,128)S(1)}, u32[]{:S(2)}, u32[]{:S(2)}) collective-permute-start(f32[8,512]{1,0:T(8,128)S(1)} %slice.19), channel_id=1, source_target_pairs={{0,16},{16,0},{1,17},{17,1},{2,18},{18,2},{3,19},{19,3},{4,20},{20... | collective-permute-start | bytes 49160 | tf_op jit(solution)/shard_map/ppermute | solution.py:32

commit v5 on v2

v5 whole, which is shorter than its diff:
```python
import math

import jax
import jax.numpy as jnp
from jax import lax
from jax.experimental import pallas as pl
from jax.experimental.pallas import tpu as pltpu
from jax.sharding import Mesh, PartitionSpec as P

D = 5120
FF = 25600
SEG_LEN = 256
SEQ_PACK = 4
TEST_SEQS = 8
NX, NZ, NC, NY, NH = 4, 4, 2, 8, 2
DP = ("x", "z", "c")
FFN = ("y", "h")
LANES = 128
BLOCKS = 8
SCALE_ROWS = 16
STEPS = 128.0
TOP = 32000.0


def swap(value, axis):
    return lax.ppermute(value, axis, [(0, 1), (1, 0)])


ORDER = (3, 1, 2)


def around(value, axis):
    return [lax.ppermute(value, axis, [(i, (i + s) % 4) for i in range(4)]) for s in ORDER]


def behind(k):
    return jnp.where(k == 0, 0, jnp.where(k == 1, ORDER[0], jnp.where(k == 2, ORDER[1], ORDER[2])))


def scales(pieces):
    most = jnp.max(jnp.abs(pieces[0]), axis=0, keepdims=True)
    for p in pieces[1:]:
        most = jnp.maximum(most, jnp.max(jnp.abs(p), axis=0, keepdims=True))
    e = jnp.ceil(jnp.log(jnp.maximum(most, 1e-30)) * STEPS)
    return e, jnp.exp(e * (-1.0 / STEPS)) * TOP


def steps_of(value, factor):
    return jnp.round(value * factor).astype(jnp.int32).astype(jnp.int16)


def factors_of(tail):
    return jnp.exp(tail.astype(jnp.float32) * (1.0 / STEPS)) * (1.0 / TOP)


def tail_of(exponents):
    return jnp.concatenate(exponents, 0).astype(jnp.int32).astype(jnp.int16)


def gram_kernel(*refs):
    act, act_other, grad, grad_other = refs[-8:-4]
    out, low, a_gram, g_gram = refs[-4:]
    chunks = refs[:-8]
    wide, n = act.shape
    height = chunks[0].shape[0]
    base = wide // LANES * LANES
    low[: wide - base, :] = jnp.zeros((wide - base, 2 * n), jnp.bfloat16)
    low[wide - base :, :n] = grad[...]
    low[wide - base :, n:] = grad_other[...]
    for j, t in enumerate(chunks):
        rows = slice(j * height, (j + 1) * height)
        left = t[:, :wide]
        a_gram[rows, :n] = jnp.dot(left, act[...], preferred_element_type=jnp.float32)
        a_gram[rows, n:] = jnp.dot(left, act_other[...], preferred_element_type=jnp.float32)
        g_gram[rows, :] = jnp.dot(t[:, base:], low[...], preferred_element_type=jnp.float32)
    per = height // NY
    count = len(chunks)
    exponents = []
    for k, gram in enumerate((a_gram, g_gram)):
        for b in range(BLOCKS):
            cols = slice(b * LANES, (b + 1) * LANES)
            e, factor = scales([gram[:, cols]])
            exponents.append(e)
            for d in range(NY):
                for j in range(count):
                    top = (2 * b + k) * per * count + j * per
                    first = j * height + d * per
                    out[d, top : top + per, :] = steps_of(gram[first : first + per, cols], factor)
    tail = tail_of(exponents)
    for d in range(NY):
        out[d, 2 * BLOCKS * per * count :, :] = tail


def unpack_kernel(got, out):
    rows = (got.shape[1] - SCALE_ROWS) // (2 * BLOCKS)
    factors = [factors_of(got[s, 2 * BLOCKS * rows :, :]) for s in range(NY)]
    exponents = []
    for k in range(2):
        for b in range(BLOCKS):
            top = (2 * b + k) * rows
            at = k * BLOCKS + b
            total = jnp.zeros((rows, LANES), jnp.float32)
            for s in range(NY):
                block = got[s, top : top + rows, :].astype(jnp.float32)
                total = total + block * factors[s][at : at + 1]
            e, factor = scales([total])
            exponents.append(e)
            out[top : top + rows, :] = steps_of(total, factor)
    out[2 * BLOCKS * rows :, :] = tail_of(exponents)


def joint_kernel(*refs):
    out = refs[-1]
    groups = [refs[i : i + 3] for i in range(0, len(refs) - 1, 3)]
    totals = [0.0] * BLOCKS
    for onehot, own, other in groups:
        rows = (own.shape[0] - SCALE_ROWS) // (2 * BLOCKS)
        f_own = factors_of(own[2 * BLOCKS * rows :, :])
        f_other = factors_of(other[2 * BLOCKS * rows :, :])
        for b in range(BLOCKS):
            sums = []
            for k in range(2):
                top, at = (2 * b + k) * rows, k * BLOCKS + b
                sums.append(
                    own[top : top + rows, :].astype(jnp.float32) * f_own[at : at + 1]
                    + other[top : top + rows, :].astype(jnp.float32) * f_other[at : at + 1]
                )
            totals[b] = totals[b] + lax.dot_general(
                onehot[...],
                sums[0] * sums[1],
                (((1,), (0,)), ((), ())),
                precision=lax.Precision.HIGHEST,
                preferred_element_type=jnp.float32,
            )
    for b in range(BLOCKS):
        out[:, b * LANES : (b + 1) * LANES] = totals[b]


VMEM = pl.BlockSpec(memory_space=pltpu.VMEM)


def call(kernel, shape, dtype, *args, scratch=()):
    return pl.pallas_call(
        kernel,
        out_shape=jax.ShapeDtypeStruct(shape, dtype),
        in_specs=[VMEM] * len(args),
        out_specs=VMEM,
        scratch_shapes=list(scratch),
        compiler_params=pltpu.CompilerParams(vmem_limit_bytes=32 << 20),
    )(*args)


def sums_over_y(chunks, train):
    count = len(chunks)
    height, wide = chunks[0].shape[0], train[0].shape[0]
    tall = 2 * BLOCKS * (height // NY) * count + SCALE_ROWS
    base = wide // LANES * LANES
    tokens = 2 * train[0].shape[1]
    scratch = [
        pltpu.VMEM((chunks[0].shape[1] - base, tokens), jnp.bfloat16),
        pltpu.VMEM((count * height, tokens), jnp.float32),
        pltpu.VMEM((count * height, tokens), jnp.float32),
    ]
    packed = call(gram_kernel, (NY, tall, LANES), jnp.int16, *chunks, *train, scratch=scratch)
    got = lax.all_to_all(packed, "y", 0, 0, tiled=True)
    return call(unpack_kernel, (tall, LANES), jnp.int16, got)


def on_device(
    train_act, train_grad, train_seg, train_mask, test_act, test_grad, test_seg, test_mask
):
    x, y, z, c = (lax.axis_index(a) for a in ("x", "y", "z", "c"))
    own = jnp.concatenate([test_act, test_grad], 1)
    own = jnp.concatenate([own] + around(own, "z"), 0)
    act, grad = train_act.T, train_grad.T
    train = (act, swap(act, "c"), grad, swap(grad, "c"))
    others = around(own, "x")
    local = test_act.shape[0]
    per = own.shape[0] // NY
    packs = [sums_over_y([own], train), sums_over_y(others, train)]
    from_z = (z - behind(y * per // local)) % NZ

    def here(values):
        cut = lax.dynamic_slice(
            values.reshape(NX, NZ, NC, local), (0, from_z, c, y * per % local), (NX, 1, 1, per)
        ).reshape(NX, per)
        return [
            jnp.sum(jnp.where(jnp.arange(NX)[:, None] == (x - s) % NX, cut, 0), 0, keepdims=True)
            for s in (0,) + ORDER
        ]

    segs, masks = here(test_seg), here(test_mask)
    onehots = [
        ((seg == jnp.arange(TEST_SEQS, dtype=jnp.int32)[:, None]) & (mask != 0)).astype(jnp.float32)
        for seg, mask in zip(segs, masks)
    ]
    onehots = [onehots[0], jnp.concatenate(onehots[1:], 1)]
    args = []
    for onehot, pack in zip(onehots, packs):
        args += [onehot, pack, swap(pack, "h")]
    rows = call(joint_kernel, (TEST_SEQS, BLOCKS * LANES), jnp.float32, *args)
    n = train_act.shape[0]
    mine, theirs = rows[:, :n], rows[:, n:]
    total = mine + swap(theirs, "c")
    train_onehot = (
        (train_seg == jnp.arange(SEQ_PACK, dtype=jnp.int32)[:, None]) & (train_mask != 0)
    ).astype(jnp.float32)
    scores = lax.dot_general(
        train_onehot, total, (((1,), (1,)), ((), ())), precision=lax.Precision.HIGHEST
    )
    scores = lax.psum(scores, "y")
    return scores * (1.0 / (SEG_LEN * math.sqrt(FF * D)))


def solution(mesh):
    fine = Mesh(mesh.devices.reshape(NX, NZ, NC, NY, NH), ("x", "z", "c", "y", "h"))
    return jax.shard_map(
        on_device,
        mesh=fine,
        in_specs=(P(DP, FFN), P(DP, FFN), P(DP, None), P(DP, None), P(DP, FFN), P(DP, FFN), P(), P()),
        out_specs=P(DP, None),
        check_vma=False,
    )
```

time: 188 us -> 159 us (0.85)
  the two profiles are of different devices: /device:TPU:6 before, /device:TPU:8 now
where the time goes in v5:
time: 159 us
  starting transfers between devices  65.3 us (41%)
  waiting for transfers between devices  59.8 us (38%)
  blocking collectives  16.3 us (10%)
  local copies, waits for them, and re-layouts  9.15 us (6%)
  Pallas kernels  5.79 us (4%)
  other arithmetic  1.89 us (1%)
    all_to_all x2, waiting for transfers between devices, sums_over_y(): got = lax.all_to_all(packed, 'y', 0, 0, tiled=True)  34.6 us
    ppermute x5, starting transfers between devices, swap(): return lax.ppermute(value, axis, [(0, 1), (1, 0)])  28.2 us
    ppermute x6, starting transfers between devices, around(): lax.ppermute(value, axis, [(i, (i + s) % 4) for i in range(4)])  24.5 us
    ppermute x6, waiting for transfers between devices, around(): lax.ppermute(value, axis, [(i, (i + s) % 4) for i in range(4)])  19.7 us
    psum x1, blocking collectives, on_device(): scores = lax.psum(scores, 'y')  16.3 us
    all_to_all x2, starting transfers between devices, sums_over_y(): got = lax.all_to_all(packed, 'y', 0, 0, tiled=True)  12.6 us
    unnamed x28, local copies, waits for them, and re-layouts  8.83 us
    pallas_call x5, Pallas kernels, call(): pl.pallas_call(kernel, out_shape=jax.ShapeDtypeStruct(shape, dtype), in_s...  5.79 us
  transfers between devices with their start and end apart: 13, of which 9 were waited for; matrix products, arithmetic and copies ran while one was open for 1% of the time, Pallas kernels for 2%

profile of v5, /device:TPU:8, one launch (start us, length us, event | category | flops | bytes accessed | tf_op | source)
XLA Modules:
  0.0 158.7 jit_solution(16323732672219782294)
XLA Ops:
  0.0 1.9 %collective-permute-start.3 = (bf16[1600,512]{1,0:T(8,128)(2,1)}, bf16[1600,512]{1,0:T(8,128)(2,1)S(1)}, u32[]{:S(2)}, u32[]{:S(2)}) collective-permute-start(bf16[1600,512]{1,0:T(8,128)(2,1)} %bitcast.5), channel_id=1, source_target_pairs={{0,16},{16,0},{1,17},{17,1},{2,18},{18,2},{3,19},{19,3},{4,20},{20... | collective-permute-start | bytes 4915208 | tf_op jit(solution)/shard_map/ppermute | solution.py:26
  2.9 6.1 %collective-permute-start.2 = (bf16[32,1920]{1,0:T(8,128)(2,1)S(1)}, bf16[32,1920]{1,0:T(8,128)(2,1)S(1)}, u32[]{:S(2)}, u32[]{:S(2)}) collective-permute-start(bf16[32,1920]{1,0:T(8,128)(2,1)S(1)} %pad_maximum_fusion.1), channel_id=1, source_target_pairs={{0,64},{32,96},{64,0},{96,32},{1,65},{33,97},{65,1},{97,33},{2,66}... | collective-permute-start | bytes 368648 | tf_op jit(solution)/shard_map/ppermute | solution.py:33
  9.0 4.3 %collective-permute-start.1 = (bf16[32,1920]{1,0:T(8,128)(2,1)S(1)}, bf16[32,1920]{1,0:T(8,128)(2,1)S(1)}, u32[]{:S(2)}, u32[]{:S(2)}) collective-permute-start(bf16[32,1920]{1,0:T(8,128)(2,1)S(1)} %pad_maximum_fusion.1), channel_id=1, source_target_pairs={{0,32},{32,64},{64,96},{96,0},{1,33},{33,65},{65,97},{97,1},{2,34}... | collective-permute-start | bytes 368648 | tf_op jit(solution)/shard_map/ppermute | solution.py:33
  13.3 3.4 %collective-permute-start = (bf16[32,1920]{1,0:T(8,128)(2,1)S(1)}, bf16[32,1920]{1,0:T(8,128)(2,1)S(1)}, u32[]{:S(2)}, u32[]{:S(2)}) collective-permute-start(bf16[32,1920]{1,0:T(8,128)(2,1)S(1)} %pad_maximum_fusion.1), channel_id=1, source_target_pairs={{0,96},{32,0},{64,32},{96,64},{1,97},{33,1},{65,33},{97,65},{2,98}... | collective-permute-start | bytes 368648 | tf_op jit(solution)/shard_map/ppermute | solution.py:33
  16.7 2.2 %collective-permute-done.1 = bf16[32,1920]{1,0:T(8,128)(2,1)S(1)} collective-permute-done((bf16[32,1920]{1,0:T(8,128)(2,1)S(1)}, bf16[32,1920]{1,0:T(8,128)(2,1)S(1)}, u32[]{:S(2)}, u32[]{:S(2)}) %collective-permute-start.1) | collective-permute-done | bytes 122912 | tf_op jit(solution)/shard_map/ppermute | solution.py:33
  18.9 2.0 %collective-permute-done = bf16[32,1920]{1,0:T(8,128)(2,1)S(1)} collective-permute-done((bf16[32,1920]{1,0:T(8,128)(2,1)S(1)}, bf16[32,1920]{1,0:T(8,128)(2,1)S(1)}, u32[]{:S(2)}, u32[]{:S(2)}) %collective-permute-start) | collective-permute-done | bytes 122912 | tf_op jit(solution)/shard_map/ppermute | solution.py:33
  21.0 4.7 %collective-permute-start.6 = (bf16[128,1920]{1,0:T(8,128)(2,1)S(1)}, bf16[128,1920]{1,0:T(8,128)(2,1)S(1)}, u32[]{:S(2)}, u32[]{:S(2)}) collective-permute-start(bf16[128,1920]{1,0:T(8,128)(2,1)S(1)} %pad_maximum_fusion.refs_0_), channel_id=1, source_target_pairs={{0,384},{128,0},{256,128},{384,256},{1,385},{129,1},{257,129},{385... | collective-permute-start | bytes 1474568 | tf_op jit(solution)/shard_map/ppermute | solution.py:33
  25.7 1.9 %collective-permute-start.7 = (bf16[128,1920]{1,0:T(8,128)(2,1)S(1)}, bf16[128,1920]{1,0:T(8,128)(2,1)S(1)}, u32[]{:S(2)}, u32[]{:S(2)}) collective-permute-start(bf16[128,1920]{1,0:T(8,128)(2,1)S(1)} %pad_maximum_fusion.refs_0_), channel_id=1, source_target_pairs={{0,128},{128,256},{256,384},{384,0},{1,129},{129,257},{257,385},{3... | collective-permute-start | bytes 1474568 | tf_op jit(solution)/shard_map/ppermute | solution.py:33
  27.6 4.2 %collective-permute-start.8 = (bf16[128,1920]{1,0:T(8,128)(2,1)S(1)}, bf16[128,1920]{1,0:T(8,128)(2,1)S(1)}, u32[]{:S(2)}, u32[]{:S(2)}) collective-permute-start(bf16[128,1920]{1,0:T(8,128)(2,1)S(1)} %pad_maximum_fusion.refs_0_), channel_id=1, source_target_pairs={{0,256},{128,384},{256,0},{384,128},{1,257},{129,385},{257,1},{385... | collective-permute-start | bytes 1474568 | tf_op jit(solution)/shard_map/ppermute | solution.py:33
  32.6 1.9 %collective-permute-start.4 = (bf16[320,512]{1,0:T(8,128)(2,1)}, bf16[320,512]{1,0:T(8,128)(2,1)S(1)}, u32[]{:S(2)}, u32[]{:S(2)}) collective-permute-start(bf16[320,512]{1,0:T(8,128)(2,1)} %bitcast.8), channel_id=1, source_target_pairs={{0,16},{16,0},{1,17},{17,1},{2,18},{18,2},{3,19},{19,3},{4,20},{20... | collective-permute-start | bytes 983048 | tf_op jit(solution)/shard_map/ppermute | solution.py:26
  34.5 1.8 %collective-permute-done.4.refs_4_.refs_6_ = bf16[320,512]{1,0:T(8,128)(2,1)S(1)} collective-permute-done((bf16[320,512]{1,0:T(8,128)(2,1)}, bf16[320,512]{1,0:T(8,128)(2,1)S(1)}, u32[]{:S(2)}, u32[]{:S(2)}) %collective-permute-start.4) | collective-permute-done | bytes 327712 | tf_op jit(solution)/shard_map/ppermute | solution.py:26
  36.3 10.2 %collective-permute-done.6.refs_0_ = bf16[128,1920]{1,0:T(8,128)(2,1)S(1)} collective-permute-done((bf16[128,1920]{1,0:T(8,128)(2,1)S(1)}, bf16[128,1920]{1,0:T(8,128)(2,1)S(1)}, u32[]{:S(2)}, u32[]{:S(2)}) %collective-permute-start.6) | collective-permute-done | bytes 491552 | tf_op jit(solution)/shard_map/ppermute | solution.py:33
  46.4 5.3 %collective-permute-done.7.refs_1_ = bf16[128,1920]{1,0:T(8,128)(2,1)S(1)} collective-permute-done((bf16[128,1920]{1,0:T(8,128)(2,1)S(1)}, bf16[128,1920]{1,0:T(8,128)(2,1)S(1)}, u32[]{:S(2)}, u32[]{:S(2)}) %collective-permute-start.7) | collective-permute-done | bytes 491552 | tf_op jit(solution)/shard_map/ppermute | solution.py:33
  54.1 2.3 %shard_map.84 = s16[8,784,128]{2,1,0:T(8,128)(2,1)S(1)} custom-call(bf16[128,1920]{1,0:T(8,128)(2,1)S(1)} %collective-permute-done.6.refs_0_, bf16[128,1920]{1,0:T(8,128)(2,1)S(1)} %collective-permute-done.7.refs_1_, bf16[128,1920]{1,0:T(8,128)(2,1)S(1)} %collective-permute-done.8.refs_2_, bf16[1600,512]{1,0:T(8,128)(2,1)S(1)} %bitcast.6, ...), custom_call_target="tpu_custom_call" | custom-call | tf_op jit(solution)/shard_map/pallas_call | solution.py:143
  58.3 7.7 %all-to-all-start.1 = ((s16[8,784,128]{2,1,0:T(8,128)(2,1)}), s16[8,784,128]{2,1,0:T(8,128)(2,1)}, u32[]{:S(2)}, u32[]{:S(2)}) async-start(s16[8,784,128]{2,1,0:T(8,128)(2,1)} %copy-done.2), calls=%async_computation.1 | async-start | bytes 3211264 | tf_op jit(solution)/shard_map/all_to_all | solution.py:165
  71.2 31.8 %all-to-all-done.1.got = s16[8,784,128]{2,1,0:T(8,128)(2,1)} async-done(((s16[8,784,128]{2,1,0:T(8,128)(2,1)}), s16[8,784,128]{2,1,0:T(8,128)(2,1)}, u32[]{:S(2)}, u32[]{:S(2)}) %all-to-all-start.1) | async-done | bytes 1605664 | tf_op jit(solution)/shard_map/all_to_all | solution.py:165
  103.0 4.9 %all-to-all-start = ((s16[8,272,128]{2,1,0:T(8,128)(2,1)}), s16[8,272,128]{2,1,0:T(8,128)(2,1)S(1)}, u32[]{:S(2)}, u32[]{:S(2)}) async-start(s16[8,272,128]{2,1,0:T(8,128)(2,1)} %copy-done.3), calls=%async_computation | async-start | bytes 1114112 | tf_op jit(solution)/shard_map/all_to_all | solution.py:165
  108.0 2.0 %shard_map.85.refs_4_ = s16[784,128]{1,0:T(8,128)(2,1)S(1)} custom-call(s16[8,784,128]{2,1,0:T(8,128)(2,1)} %all-to-all-done.1.got), custom_call_target="tpu_custom_call" | custom-call | tf_op jit(solution)/shard_map/pallas_call | solution.py:143
  109.9 10.2 %collective-permute-start.9 = (s16[784,128]{1,0:T(8,128)(2,1)S(1)}, s16[784,128]{1,0:T(8,128)(2,1)S(1)}, u32[]{:S(2)}, u32[]{:S(2)}) collective-permute-start(s16[784,128]{1,0:T(8,128)(2,1)S(1)} %shard_map.85.refs_4_), channel_id=1, source_target_pairs={{0,1},{1,0},{2,3},{3,2},{4,5},{5,4},{6,7},{7,6},{8,9},{9,8},{10,11... | collective-permute-start | bytes 602120 | tf_op jit(solution)/shard_map/ppermute | solution.py:26
  120.1 2.9 %all-to-all-done.got = s16[8,272,128]{2,1,0:T(8,128)(2,1)S(1)} async-done(((s16[8,272,128]{2,1,0:T(8,128)(2,1)}), s16[8,272,128]{2,1,0:T(8,128)(2,1)S(1)}, u32[]{:S(2)}, u32[]{:S(2)}) %all-to-all-start) | async-done | bytes 557088 | tf_op jit(solution)/shard_map/all_to_all | solution.py:165
  123.2 12.3 %collective-permute-start.5 = (s16[272,128]{1,0:T(8,128)(2,1)S(1)}, s16[272,128]{1,0:T(8,128)(2,1)S(1)}, u32[]{:S(2)}, u32[]{:S(2)}) collective-permute-start(s16[272,128]{1,0:T(8,128)(2,1)S(1)} %shard_map.83.refs_1_), channel_id=1, source_target_pairs={{0,1},{1,0},{2,3},{3,2},{4,5},{5,4},{6,7},{7,6},{8,9},{9,8},{10,11... | collective-permute-start | bytes 208904 | tf_op jit(solution)/shard_map/ppermute | solution.py:26
  135.6 2.5 %collective-permute-done.5.refs_2_ = s16[272,128]{1,0:T(8,128)(2,1)S(1)} collective-permute-done((s16[272,128]{1,0:T(8,128)(2,1)S(1)}, s16[272,128]{1,0:T(8,128)(2,1)S(1)}, u32[]{:S(2)}, u32[]{:S(2)}) %collective-permute-start.5) | collective-permute-done | bytes 69664 | tf_op jit(solution)/shard_map/ppermute | solution.py:26
  138.6 1.9 %collective-permute-start.10 = (f32[8,512]{1,0:T(8,128)S(1)}, f32[8,512]{1,0:T(8,128)S(1)}, u32[]{:S(2)}, u32[]{:S(2)}) collective-permute-start(f32[8,512]{1,0:T(8,128)S(1)} %slice.9), channel_id=1, source_target_pairs={{0,16},{16,0},{1,17},{17,1},{2,18},{18,2},{3,19},{19,3},{4,20},{20... | collective-permute-start | bytes 49160 | tf_op jit(solution)/shard_map/ppermute | solution.py:26
  141.8 16.3 %psum.7 = f32[4,8]{1,0:T(4,128)S(1)} all-reduce(f32[4,8]{1,0:T(4,128)S(1)} %fusion), channel_id=1, replica_groups=mesh['x'=4,'z'=4,'c'=2,'y'=8,'h'=2] {'y'}, use_global_device_ids=true, to_apply=%region_8.9 | all-reduce | flops 32 | bytes 256 | tf_op jit(solution)/shard_map/psum | solution.py:211
  (59 shorter events, 13.8 us)
Async XLA Ops:
  0.0 51.7 %collective-permute-start.3 = (bf16[1600,512]{1,0:T(8,128)(2,1)}, bf16[1600,512]{1,0:T(8,128)(2,1)S(1)}, u32[]{:S(2)}, u32[]{:S(2)}) collective-permute-start(bf16[1600,512]{1,0:T(8,128)(2,1)} %bitcast.5), channel_id=1, source_target_pairs={{0,16},{16,0},{1,17},{17,1},{2,18},{18,2},{3,19},{19,3},{4,20},{20... | collective-permute-start | bytes 4915208 | tf_op jit(solution)/shard_map/ppermute | solution.py:26
  2.9 13.7 %collective-permute-start.2 = (bf16[32,1920]{1,0:T(8,128)(2,1)S(1)}, bf16[32,1920]{1,0:T(8,128)(2,1)S(1)}, u32[]{:S(2)}, u32[]{:S(2)}) collective-permute-start(bf16[32,1920]{1,0:T(8,128)(2,1)S(1)} %pad_maximum_fusion.1), channel_id=1, source_target_pairs={{0,64},{32,96},{64,0},{96,32},{1,65},{33,97},{65,1},{97,33},{2,66}... | collective-permute-start | bytes 368648 | tf_op jit(solution)/shard_map/ppermute | solution.py:33
  9.0 9.9 %collective-permute-start.1 = (bf16[32,1920]{1,0:T(8,128)(2,1)S(1)}, bf16[32,1920]{1,0:T(8,128)(2,1)S(1)}, u32[]{:S(2)}, u32[]{:S(2)}) collective-permute-start(bf16[32,1920]{1,0:T(8,128)(2,1)S(1)} %pad_maximum_fusion.1), channel_id=1, source_target_pairs={{0,32},{32,64},{64,96},{96,0},{1,33},{33,65},{65,97},{97,1},{2,34}... | collective-permute-start | bytes 368648 | tf_op jit(solution)/shard_map/ppermute | solution.py:33
  13.3 7.7 %collective-permute-start = (bf16[32,1920]{1,0:T(8,128)(2,1)S(1)}, bf16[32,1920]{1,0:T(8,128)(2,1)S(1)}, u32[]{:S(2)}, u32[]{:S(2)}) collective-permute-start(bf16[32,1920]{1,0:T(8,128)(2,1)S(1)} %pad_maximum_fusion.1), channel_id=1, source_target_pairs={{0,96},{32,0},{64,32},{96,64},{1,97},{33,1},{65,33},{97,65},{2,98}... | collective-permute-start | bytes 368648 | tf_op jit(solution)/shard_map/ppermute | solution.py:33
  21.0 25.5 %collective-permute-start.6 = (bf16[128,1920]{1,0:T(8,128)(2,1)S(1)}, bf16[128,1920]{1,0:T(8,128)(2,1)S(1)}, u32[]{:S(2)}, u32[]{:S(2)}) collective-permute-start(bf16[128,1920]{1,0:T(8,128)(2,1)S(1)} %pad_maximum_fusion.refs_0_), channel_id=1, source_target_pairs={{0,384},{128,0},{256,128},{384,256},{1,385},{129,1},{257,129},{385... | collective-permute-start | bytes 1474568 | tf_op jit(solution)/shard_map/ppermute | solution.py:33
  25.7 26.1 %collective-permute-start.7 = (bf16[128,1920]{1,0:T(8,128)(2,1)S(1)}, bf16[128,1920]{1,0:T(8,128)(2,1)S(1)}, u32[]{:S(2)}, u32[]{:S(2)}) collective-permute-start(bf16[128,1920]{1,0:T(8,128)(2,1)S(1)} %pad_maximum_fusion.refs_0_), channel_id=1, source_target_pairs={{0,128},{128,256},{256,384},{384,0},{1,129},{129,257},{257,385},{3... | collective-permute-start | bytes 1474568 | tf_op jit(solution)/shard_map/ppermute | solution.py:33
  27.6 24.2 %collective-permute-start.8 = (bf16[128,1920]{1,0:T(8,128)(2,1)S(1)}, bf16[128,1920]{1,0:T(8,128)(2,1)S(1)}, u32[]{:S(2)}, u32[]{:S(2)}) collective-permute-start(bf16[128,1920]{1,0:T(8,128)(2,1)S(1)} %pad_maximum_fusion.refs_0_), channel_id=1, source_target_pairs={{0,256},{128,384},{256,0},{384,128},{1,257},{129,385},{257,1},{385... | collective-permute-start | bytes 1474568 | tf_op jit(solution)/shard_map/ppermute | solution.py:33
  32.6 3.7 %collective-permute-start.4 = (bf16[320,512]{1,0:T(8,128)(2,1)}, bf16[320,512]{1,0:T(8,128)(2,1)S(1)}, u32[]{:S(2)}, u32[]{:S(2)}) collective-permute-start(bf16[320,512]{1,0:T(8,128)(2,1)} %bitcast.8), channel_id=1, source_target_pairs={{0,16},{16,0},{1,17},{17,1},{2,18},{18,2},{3,19},{19,3},{4,20},{20... | collective-permute-start | bytes 983048 | tf_op jit(solution)/shard_map/ppermute | solution.py:26
  51.7 1.4 copy-start
  53.2 1.0 copy-start.6
  56.4 1.2 copy-start.2
  58.3 7.7 %copy-start.10 = (s32[1024]{0:T(1024)S(1)}, s32[1024]{0:T(1024)}, u32[]{:S(2)}) copy-start(s32[1024]{0:T(1024)} %param.14) | copy-start | bytes 12292
  58.3 7.8 %copy-start.11 = (s32[1024]{0:T(1024)S(1)}, s32[1024]{0:T(1024)}, u32[]{:S(2)}) copy-start(s32[1024]{0:T(1024)} %param.15) | copy-start | bytes 12292
  58.3 8.2 %copy-start.1 = (bf16[512,1600]{0,1:T(8,128)(2,1)S(1)}, bf16[512,1600]{0,1:T(8,128)(2,1)}, u32[]{:S(2)}) copy-start(bf16[512,1600]{0,1:T(8,128)(2,1)} %param.8) | copy-start | bytes 4915204
  58.3 44.6 %all-to-all-start.1 = ((s16[8,784,128]{2,1,0:T(8,128)(2,1)}), s16[8,784,128]{2,1,0:T(8,128)(2,1)}, u32[]{:S(2)}, u32[]{:S(2)}) async-start(s16[8,784,128]{2,1,0:T(8,128)(2,1)} %copy-done.2), calls=%async_computation.1 | async-start | bytes 3211264 | tf_op jit(solution)/shard_map/all_to_all | solution.py:165
  66.6 1.0 copy-start.5
  67.6 1.0 copy-start.7
  68.6 1.0 copy-start.9
  103.0 20.0 %all-to-all-start = ((s16[8,272,128]{2,1,0:T(8,128)(2,1)}), s16[8,272,128]{2,1,0:T(8,128)(2,1)S(1)}, u32[]{:S(2)}, u32[]{:S(2)}) async-start(s16[8,272,128]{2,1,0:T(8,128)(2,1)} %copy-done.3), calls=%async_computation | async-start | bytes 1114112 | tf_op jit(solution)/shard_map/all_to_all | solution.py:165
  107.9 32.6 %copy-start.13 = (s32[1,512]{1,0:T(1,128)S(1)}, s32[1,512]{1,0:T(1,128)}, u32[]{:S(2)}) copy-start(s32[1,512]{1,0:T(1,128)} %param.11) | copy-start | bytes 6148
  107.9 33.8 %copy-start.12 = (s32[1,512]{1,0:T(1,128)S(1)}, s32[1,512]{1,0:T(1,128)}, u32[]{:S(2)}) copy-start(s32[1,512]{1,0:T(1,128)} %param.10) | copy-start | bytes 6148
  109.9 28.2 %collective-permute-start.9 = (s16[784,128]{1,0:T(8,128)(2,1)S(1)}, s16[784,128]{1,0:T(8,128)(2,1)S(1)}, u32[]{:S(2)}, u32[]{:S(2)}) collective-permute-start(s16[784,128]{1,0:T(8,128)(2,1)S(1)} %shard_map.85.refs_4_), channel_id=1, source_target_pairs={{0,1},{1,0},{2,3},{3,2},{4,5},{5,4},{6,7},{7,6},{8,9},{9,8},{10,11... | collective-permute-start | bytes 602120 | tf_op jit(solution)/shard_map/ppermute | solution.py:26
  123.2 14.9 %collective-permute-start.5 = (s16[272,128]{1,0:T(8,128)(2,1)S(1)}, s16[272,128]{1,0:T(8,128)(2,1)S(1)}, u32[]{:S(2)}, u32[]{:S(2)}) collective-permute-start(s16[272,128]{1,0:T(8,128)(2,1)S(1)} %shard_map.83.refs_1_), channel_id=1, source_target_pairs={{0,1},{1,0},{2,3},{3,2},{4,5},{5,4},{6,7},{7,6},{8,9},{9,8},{10,11... | collective-permute-start | bytes 208904 | tf_op jit(solution)/shard_map/ppermute | solution.py:26
  138.6 3.1 %collective-permute-start.10 = (f32[8,512]{1,0:T(8,128)S(1)}, f32[8,512]{1,0:T(8,128)S(1)}, u32[]{:S(2)}, u32[]{:S(2)}) collective-permute-start(f32[8,512]{1,0:T(8,128)S(1)} %slice.9), channel_id=1, source_target_pairs={{0,16},{16,0},{1,17},{17,1},{2,18},{18,2},{3,19},{19,3},{4,20},{20... | collective-permute-start | bytes 49160 | tf_op jit(solution)/shard_map/ppermute | solution.py:26
  (3 other events, 2.3 us)

commit v6 on v4

--- a/solution.py
+++ b/solution.py
@@ -85,6 +85,25 @@
     pack(Pieces(chunks[0].shape[1] // LANES, pieces), out, [(d,) for d in range(NY)])
 
 
+def grad_kernel(order, test, own, other, out, gram):
+    n = own.shape[1]
+    gram[:, :n] = jnp.dot(test[...], own[...], preferred_element_type=jnp.float32)
+    gram[:, n:] = jnp.dot(test[...], other[...], preferred_element_type=jnp.float32)
+    height = test.shape[0] // NX
+    rows = test.shape[0] // NY
+    per = height // rows
+
+    def pieces(b):
+        cols = slice(b * LANES, (b + 1) * LANES)
+        found = []
+        for d in range(NY):
+            first = pl.multiple_of(order[d // per] * height + (d % per) * rows, rows)
+            found.append(gram[pl.ds(first, rows), cols])
+        return found
+
+    pack(Pieces(2 * n // LANES, pieces), out, [(d,) for d in range(NY)])
+
+
 def unpack_kernel(got, out):
     blocks = BLOCKS
     rows = (got.shape[1] - SCALE_ROWS) // blocks
@@ -134,12 +153,26 @@
     )(*args)
 
 
-def sum_over_y(chunks):
+def sum_over_y(packed):
+    got = lax.all_to_all(packed, "y", 0, 0, tiled=True)
+    return call(unpack_kernel, packed.shape[1:], jnp.int16, got)
+
+
+def pack_acts(chunks):
     rows = chunks[0].shape[0] * len(chunks) // NY
-    height = BLOCKS * rows + SCALE_ROWS
-    packed = call(pack_kernel, (NY, height, LANES), jnp.int16, *chunks)
-    got = lax.all_to_all(packed, "y", 0, 0, tiled=True)
-    return call(unpack_kernel, (height, LANES), jnp.int16, got)
+    return call(pack_kernel, (NY, BLOCKS * rows + SCALE_ROWS, LANES), jnp.int16, *chunks)
+
+
+def pack_grads(order, test, own, other):
+    rows = test.shape[0] // NY
+    return pl.pallas_call(
+        grad_kernel,
+        out_shape=jax.ShapeDtypeStruct((NY, BLOCKS * rows + SCALE_ROWS, LANES), jnp.int16),
+        in_specs=[pl.BlockSpec(memory_space=pltpu.SMEM), VMEM, VMEM, VMEM],
+        out_specs=VMEM,
+        scratch_shapes=[pltpu.VMEM((test.shape[0], 2 * own.shape[1]), jnp.float32)],
+        compiler_params=pltpu.CompilerParams(vmem_limit_bytes=24 << 20),
+    )(order, test, own, other)
 
 
 def on_device(
@@ -149,16 +182,17 @@
     wide = test_act.shape[1]
     both_z = lax.all_gather(jnp.concatenate([test_act, test_grad], 1), "z", axis=0, tiled=True)
     act_z, grad_z = both_z[:, :wide], both_z[:, wide:]
-    other_grad, other_act = swap(train_grad, "c"), swap(train_act, "c")
-    grads = over_x(grad_z)
+    other_grad, other_act = swap(train_grad.T, "c"), swap(train_act, "c")
+    grads = lax.all_gather(grad_z, "x", axis=0, tiled=True)
     acts = over_x(act_z)
 
     def grams(chunks, own, other):
         both = jnp.concatenate([own, other], 0)
         return [cross_rows(t, both) for t in chunks]
 
-    grad_y = sum_over_y(grams(grads, train_grad, other_grad))
-    act_y = sum_over_y(grams(acts, train_act, other_act))
+    order = jnp.stack([(x - step) % NX for step in (0, 1, 3, 2)])
+    grad_y = sum_over_y(pack_grads(order, grads, train_grad.T, other_grad))
+    act_y = sum_over_y(pack_acts(grams(acts, train_act, other_act)))
     behind = (y // 2) ^ (y // 4)
     local = test_act.shape[0]
     seg, mask = (
@@ -182,15 +216,20 @@
         grad_other,
     )
     n = train_act.shape[0]
-    mine, theirs = rows[:, :n], rows[:, n:]
-    total = mine + swap(theirs, "c")
-    train_onehot = (
-        (train_seg == jnp.arange(SEQ_PACK, dtype=jnp.int32)[:, None]) & (train_mask != 0)
-    ).astype(jnp.float32)
-    scores = lax.dot_general(
-        train_onehot, total, (((1,), (1,)), ((), ())), precision=lax.Precision.HIGHEST
-    )
-    scores = lax.psum(scores, "y")
+    masked = jnp.where(train_mask != 0, train_seg, -1)
+
+    def by_sequence(of, values):
+        train_onehot = (of == jnp.arange(SEQ_PACK, dtype=jnp.int32)[:, None]).astype(jnp.float32)
+        scores = lax.dot_general(
+            train_onehot, values, (((1,), (1,)), ((), ())), precision=lax.Precision.HIGHEST
+        )
+        return jnp.pad(scores, ((0, 4), (0, LANES - TEST_SEQS)))
+
+    mine, theirs = by_sequence(masked, rows[:, :n]), by_sequence(swap(masked, "c"), rows[:, n:])
+    to = jnp.arange(NY * NC)[:, None, None] % NC
+    spread = jnp.where(to == c, mine[None], theirs[None])
+    got = lax.all_to_all(spread, ("y", "c"), 0, 0, tiled=True)
+    scores = jnp.sum(got, 0)[:SEQ_PACK, :TEST_SEQS]
     return scores * (1.0 / (SEG_LEN * math.sqrt(FF * D)))
 
 

time: 135 us -> 129 us (0.956)
  the two profiles are of different devices: /device:TPU:6 before, /device:TPU:1 now
where the time goes in v6:
time: 129 us; the launch traced here: 128 us
  starting transfers between devices  54 us (42%)
  blocking collectives  38.5 us (30%)
  waiting for transfers between devices  21.7 us (17%)
  Pallas kernels  5.34 us (4%)
  local copies, waits for them, and re-layouts  3.42 us (3%)
  matrix products  2.9 us (2%)
  other arithmetic  1.93 us (1%)
    ppermute x5, starting transfers between devices, swap(): return lax.ppermute(value, axis, [(0, 1), (1, 0)])  33.9 us
    all_to_all x1, blocking collectives, on_device(): got = lax.all_to_all(spread, ('y', 'c'), 0, 0, tiled=True)  15.9 us
    all_gather x1, blocking collectives, on_device(): lax.all_gather(jnp.concatenate([test_act, test_grad], 1), 'z', axis=0, ti...  12.2 us
    all_to_all x2, waiting for transfers between devices, sum_over_y(): got = lax.all_to_all(packed, 'y', 0, 0, tiled=True)  11.2 us
    all_gather x1, blocking collectives, on_device(): grads = lax.all_gather(grad_z, 'x', axis=0, tiled=True)  10.4 us
    all_to_all x2, starting transfers between devices, sum_over_y(): got = lax.all_to_all(packed, 'y', 0, 0, tiled=True)  10.4 us
    ppermute x3, starting transfers between devices, over_x(): lax.ppermute(value, 'x', [(i, (i + step) % NX) for i in range(NX)])  9.77 us
    ppermute x3, waiting for transfers between devices, over_x(): lax.ppermute(value, 'x', [(i, (i + step) % NX) for i in range(NX)])  8.11 us
  transfers between devices with their start and end apart: 10, of which 4 were waited for; matrix products, arithmetic and copies ran while one was open for 5% of the time, Pallas kernels for 4%

profile of v6, /device:TPU:1, one launch (start us, length us, event | category | flops | bytes accessed | tf_op | source)
XLA Modules:
  0.0 128.2 jit_solution(13924733346562589493)
XLA Ops:
  0.0 8.8 %collective-permute-start = (bf16[512,1600]{0,1:T(8,128)(2,1)}, bf16[512,1600]{0,1:T(8,128)(2,1)}, u32[]{:S(2)}, u32[]{:S(2)}) collective-permute-start(bf16[512,1600]{0,1:T(8,128)(2,1)} %param.8), channel_id=1, source_target_pairs={{0,16},{16,0},{1,17},{17,1},{2,18},{18,2},{3,19},{19,3},{4,20},{20... | collective-permute-start | bytes 4915208 | tf_op jit(solution)/shard_map/ppermute | solution.py:32
  8.8 1.9 %collective-permute-start.5 = (bf16[320,512]{1,0:T(8,128)(2,1)}, bf16[320,512]{1,0:T(8,128)(2,1)S(1)}, u32[]{:S(2)}, u32[]{:S(2)}) collective-permute-start(bf16[320,512]{1,0:T(8,128)(2,1)} %bitcast.14), channel_id=1, source_target_pairs={{0,16},{16,0},{1,17},{17,1},{2,18},{18,2},{3,19},{19,3},{4,20},{20... | collective-permute-start | bytes 983048 | tf_op jit(solution)/shard_map/ppermute | solution.py:32
  10.7 1.1 pad_maximum_fusion
  11.8 12.2 %all_gather.6 = bf16[128,1920]{1,0:T(8,128)(2,1)S(1)} all-gather(bf16[32,1920]{1,0:T(8,128)(2,1)S(1)} %pad_maximum_fusion), channel_id=1, replica_groups=mesh['x'=4,'z'=4,'c'=2,'y'=8,'h'=2] {'z'}, dimensions={0}, use_global_device_ids=true | all-gather | bytes 614400 | tf_op jit(solution)/shard_map/all_gather | solution.py:183
  24.3 10.4 %all_gather.7.test = bf16[512,320]{1,0:T(8,128)(2,1)S(1)} all-gather(bf16[128,320]{1,0:T(8,128)(2,1)S(1)} %slice.21), channel_id=1, replica_groups=mesh['x'=4,'z'=4,'c'=2,'y'=8,'h'=2] {'x'}, dimensions={0}, use_global_device_ids=true | all-gather | bytes 409600 | tf_op jit(solution)/shard_map/all_gather | solution.py:186
  34.7 1.0 copy-done
  35.6 2.8 %shard_map.84 = s16[8,528,128]{2,1,0:T(8,128)(2,1)} custom-call(s32[4]{0:T(128)S(1)} %pad_add_fusion.order, bf16[512,320]{1,0:T(8,128)(2,1)S(1)} %all_gather.7.test, bf16[320,512]{1,0:T(8,128)(2,1)S(1)} %bitcast.15, bf16[320,512]{1,0:T(8,128)(2,1)S(1)} %collective-permute-done.5.other), custom_call_target="tpu_custom_call" | custom-call | tf_op jit(solution)/shard_map/pallas_call | solution.py:168
  38.4 5.4 %all-to-all-start.1 = ((s16[8,528,128]{2,1,0:T(8,128)(2,1)}), s16[8,528,128]{2,1,0:T(8,128)(2,1)S(1)}, u32[]{:S(2)}, u32[]{:S(2)}) async-start(s16[8,528,128]{2,1,0:T(8,128)(2,1)} %shard_map.84), calls=%async_computation.1 | async-start | bytes 2162688 | tf_op jit(solution)/shard_map/all_to_all | solution.py:157
  43.8 3.5 %collective-permute-start.1 = (bf16[128,1600]{1,0:T(8,128)(2,1)S(1)}, bf16[128,1600]{1,0:T(8,128)(2,1)S(1)}, u32[]{:S(2)}, u32[]{:S(2)}) collective-permute-start(bf16[128,1600]{1,0:T(8,128)(2,1)S(1)} %slice.20), channel_id=1, source_target_pairs={{0,128},{128,256},{256,384},{384,0},{1,129},{129,257},{257,385},{3... | collective-permute-start | bytes 1228808 | tf_op jit(solution)/shard_map/ppermute | solution.py:37
  47.4 3.1 %collective-permute-start.2 = (bf16[128,1600]{1,0:T(8,128)(2,1)S(1)}, bf16[128,1600]{1,0:T(8,128)(2,1)S(1)}, u32[]{:S(2)}, u32[]{:S(2)}) collective-permute-start(bf16[128,1600]{1,0:T(8,128)(2,1)S(1)} %slice.20), channel_id=1, source_target_pairs={{0,384},{128,0},{256,128},{384,256},{1,385},{129,1},{257,129},{385... | collective-permute-start | bytes 1228808 | tf_op jit(solution)/shard_map/ppermute | solution.py:37
  50.5 3.1 %collective-permute-start.3 = (bf16[128,1600]{1,0:T(8,128)(2,1)S(1)}, bf16[128,1600]{1,0:T(8,128)(2,1)S(1)}, u32[]{:S(2)}, u32[]{:S(2)}) collective-permute-start(bf16[128,1600]{1,0:T(8,128)(2,1)S(1)} %slice.20), channel_id=1, source_target_pairs={{0,256},{128,384},{256,0},{384,128},{1,257},{129,385},{257,1},{385... | collective-permute-start | bytes 1228808 | tf_op jit(solution)/shard_map/ppermute | solution.py:37
  53.9 1.7 %constant_dynamic-update-slice_fusion = bf16[1024,1600]{0,1:T(8,128)(2,1)S(1)} fusion(bf16[1024,1600]{0,1:T(8,128)(2,1)S(1)} %constant_dynamic-update-slice_fusion.1, bf16[512,1600]{0,1:T(8,128)(2,1)} %collective-permute-done), kind=kLoop, calls=%fused_computation.9 | loop fusion | bytes 3276800 | tf_op jit(solution)/shard_map/concatenate | solution.py:190
  55.5 0.7 fusion.9.refs_0_
  56.2 0.7 fusion.11.refs_1_
  57.6 8.1 %collective-permute-done.3 = bf16[128,1600]{1,0:T(8,128)(2,1)S(1)} collective-permute-done((bf16[128,1600]{1,0:T(8,128)(2,1)S(1)}, bf16[128,1600]{1,0:T(8,128)(2,1)S(1)}, u32[]{:S(2)}, u32[]{:S(2)}) %collective-permute-start.3) | collective-permute-done | bytes 409632 | tf_op jit(solution)/shard_map/ppermute | solution.py:37
  66.4 1.5 %shard_map.82 = s16[8,528,128]{2,1,0:T(8,128)(2,1)} custom-call(f32[128,1024]{1,0:T(8,128)S(1)} %fusion.9.refs_0_, f32[128,1024]{1,0:T(8,128)S(1)} %fusion.11.refs_1_, f32[128,1024]{1,0:T(8,128)S(1)} %fusion.12.refs_2_, f32[128,1024]{1,0:T(8,128)S(1)} %fusion.13.refs_3_), custom_call_target="tpu_custom_call" | custom-call | tf_op jit(solution)/shard_map/pallas_call | solution.py:147
  67.9 1.6 %all-to-all-done.1.got = s16[8,528,128]{2,1,0:T(8,128)(2,1)S(1)} async-done(((s16[8,528,128]{2,1,0:T(8,128)(2,1)}), s16[8,528,128]{2,1,0:T(8,128)(2,1)S(1)}, u32[]{:S(2)}, u32[]{:S(2)}) %all-to-all-start.1) | async-done | bytes 1081376 | tf_op jit(solution)/shard_map/all_to_all | solution.py:157
  69.5 5.0 %all-to-all-start = ((s16[8,528,128]{2,1,0:T(8,128)(2,1)}), s16[8,528,128]{2,1,0:T(8,128)(2,1)S(1)}, u32[]{:S(2)}, u32[]{:S(2)}) async-start(s16[8,528,128]{2,1,0:T(8,128)(2,1)} %shard_map.82), calls=%async_computation | async-start | bytes 2162688 | tf_op jit(solution)/shard_map/all_to_all | solution.py:157
  74.5 7.3 %collective-permute-start.7 = (s32[1,512]{1,0:T(1,128)S(1)}, s32[1,512]{1,0:T(1,128)S(1)}, u32[]{:S(2)}, u32[]{:S(2)}) collective-permute-start(s32[1,512]{1,0:T(1,128)S(1)} %compare_select_fusion), channel_id=1, source_target_pairs={{0,16},{16,0},{1,17},{17,1},{2,18},{18,2},{3,19},{19,3},{4,20},{20... | collective-permute-start | bytes 6152 | tf_op jit(solution)/shard_map/ppermute | solution.py:32
  82.7 7.9 %collective-permute-start.6 = (s16[528,128]{1,0:T(8,128)(2,1)S(1)}, s16[528,128]{1,0:T(8,128)(2,1)S(1)}, u32[]{:S(2)}, u32[]{:S(2)}) collective-permute-start(s16[528,128]{1,0:T(8,128)(2,1)S(1)} %shard_map.85.grad_own), channel_id=1, source_target_pairs={{0,1},{1,0},{2,3},{3,2},{4,5},{5,4},{6,7},{7,6},{8,9},{9,8},{10,11... | collective-permute-start | bytes 405512 | tf_op jit(solution)/shard_map/ppermute | solution.py:32
  90.6 9.6 %all-to-all-done.got = s16[8,528,128]{2,1,0:T(8,128)(2,1)S(1)} async-done(((s16[8,528,128]{2,1,0:T(8,128)(2,1)}), s16[8,528,128]{2,1,0:T(8,128)(2,1)S(1)}, u32[]{:S(2)}, u32[]{:S(2)}) %all-to-all-start) | async-done | bytes 1081376 | tf_op jit(solution)/shard_map/all_to_all | solution.py:157
  100.6 7.9 %collective-permute-start.4 = (s16[528,128]{1,0:T(8,128)(2,1)S(1)}, s16[528,128]{1,0:T(8,128)(2,1)S(1)}, u32[]{:S(2)}, u32[]{:S(2)}) collective-permute-start(s16[528,128]{1,0:T(8,128)(2,1)S(1)} %shard_map.83.act_own), channel_id=1, source_target_pairs={{0,1},{1,0},{2,3},{3,2},{4,5},{5,4},{6,7},{7,6},{8,9},{9,8},{10,11... | collective-permute-start | bytes 405512 | tf_op jit(solution)/shard_map/ppermute | solution.py:32
  108.6 2.3 %collective-permute-done.4.act_other = s16[528,128]{1,0:T(8,128)(2,1)S(1)} collective-permute-done((s16[528,128]{1,0:T(8,128)(2,1)S(1)}, s16[528,128]{1,0:T(8,128)(2,1)S(1)}, u32[]{:S(2)}, u32[]{:S(2)}) %collective-permute-start.4) | collective-permute-done | bytes 135200 | tf_op jit(solution)/shard_map/ppermute | solution.py:32
  111.7 15.9 %all_to_all.15 = f32[16,8,128]{2,1,0:T(8,128)S(1)} all-to-all(f32[16,8,128]{2,1,0:T(8,128)S(1)} %broadcast_select_fusion), channel_id=1, replica_groups=mesh['x'=4,'z'=4,'c'=2,'y'=8,'h'=2] {'y','c'}, dimensions={0} | all-to-all | bytes 131072 | tf_op jit(solution)/shard_map/all_to_all | solution.py:231
  (42 shorter events, 4.2 us)
Async XLA Ops:
  0.0 53.9 %collective-permute-start = (bf16[512,1600]{0,1:T(8,128)(2,1)}, bf16[512,1600]{0,1:T(8,128)(2,1)}, u32[]{:S(2)}, u32[]{:S(2)}) collective-permute-start(bf16[512,1600]{0,1:T(8,128)(2,1)} %param.8), channel_id=1, source_target_pairs={{0,16},{16,0},{1,17},{17,1},{2,18},{18,2},{3,19},{19,3},{4,20},{20... | collective-permute-start | bytes 4915208 | tf_op jit(solution)/shard_map/ppermute | solution.py:32
  8.8 25.9 %collective-permute-start.5 = (bf16[320,512]{1,0:T(8,128)(2,1)}, bf16[320,512]{1,0:T(8,128)(2,1)S(1)}, u32[]{:S(2)}, u32[]{:S(2)}) collective-permute-start(bf16[320,512]{1,0:T(8,128)(2,1)} %bitcast.14), channel_id=1, source_target_pairs={{0,16},{16,0},{1,17},{17,1},{2,18},{18,2},{3,19},{19,3},{4,20},{20... | collective-permute-start | bytes 983048 | tf_op jit(solution)/shard_map/ppermute | solution.py:32
  10.7 42.9 %copy-start.1 = (bf16[512,1600]{0,1:T(8,128)(2,1)S(1)}, bf16[512,1600]{0,1:T(8,128)(2,1)}, u32[]{:S(2)}) copy-start(bf16[512,1600]{0,1:T(8,128)(2,1)} %param.8) | copy-start | bytes 4915204
  34.7 1.0 copy-start
  38.4 31.1 %all-to-all-start.1 = ((s16[8,528,128]{2,1,0:T(8,128)(2,1)}), s16[8,528,128]{2,1,0:T(8,128)(2,1)S(1)}, u32[]{:S(2)}, u32[]{:S(2)}) async-start(s16[8,528,128]{2,1,0:T(8,128)(2,1)} %shard_map.84), calls=%async_computation.1 | async-start | bytes 2162688 | tf_op jit(solution)/shard_map/all_to_all | solution.py:157
  43.8 12.4 %collective-permute-start.1 = (bf16[128,1600]{1,0:T(8,128)(2,1)S(1)}, bf16[128,1600]{1,0:T(8,128)(2,1)S(1)}, u32[]{:S(2)}, u32[]{:S(2)}) collective-permute-start(bf16[128,1600]{1,0:T(8,128)(2,1)S(1)} %slice.20), channel_id=1, source_target_pairs={{0,128},{128,256},{256,384},{384,0},{1,129},{129,257},{257,385},{3... | collective-permute-start | bytes 1228808 | tf_op jit(solution)/shard_map/ppermute | solution.py:37
  47.4 9.6 %collective-permute-start.2 = (bf16[128,1600]{1,0:T(8,128)(2,1)S(1)}, bf16[128,1600]{1,0:T(8,128)(2,1)S(1)}, u32[]{:S(2)}, u32[]{:S(2)}) collective-permute-start(bf16[128,1600]{1,0:T(8,128)(2,1)S(1)} %slice.20), channel_id=1, source_target_pairs={{0,384},{128,0},{256,128},{384,256},{1,385},{129,1},{257,129},{385... | collective-permute-start | bytes 1228808 | tf_op jit(solution)/shard_map/ppermute | solution.py:37
  50.5 15.2 %collective-permute-start.3 = (bf16[128,1600]{1,0:T(8,128)(2,1)S(1)}, bf16[128,1600]{1,0:T(8,128)(2,1)S(1)}, u32[]{:S(2)}, u32[]{:S(2)}) collective-permute-start(bf16[128,1600]{1,0:T(8,128)(2,1)S(1)} %slice.20), channel_id=1, source_target_pairs={{0,256},{128,384},{256,0},{384,128},{1,257},{129,385},{257,1},{385... | collective-permute-start | bytes 1228808 | tf_op jit(solution)/shard_map/ppermute | solution.py:37
  66.3 8.1 %copy-start.4 = (s32[1,512]{1,0:T(1,128)S(1)}, s32[1,512]{1,0:T(1,128)}, u32[]{:S(2)}) copy-start(s32[1,512]{1,0:T(1,128)} %param.10) | copy-start | bytes 6148
  66.4 8.1 %copy-start.5 = (s32[1,512]{1,0:T(1,128)S(1)}, s32[1,512]{1,0:T(1,128)}, u32[]{:S(2)}) copy-start(s32[1,512]{1,0:T(1,128)} %param.11) | copy-start | bytes 6148
  66.4 15.5 %copy-start.2 = (s32[1024]{0:T(1024)S(1)}, s32[1024]{0:T(1024)}, u32[]{:S(2)}) copy-start(s32[1024]{0:T(1024)} %param.14) | copy-start | bytes 12292
  66.4 15.7 %copy-start.3 = (s32[1024]{0:T(1024)S(1)}, s32[1024]{0:T(1024)}, u32[]{:S(2)}) copy-start(s32[1024]{0:T(1024)} %param.15) | copy-start | bytes 12292
  69.5 30.7 %all-to-all-start = ((s16[8,528,128]{2,1,0:T(8,128)(2,1)}), s16[8,528,128]{2,1,0:T(8,128)(2,1)S(1)}, u32[]{:S(2)}, u32[]{:S(2)}) async-start(s16[8,528,128]{2,1,0:T(8,128)(2,1)} %shard_map.82), calls=%async_computation | async-start | bytes 2162688 | tf_op jit(solution)/shard_map/all_to_all | solution.py:157
  74.5 36.8 %collective-permute-start.7 = (s32[1,512]{1,0:T(1,128)S(1)}, s32[1,512]{1,0:T(1,128)S(1)}, u32[]{:S(2)}, u32[]{:S(2)}) collective-permute-start(s32[1,512]{1,0:T(1,128)S(1)} %compare_select_fusion), channel_id=1, source_target_pairs={{0,16},{16,0},{1,17},{17,1},{2,18},{18,2},{3,19},{19,3},{4,20},{20... | collective-permute-start | bytes 6152 | tf_op jit(solution)/shard_map/ppermute | solution.py:32
  82.7 25.9 %collective-permute-start.6 = (s16[528,128]{1,0:T(8,128)(2,1)S(1)}, s16[528,128]{1,0:T(8,128)(2,1)S(1)}, u32[]{:S(2)}, u32[]{:S(2)}) collective-permute-start(s16[528,128]{1,0:T(8,128)(2,1)S(1)} %shard_map.85.grad_own), channel_id=1, source_target_pairs={{0,1},{1,0},{2,3},{3,2},{4,5},{5,4},{6,7},{7,6},{8,9},{9,8},{10,11... | collective-permute-start | bytes 405512 | tf_op jit(solution)/shard_map/ppermute | solution.py:32
  100.6 10.3 %collective-permute-start.4 = (s16[528,128]{1,0:T(8,128)(2,1)S(1)}, s16[528,128]{1,0:T(8,128)(2,1)S(1)}, u32[]{:S(2)}, u32[]{:S(2)}) collective-permute-start(s16[528,128]{1,0:T(8,128)(2,1)S(1)} %shard_map.83.act_own), channel_id=1, source_target_pairs={{0,1},{1,0},{2,3},{3,2},{4,5},{5,4},{6,7},{7,6},{8,9},{9,8},{10,11... | collective-permute-start | bytes 405512 | tf_op jit(solution)/shard_map/ppermute | solution.py:32

commit v7 on v6

v7 whole, which is shorter than its diff:
```python
import math

import jax
import jax.numpy as jnp
from jax import lax
from jax.experimental import pallas as pl
from jax.experimental.pallas import tpu as pltpu
from jax.sharding import Mesh, PartitionSpec as P

D = 5120
FF = 25600
SEG_LEN = 256
SEQ_PACK = 4
TEST_SEQS = 8
NX, NZ, NC, NY, NH = 4, 4, 2, 8, 2
DP = ("x", "z", "c")
FFN = ("y", "h")
LANES = 128
BLOCKS = 8
SCALE_ROWS = 16
STEPS = 128.0
TOP = 32000.0


def cross_rows(left, right):
    return lax.dot_general(
        left, right, (((1,), (1,)), ((), ())), preferred_element_type=jnp.float32
    )


def swap(value, axis):
    return lax.ppermute(value, axis, [(0, 1), (1, 0)])


ORDER = (1, 3, 2)
REGIONS = ((0, 64), (BLOCKS * 64 + SCALE_ROWS, 16))


def around(value, axis):
    return [value] + [
        lax.ppermute(value, axis, [(i, (i + step) % 4) for i in range(4)]) for step in ORDER
    ]


def step_of(k):
    return k ^ (k // 2)


def pack(parts, out, lead, base=0):
    blocks = parts.blocks
    exponents = []
    for b in range(blocks):
        pieces = parts(b)
        rows = pieces[0].shape[0]
        most = jnp.max(jnp.abs(pieces[0]), axis=0, keepdims=True)
        for p in pieces[1:]:
            most = jnp.maximum(most, jnp.max(jnp.abs(p), axis=0, keepdims=True))
        e = jnp.ceil(jnp.log(jnp.maximum(most, 1e-30)) * STEPS)
        factor = jnp.exp(e * (-1.0 / STEPS)) * TOP
        exponents.append(e)
        for i, p in enumerate(pieces):
            q = jnp.round(p * factor).astype(jnp.int32).astype(jnp.int16)
            out[lead[i] + (slice(base + b * rows, base + (b + 1) * rows), slice(None))] = q
    pad = [jnp.zeros((SCALE_ROWS - blocks, LANES), jnp.float32)]
    tail = jnp.concatenate(exponents + pad, 0).astype(jnp.int32).astype(jnp.int16)
    top = base + blocks * rows
    for at in lead:
        out[at + (slice(top, top + SCALE_ROWS), slice(None))] = tail


class Pieces:
    def __init__(self, blocks, get):
        self.blocks, self.get = blocks, get

    def __call__(self, b):
        return self.get(b)


def factors_of(tail):
    return jnp.exp(tail.astype(jnp.float32) * (1.0 / STEPS)) * (1.0 / TOP)


def pack_kernel(*refs):
    chunks, out = refs[:-1], refs[-1]
    per = chunks[0].shape[0] // NY

    def pieces(b):
        cols = slice(b * LANES, (b + 1) * LANES)
        return [
            jnp.concatenate([r[d * per : (d + 1) * per, cols] for r in chunks], 0) for d in range(NY)
        ]

    pack(Pieces(BLOCKS, pieces), out, [(d,) for d in range(NY)])


def first_kernel(order, test, own, other, act_gram, out, gram):
    n = own.shape[1]
    gram[:, :n] = jnp.dot(test[...], own[...], preferred_element_type=jnp.float32)
    gram[:, n:] = jnp.dot(test[...], other[...], preferred_element_type=jnp.float32)
    height = test.shape[0] // NX
    per = height // NY

    def grads(b):
        cols = slice(b * LANES, (b + 1) * LANES)
        found = []
        for d in range(NY):
            firsts = [pl.multiple_of(order[j] * height + d * per, per) for j in range(NX)]
            found.append(jnp.concatenate([gram[pl.ds(f, per), cols] for f in firsts], 0))
        return found

    def acts(b):
        cols = slice(b * LANES, (b + 1) * LANES)
        return [act_gram[d * per : (d + 1) * per, cols] for d in range(NY)]

    lead = [(d,) for d in range(NY)]
    for (base, _), get in zip(REGIONS, (grads, acts)):
        pack(Pieces(BLOCKS, get), out, lead, base)


def unpack(got, out, base, rows):
    top = base + BLOCKS * rows
    factors = [factors_of(got[s, top : top + SCALE_ROWS, :]) for s in range(NY)]

    def pieces(b):
        total = jnp.zeros((rows, LANES), jnp.float32)
        for s in range(NY):
            block = got[s, base + b * rows : base + (b + 1) * rows, :].astype(jnp.float32)
            total = total + block * factors[s][b : b + 1]
        return [total]

    pack(Pieces(BLOCKS, pieces), out, [()], base)


def unpack_first_kernel(got, out):
    for base, rows in REGIONS:
        unpack(got, out, base, rows)


def unpack_kernel(got, out):
    unpack(got, out, 0, (got.shape[1] - SCALE_ROWS) // BLOCKS)


def joint_kernel(onehot, first_own, first_other, rest_own, rest_other, out):
    def reader(own, other, base, rows):
        top = base + BLOCKS * rows
        f_own = factors_of(own[top : top + SCALE_ROWS, :])
        f_other = factors_of(other[top : top + SCALE_ROWS, :])

        def read(b):
            at = slice(base + b * rows, base + (b + 1) * rows)
            return (
                own[at, :].astype(jnp.float32) * f_own[b : b + 1]
                + other[at, :].astype(jnp.float32) * f_other[b : b + 1]
            )

        return read

    grads = reader(first_own, first_other, *REGIONS[0])
    acts = reader(first_own, first_other, *REGIONS[1])
    rest = reader(rest_own, rest_other, 0, (rest_own.shape[0] - SCALE_ROWS) // BLOCKS)
    for b in range(BLOCKS):
        joint = jnp.concatenate([acts(b), rest(b)], 0) * grads(b)
        out[:, b * LANES : (b + 1) * LANES] = lax.dot_general(
            onehot[...],
            joint,
            (((1,), (0,)), ((), ())),
            precision=lax.Precision.HIGHEST,
            preferred_element_type=jnp.float32,
        )


VMEM = pl.BlockSpec(memory_space=pltpu.VMEM)


def call(kernel, shape, dtype, *args):
    return pl.pallas_call(
        kernel,
        out_shape=jax.ShapeDtypeStruct(shape, dtype),
        in_specs=[VMEM] * len(args),
        out_specs=VMEM,
        compiler_params=pltpu.CompilerParams(vmem_limit_bytes=24 << 20),
    )(*args)


def sum_over_y(packed, kernel):
    got = lax.all_to_all(packed, "y", 0, 0, tiled=True)
    return call(kernel, packed.shape[1:], jnp.int16, got)


def pack_acts(chunks):
    rows = chunks[0].shape[0] * len(chunks) // NY
    return call(pack_kernel, (NY, BLOCKS * rows + SCALE_ROWS, LANES), jnp.int16, *chunks)


def pack_first(order, test, own, other, act_gram):
    base, rows = REGIONS[1]
    return pl.pallas_call(
        first_kernel,
        out_shape=jax.ShapeDtypeStruct((NY, base + BLOCKS * rows + SCALE_ROWS, LANES), jnp.int16),
        in_specs=[pl.BlockSpec(memory_space=pltpu.SMEM)] + [VMEM] * 4,
        out_specs=VMEM,
        scratch_shapes=[pltpu.VMEM((test.shape[0], 2 * own.shape[1]), jnp.float32)],
        compiler_params=pltpu.CompilerParams(vmem_limit_bytes=24 << 20),
    )(order, test, own, other, act_gram)


def on_device(
    train_act, train_grad, train_seg, train_mask, test_act, test_grad, test_seg, test_mask
):
    x, y, z, c = (lax.axis_index(a) for a in ("x", "y", "z", "c"))
    wide = test_act.shape[1]
    both_z = jnp.concatenate(around(jnp.concatenate([test_act, test_grad], 1), "z"), 0)
    act_z, grad_z = both_z[:, :wide], both_z[:, wide:]
    other_grad, other_act = swap(train_grad.T, "c"), swap(train_act, "c")
    grads = lax.all_gather(grad_z, "x", axis=0, tiled=True)
    acts = around(act_z, "x")
    both = jnp.concatenate([train_act, other_act], 0)
    grams = [cross_rows(t, both) for t in acts]
    order = jnp.stack([(x - step) % NX for step in (0,) + ORDER])
    first = sum_over_y(
        pack_first(order, grads, train_grad.T, other_grad, grams[0]), unpack_first_kernel
    )
    rest = sum_over_y(pack_acts(grams[1:]), unpack_kernel)
    local = test_act.shape[0]
    per = NZ * local // NY
    from_z, from_row = (z - step_of(y * per // local)) % NZ, y * per % local

    def here(values):
        cut = lax.dynamic_slice(
            values.reshape(NX, NZ, NC, local), (0, from_z, c, from_row), (NX, 1, 1, per)
        ).reshape(NX, per)
        return jnp.concatenate(
            [
                jnp.sum(jnp.where(jnp.arange(NX)[:, None] == (x - s) % NX, cut, 0), 0, keepdims=True)
                for s in (0,) + ORDER
            ],
            1,
        )

    test_onehot = (
        (here(test_seg) == jnp.arange(TEST_SEQS, dtype=jnp.int32)[:, None]) & (here(test_mask) != 0)
    ).astype(jnp.float32)
    rows = call(
        joint_kernel,
        (TEST_SEQS, BLOCKS * LANES),
        jnp.float32,
        test_onehot,
        first,
        swap(first, "h"),
        rest,
        swap(rest, "h"),
    )
    n = train_act.shape[0]
    masked = jnp.where(train_mask != 0, train_seg, -1)

    def by_sequence(of, values):
        train_onehot = (of == jnp.arange(SEQ_PACK, dtype=jnp.int32)[:, None]).astype(jnp.float32)
        scores = lax.dot_general(
            train_onehot, values, (((1,), (1,)), ((), ())), precision=lax.Precision.HIGHEST
        )
        return jnp.pad(scores, ((0, 4), (0, LANES - TEST_SEQS)))

    mine, theirs = by_sequence(masked, rows[:, :n]), by_sequence(swap(masked, "c"), rows[:, n:])
    to = jnp.arange(NY * NC)[:, None, None] % NC
    spread = jnp.where(to == c, mine[None], theirs[None])
    got = lax.all_to_all(spread, ("y", "c"), 0, 0, tiled=True)
    scores = jnp.sum(got, 0)[:SEQ_PACK, :TEST_SEQS]
    return scores * (1.0 / (SEG_LEN * math.sqrt(FF * D)))


def solution(mesh):
    fine = Mesh(mesh.devices.reshape(NX, NZ, NC, NY, NH), ("x", "z", "c", "y", "h"))
    return jax.shard_map(
        on_device,
        mesh=fine,
        in_specs=(P(DP, FFN), P(DP, FFN), P(DP, None), P(DP, None), P(DP, FFN), P(DP, FFN), P(), P()),
        out_specs=P(DP, None),
        check_vma=False,
    )
```

time: 129 us -> 137 us (1.062)
  waiting for transfers between devices: 21.7 us -> 40.3 us
  blocking collectives: 38.5 us -> 20.9 us
  matrix products: 2.9 us -> 6.68 us
  starting transfers between devices: 54 us -> 56.4 us
    all_to_all x2, waiting for transfers between devices: 11.2 us -> 24.8 us  [sum_over_y(): got = lax.all_to_all(packed, 'y', 0, 0, tiled=True)]
    all_gather x1 -> x0, blocking collectives: 12.2 us -> none  [on_device(): lax.all_gather(jnp.concatenate([test_act, test_grad], 1), 'z', axis=0, ti...]
    ppermute x3 -> x6, starting transfers between devices: 9.77 us -> 17.7 us  [around(): lax.ppermute(value, axis, [(i, (i + step) % 4) for i in range(4)])]
    all_to_all x1, blocking collectives: 15.9 us -> 11.3 us  [on_device(): got = lax.all_to_all(spread, ('y', 'c'), 0, 0, tiled=True)]
    ppermute x3 -> x6, waiting for transfers between devices: 8.11 us -> 12.6 us  [around(): lax.ppermute(value, axis, [(i, (i + step) % 4) for i in range(4)])]
    ppermute x5, starting transfers between devices: 33.9 us -> 29.6 us  [swap(): return lax.ppermute(value, axis, [(0, 1), (1, 0)])]
    dot_general x4, matrix products: 2.64 us -> 6.42 us  [cross_rows(): lax.dot_general(left, right, (((1,), (1,)), ((), ())), preferred_element_...]
    unnamed x13, local copies, waits for them, and re-layouts: 1.24 us -> 2.84 us
  transfers between devices with their start and end apart: 10 -> 13, of which waited for: 4 -> 7; matrix products, arithmetic and copies ran while one was open for 5% -> 9% of each run, Pallas kernels for 4% -> 2%
where the time goes in v7:
time: 137 us
  starting transfers between devices  56.4 us (41%)
  waiting for transfers between devices  40.3 us (29%)
  blocking collectives  20.9 us (15%)
  matrix products  6.68 us (5%)
  Pallas kernels  5.47 us (4%)
  local copies, waits for them, and re-layouts  4.48 us (3%)
  other arithmetic  2.17 us (2%)
    ppermute x5, starting transfers between devices, swap(): return lax.ppermute(value, axis, [(0, 1), (1, 0)])  29.6 us
    all_to_all x2, waiting for transfers between devices, sum_over_y(): got = lax.all_to_all(packed, 'y', 0, 0, tiled=True)  24.8 us
    ppermute x6, starting transfers between devices, around(): lax.ppermute(value, axis, [(i, (i + step) % 4) for i in range(4)])  17.7 us
    ppermute x6, waiting for transfers between devices, around(): lax.ppermute(value, axis, [(i, (i + step) % 4) for i in range(4)])  12.6 us
    all_to_all x1, blocking collectives, on_device(): got = lax.all_to_all(spread, ('y', 'c'), 0, 0, tiled=True)  11.3 us
    all_gather x1, blocking collectives, on_device(): grads = lax.all_gather(grad_z, 'x', axis=0, tiled=True)  9.63 us
    all_to_all x2, starting transfers between devices, sum_over_y(): got = lax.all_to_all(packed, 'y', 0, 0, tiled=True)  9.08 us
    dot_general x4, matrix products, cross_rows(): lax.dot_general(left, right, (((1,), (1,)), ((), ())), preferred_element_...  6.42 us
  transfers between devices with their start and end apart: 13, of which 7 were waited for; matrix products, arithmetic and copies ran while one was open for 9% of the time, Pallas kernels for 2%

profile of v7, /device:TPU:1, one launch (start us, length us, event | category | flops | bytes accessed | tf_op | source)
XLA Modules:
  0.0 136.7 jit_solution(15991265565796474533)
XLA Ops:
  0.0 8.8 %collective-permute-start.4 = (bf16[512,1600]{0,1:T(8,128)(2,1)}, bf16[512,1600]{0,1:T(8,128)(2,1)S(1)}, u32[]{:S(2)}, u32[]{:S(2)}) collective-permute-start(bf16[512,1600]{0,1:T(8,128)(2,1)} %param.8), channel_id=1, source_target_pairs={{0,16},{16,0},{1,17},{17,1},{2,18},{18,2},{3,19},{19,3},{4,20},{20... | collective-permute-start | bytes 4915208 | tf_op jit(solution)/shard_map/ppermute | solution.py:32
  11.7 5.2 %collective-permute-start.1 = (bf16[32,1920]{1,0:T(8,128)(2,1)S(1)}, bf16[32,1920]{1,0:T(8,128)(2,1)S(1)}, u32[]{:S(2)}, u32[]{:S(2)}) collective-permute-start(bf16[32,1920]{1,0:T(8,128)(2,1)S(1)} %pad_maximum_fusion.3), channel_id=1, source_target_pairs={{0,96},{32,0},{64,32},{96,64},{1,97},{33,1},{65,33},{97,65},{2,98}... | collective-permute-start | bytes 368648 | tf_op jit(solution)/shard_map/ppermute | solution.py:41
  16.9 1.9 %collective-permute-start.2 = (bf16[32,1920]{1,0:T(8,128)(2,1)S(1)}, bf16[32,1920]{1,0:T(8,128)(2,1)S(1)}, u32[]{:S(2)}, u32[]{:S(2)}) collective-permute-start(bf16[32,1920]{1,0:T(8,128)(2,1)S(1)} %pad_maximum_fusion.3), channel_id=1, source_target_pairs={{0,64},{32,96},{64,0},{96,32},{1,65},{33,97},{65,1},{97,33},{2,66}... | collective-permute-start | bytes 368648 | tf_op jit(solution)/shard_map/ppermute | solution.py:41
  18.8 2.5 %collective-permute-start.3 = (bf16[320,512]{1,0:T(8,128)(2,1)}, bf16[320,512]{1,0:T(8,128)(2,1)S(1)}, u32[]{:S(2)}, u32[]{:S(2)}) collective-permute-start(bf16[320,512]{1,0:T(8,128)(2,1)} %bitcast.23), channel_id=1, source_target_pairs={{0,16},{16,0},{1,17},{17,1},{2,18},{18,2},{3,19},{19,3},{4,20},{20... | collective-permute-start | bytes 983048 | tf_op jit(solution)/shard_map/ppermute | solution.py:32
  21.3 2.8 %constant_dynamic-update-slice_fusion.1 = bf16[1024,1600]{0,1:T(8,128)(2,1)} fusion(bf16[512,1600]{0,1:T(8,128)(2,1)} %param.8), kind=kLoop, calls=%fused_computation.14 | loop fusion | bytes 3276800
  24.2 2.5 %collective-permute-done.2 = bf16[32,1920]{1,0:T(8,128)(2,1)S(1)} collective-permute-done((bf16[32,1920]{1,0:T(8,128)(2,1)S(1)}, bf16[32,1920]{1,0:T(8,128)(2,1)S(1)}, u32[]{:S(2)}, u32[]{:S(2)}) %collective-permute-start.2) | collective-permute-done | bytes 122912 | tf_op jit(solution)/shard_map/ppermute | solution.py:41
  26.8 9.6 %all_gather.3.test = bf16[512,320]{1,0:T(8,128)(2,1)S(1)} all-gather(bf16[128,320]{1,0:T(8,128)(2,1)S(1)} %pad_maximum_fusion.4), channel_id=1, replica_groups=mesh['x'=4,'z'=4,'c'=2,'y'=8,'h'=2] {'x'}, dimensions={0}, use_global_device_ids=true | all-gather | bytes 409600 | tf_op jit(solution)/shard_map/all_gather | solution.py:215
  37.8 2.6 %fusion.9.act_gram = f32[128,1024]{1,0:T(8,128)S(1)} fusion(bf16[128,1600]{1,0:T(8,128)(2,1)S(1)} %pad_maximum_fusion, bf16[1024,1600]{0,1:T(8,128)(2,1)} %constant_dynamic-update-slice_fusion), kind=kOutput, calls=%fused_computation.40 | convolution fusion | flops 419430400 | bytes 4210688 | tf_op jit(solution)/shard_map/dot_general | solution.py:26
  40.4 3.1 %shard_map.82 = s16[8,672,128]{2,1,0:T(8,128)(2,1)} custom-call(s32[4]{0:T(128)S(1)} %pad_add_fusion.order, bf16[512,320]{1,0:T(8,128)(2,1)S(1)} %all_gather.3.test, bf16[320,512]{1,0:T(8,128)(2,1)S(1)} %bitcast.24, bf16[320,512]{1,0:T(8,128)(2,1)S(1)} %collective-permute-done.3.other, f32[128,1024]{1,0:T(8,128)S(1)} %fusion.9.act_gram), custom_call_target="tpu_custom_call" | custom-call | tf_op jit(solution)/shard_map/pallas_call | solution.py:197
  43.6 5.5 %all-to-all-start = ((s16[8,672,128]{2,1,0:T(8,128)(2,1)}), s16[8,672,128]{2,1,0:T(8,128)(2,1)S(1)}, u32[]{:S(2)}, u32[]{:S(2)}) async-start(s16[8,672,128]{2,1,0:T(8,128)(2,1)} %shard_map.82), calls=%async_computation | async-start | bytes 2752512 | tf_op jit(solution)/shard_map/all_to_all | solution.py:186
  49.1 2.2 %collective-permute-start.6 = (bf16[128,1600]{1,0:T(8,128)(2,1)S(1)}, bf16[128,1600]{1,0:T(8,128)(2,1)S(1)}, u32[]{:S(2)}, u32[]{:S(2)}) collective-permute-start(bf16[128,1600]{1,0:T(8,128)(2,1)S(1)} %pad_maximum_fusion), channel_id=1, source_target_pairs={{0,128},{128,256},{256,384},{384,0},{1,129},{129,257},{257,385},{3... | collective-permute-start | bytes 1228808 | tf_op jit(solution)/shard_map/ppermute | solution.py:41
  51.3 4.6 %collective-permute-start.7 = (bf16[128,1600]{1,0:T(8,128)(2,1)S(1)}, bf16[128,1600]{1,0:T(8,128)(2,1)S(1)}, u32[]{:S(2)}, u32[]{:S(2)}) collective-permute-start(bf16[128,1600]{1,0:T(8,128)(2,1)S(1)} %pad_maximum_fusion), channel_id=1, source_target_pairs={{0,384},{128,0},{256,128},{384,256},{1,385},{129,1},{257,129},{385... | collective-permute-start | bytes 1228808 | tf_op jit(solution)/shard_map/ppermute | solution.py:41
  55.9 1.9 %collective-permute-start.8 = (bf16[128,1600]{1,0:T(8,128)(2,1)S(1)}, bf16[128,1600]{1,0:T(8,128)(2,1)S(1)}, u32[]{:S(2)}, u32[]{:S(2)}) collective-permute-start(bf16[128,1600]{1,0:T(8,128)(2,1)S(1)} %pad_maximum_fusion), channel_id=1, source_target_pairs={{0,256},{128,384},{256,0},{384,128},{1,257},{129,385},{257,1},{385... | collective-permute-start | bytes 1228808 | tf_op jit(solution)/shard_map/ppermute | solution.py:41
  57.8 3.1 %collective-permute-done.6 = bf16[128,1600]{1,0:T(8,128)(2,1)S(1)} collective-permute-done((bf16[128,1600]{1,0:T(8,128)(2,1)S(1)}, bf16[128,1600]{1,0:T(8,128)(2,1)S(1)}, u32[]{:S(2)}, u32[]{:S(2)}) %collective-permute-start.6) | collective-permute-done | bytes 409632 | tf_op jit(solution)/shard_map/ppermute | solution.py:41
  60.9 2.6 %fusion.10.refs_0_ = f32[128,1024]{1,0:T(8,128)S(1)} fusion(bf16[128,1600]{1,0:T(8,128)(2,1)S(1)} %collective-permute-done.6, bf16[1024,1600]{0,1:T(8,128)(2,1)} %constant_dynamic-update-slice_fusion), kind=kOutput, calls=%fused_computation.41 | convolution fusion | flops 419430400 | bytes 4210688 | tf_op jit(solution)/shard_map/dot_general | solution.py:26
  65.6 5.6 %collective-permute-done.8 = bf16[128,1600]{1,0:T(8,128)(2,1)S(1)} collective-permute-done((bf16[128,1600]{1,0:T(8,128)(2,1)S(1)}, bf16[128,1600]{1,0:T(8,128)(2,1)S(1)}, u32[]{:S(2)}, u32[]{:S(2)}) %collective-permute-start.8) | collective-permute-done | bytes 409632 | tf_op jit(solution)/shard_map/ppermute | solution.py:41
  73.1 12.2 %all-to-all-done.got = s16[8,672,128]{2,1,0:T(8,128)(2,1)S(1)} async-done(((s16[8,672,128]{2,1,0:T(8,128)(2,1)}), s16[8,672,128]{2,1,0:T(8,128)(2,1)S(1)}, u32[]{:S(2)}, u32[]{:S(2)}) %all-to-all-start) | async-done | bytes 1376288 | tf_op jit(solution)/shard_map/all_to_all | solution.py:186
  85.3 3.5 %all-to-all-start.1 = ((s16[8,400,128]{2,1,0:T(8,128)(2,1)}), s16[8,400,128]{2,1,0:T(8,128)(2,1)S(1)}, u32[]{:S(2)}, u32[]{:S(2)}) async-start(s16[8,400,128]{2,1,0:T(8,128)(2,1)} %shard_map.84), calls=%async_computation.1 | async-start | bytes 1638400 | tf_op jit(solution)/shard_map/all_to_all | solution.py:186
  88.9 2.4 %collective-permute-start.10 = (s32[1,512]{1,0:T(1,128)S(1)}, s32[1,512]{1,0:T(1,128)S(1)}, u32[]{:S(2)}, u32[]{:S(2)}) collective-permute-start(s32[1,512]{1,0:T(1,128)S(1)} %compare_select_fusion), channel_id=1, source_target_pairs={{0,16},{16,0},{1,17},{17,1},{2,18},{18,2},{3,19},{19,3},{4,20},{20... | collective-permute-start | bytes 6152 | tf_op jit(solution)/shard_map/ppermute | solution.py:32
  92.4 8.0 %collective-permute-start.5 = (s16[672,128]{1,0:T(8,128)(2,1)S(1)}, s16[672,128]{1,0:T(8,128)(2,1)S(1)}, u32[]{:S(2)}, u32[]{:S(2)}) collective-permute-start(s16[672,128]{1,0:T(8,128)(2,1)S(1)} %shard_map.83.first_own), channel_id=1, source_target_pairs={{0,1},{1,0},{2,3},{3,2},{4,5},{5,4},{6,7},{7,6},{8,9},{9,8},{10,11... | collective-permute-start | bytes 516104 | tf_op jit(solution)/shard_map/ppermute | solution.py:32
  100.5 12.6 %all-to-all-done.1.got = s16[8,400,128]{2,1,0:T(8,128)(2,1)S(1)} async-done(((s16[8,400,128]{2,1,0:T(8,128)(2,1)}), s16[8,400,128]{2,1,0:T(8,128)(2,1)S(1)}, u32[]{:S(2)}, u32[]{:S(2)}) %all-to-all-start.1) | async-done | bytes 819232 | tf_op jit(solution)/shard_map/all_to_all | solution.py:186
  113.4 8.0 %collective-permute-start.9 = (s16[400,128]{1,0:T(8,128)(2,1)S(1)}, s16[400,128]{1,0:T(8,128)(2,1)S(1)}, u32[]{:S(2)}, u32[]{:S(2)}) collective-permute-start(s16[400,128]{1,0:T(8,128)(2,1)S(1)} %shard_map.85.rest_own), channel_id=1, source_target_pairs={{0,1},{1,0},{2,3},{3,2},{4,5},{5,4},{6,7},{7,6},{8,9},{9,8},{10,11... | collective-permute-start | bytes 307208 | tf_op jit(solution)/shard_map/ppermute | solution.py:32
  121.3 2.8 %collective-permute-done.9.rest_other = s16[400,128]{1,0:T(8,128)(2,1)S(1)} collective-permute-done((s16[400,128]{1,0:T(8,128)(2,1)S(1)}, s16[400,128]{1,0:T(8,128)(2,1)S(1)}, u32[]{:S(2)}, u32[]{:S(2)}) %collective-permute-start.9) | collective-permute-done | bytes 102432 | tf_op jit(solution)/shard_map/ppermute | solution.py:32
  124.9 11.3 %all_to_all.15 = f32[16,8,128]{2,1,0:T(8,128)S(1)} all-to-all(f32[16,8,128]{2,1,0:T(8,128)S(1)} %broadcast_select_fusion), channel_id=1, replica_groups=mesh['x'=4,'z'=4,'c'=2,'y'=8,'h'=2] {'y','c'}, dimensions={0} | all-to-all | bytes 131072 | tf_op jit(solution)/shard_map/all_to_all | solution.py:266
  (49 shorter events, 11.1 us)
Async XLA Ops:
  0.0 36.4 %collective-permute-start.4 = (bf16[512,1600]{0,1:T(8,128)(2,1)}, bf16[512,1600]{0,1:T(8,128)(2,1)S(1)}, u32[]{:S(2)}, u32[]{:S(2)}) collective-permute-start(bf16[512,1600]{0,1:T(8,128)(2,1)} %param.8), channel_id=1, source_target_pairs={{0,16},{16,0},{1,17},{17,1},{2,18},{18,2},{3,19},{19,3},{4,20},{20... | collective-permute-start | bytes 4915208 | tf_op jit(solution)/shard_map/ppermute | solution.py:32
  9.8 14.4 %collective-permute-start = (bf16[32,1920]{1,0:T(8,128)(2,1)S(1)}, bf16[32,1920]{1,0:T(8,128)(2,1)S(1)}, u32[]{:S(2)}, u32[]{:S(2)}) collective-permute-start(bf16[32,1920]{1,0:T(8,128)(2,1)S(1)} %pad_maximum_fusion.3), channel_id=1, source_target_pairs={{0,32},{32,64},{64,96},{96,0},{1,33},{33,65},{65,97},{97,1},{2,34}... | collective-permute-start | bytes 368648 | tf_op jit(solution)/shard_map/ppermute | solution.py:41
  11.7 12.5 %collective-permute-start.1 = (bf16[32,1920]{1,0:T(8,128)(2,1)S(1)}, bf16[32,1920]{1,0:T(8,128)(2,1)S(1)}, u32[]{:S(2)}, u32[]{:S(2)}) collective-permute-start(bf16[32,1920]{1,0:T(8,128)(2,1)S(1)} %pad_maximum_fusion.3), channel_id=1, source_target_pairs={{0,96},{32,0},{64,32},{96,64},{1,97},{33,1},{65,33},{97,65},{2,98}... | collective-permute-start | bytes 368648 | tf_op jit(solution)/shard_map/ppermute | solution.py:41
  16.9 9.8 %collective-permute-start.2 = (bf16[32,1920]{1,0:T(8,128)(2,1)S(1)}, bf16[32,1920]{1,0:T(8,128)(2,1)S(1)}, u32[]{:S(2)}, u32[]{:S(2)}) collective-permute-start(bf16[32,1920]{1,0:T(8,128)(2,1)S(1)} %pad_maximum_fusion.3), channel_id=1, source_target_pairs={{0,64},{32,96},{64,0},{96,32},{1,65},{33,97},{65,1},{97,33},{2,66}... | collective-permute-start | bytes 368648 | tf_op jit(solution)/shard_map/ppermute | solution.py:41
  18.8 21.6 %collective-permute-start.3 = (bf16[320,512]{1,0:T(8,128)(2,1)}, bf16[320,512]{1,0:T(8,128)(2,1)S(1)}, u32[]{:S(2)}, u32[]{:S(2)}) collective-permute-start(bf16[320,512]{1,0:T(8,128)(2,1)} %bitcast.23), channel_id=1, source_target_pairs={{0,16},{16,0},{1,17},{17,1},{2,18},{18,2},{3,19},{19,3},{4,20},{20... | collective-permute-start | bytes 983048 | tf_op jit(solution)/shard_map/ppermute | solution.py:32
  36.4 4.0 %copy-start = (bf16[512,320]{0,1:T(8,128)(2,1)S(1)}, bf16[512,320]{0,1:T(8,128)(2,1)}, u32[]{:S(2)}) copy-start(bf16[512,320]{0,1:T(8,128)(2,1)} %param.9) | copy-start | bytes 983044
  43.6 41.7 %all-to-all-start = ((s16[8,672,128]{2,1,0:T(8,128)(2,1)}), s16[8,672,128]{2,1,0:T(8,128)(2,1)S(1)}, u32[]{:S(2)}, u32[]{:S(2)}) async-start(s16[8,672,128]{2,1,0:T(8,128)(2,1)} %shard_map.82), calls=%async_computation | async-start | bytes 2752512 | tf_op jit(solution)/shard_map/all_to_all | solution.py:186
  49.1 15.9 %copy-start.1 = (bf16[1024,1600]{0,1:T(8,128)(2,1)S(1)}, bf16[1024,1600]{0,1:T(8,128)(2,1)}, u32[]{:S(2)}) copy-start(bf16[1024,1600]{0,1:T(8,128)(2,1)} %constant_dynamic-update-slice_fusion) | copy-start | bytes 9830404
  49.1 11.8 %collective-permute-start.6 = (bf16[128,1600]{1,0:T(8,128)(2,1)S(1)}, bf16[128,1600]{1,0:T(8,128)(2,1)S(1)}, u32[]{:S(2)}, u32[]{:S(2)}) collective-permute-start(bf16[128,1600]{1,0:T(8,128)(2,1)S(1)} %pad_maximum_fusion), channel_id=1, source_target_pairs={{0,128},{128,256},{256,384},{384,0},{1,129},{129,257},{257,385},{3... | collective-permute-start | bytes 1228808 | tf_op jit(solution)/shard_map/ppermute | solution.py:41
  51.3 13.7 %collective-permute-start.7 = (bf16[128,1600]{1,0:T(8,128)(2,1)S(1)}, bf16[128,1600]{1,0:T(8,128)(2,1)S(1)}, u32[]{:S(2)}, u32[]{:S(2)}) collective-permute-start(bf16[128,1600]{1,0:T(8,128)(2,1)S(1)} %pad_maximum_fusion), channel_id=1, source_target_pairs={{0,384},{128,0},{256,128},{384,256},{1,385},{129,1},{257,129},{385... | collective-permute-start | bytes 1228808 | tf_op jit(solution)/shard_map/ppermute | solution.py:41
  55.9 15.3 %collective-permute-start.8 = (bf16[128,1600]{1,0:T(8,128)(2,1)S(1)}, bf16[128,1600]{1,0:T(8,128)(2,1)S(1)}, u32[]{:S(2)}, u32[]{:S(2)}) collective-permute-start(bf16[128,1600]{1,0:T(8,128)(2,1)S(1)} %pad_maximum_fusion), channel_id=1, source_target_pairs={{0,256},{128,384},{256,0},{384,128},{1,257},{129,385},{257,1},{385... | collective-permute-start | bytes 1228808 | tf_op jit(solution)/shard_map/ppermute | solution.py:41
  65.6 23.2 %copy-start.4 = (s32[1,512]{1,0:T(1,128)S(1)}, s32[1,512]{1,0:T(1,128)}, u32[]{:S(2)}) copy-start(s32[1,512]{1,0:T(1,128)} %param.10) | copy-start | bytes 6148
  65.6 23.2 %copy-start.5 = (s32[1,512]{1,0:T(1,128)S(1)}, s32[1,512]{1,0:T(1,128)}, u32[]{:S(2)}) copy-start(s32[1,512]{1,0:T(1,128)} %param.11) | copy-start | bytes 6148
  65.6 25.7 %copy-start.2 = (s32[1024]{0:T(1024)S(1)}, s32[1024]{0:T(1024)}, u32[]{:S(2)}) copy-start(s32[1024]{0:T(1024)} %param.14) | copy-start | bytes 12292
  65.6 25.8 %copy-start.3 = (s32[1024]{0:T(1024)S(1)}, s32[1024]{0:T(1024)}, u32[]{:S(2)}) copy-start(s32[1024]{0:T(1024)} %param.15) | copy-start | bytes 12292
  85.3 27.8 %all-to-all-start.1 = ((s16[8,400,128]{2,1,0:T(8,128)(2,1)}), s16[8,400,128]{2,1,0:T(8,128)(2,1)S(1)}, u32[]{:S(2)}, u32[]{:S(2)}) async-start(s16[8,400,128]{2,1,0:T(8,128)(2,1)} %shard_map.84), calls=%async_computation.1 | async-start | bytes 1638400 | tf_op jit(solution)/shard_map/all_to_all | solution.py:186
  88.9 35.6 %collective-permute-start.10 = (s32[1,512]{1,0:T(1,128)S(1)}, s32[1,512]{1,0:T(1,128)S(1)}, u32[]{:S(2)}, u32[]{:S(2)}) collective-permute-start(s32[1,512]{1,0:T(1,128)S(1)} %compare_select_fusion), channel_id=1, source_target_pairs={{0,16},{16,0},{1,17},{17,1},{2,18},{18,2},{3,19},{19,3},{4,20},{20... | collective-permute-start | bytes 6152 | tf_op jit(solution)/shard_map/ppermute | solution.py:32
  92.4 31.7 %collective-permute-start.5 = (s16[672,128]{1,0:T(8,128)(2,1)S(1)}, s16[672,128]{1,0:T(8,128)(2,1)S(1)}, u32[]{:S(2)}, u32[]{:S(2)}) collective-permute-start(s16[672,128]{1,0:T(8,128)(2,1)S(1)} %shard_map.83.first_own), channel_id=1, source_target_pairs={{0,1},{1,0},{2,3},{3,2},{4,5},{5,4},{6,7},{7,6},{8,9},{9,8},{10,11... | collective-permute-start | bytes 516104 | tf_op jit(solution)/shard_map/ppermute | solution.py:32
  113.4 10.8 %collective-permute-start.9 = (s16[400,128]{1,0:T(8,128)(2,1)S(1)}, s16[400,128]{1,0:T(8,128)(2,1)S(1)}, u32[]{:S(2)}, u32[]{:S(2)}) collective-permute-start(s16[400,128]{1,0:T(8,128)(2,1)S(1)} %shard_map.85.rest_own), channel_id=1, source_target_pairs={{0,1},{1,0},{2,3},{3,2},{4,5},{5,4},{6,7},{7,6},{8,9},{9,8},{10,11... | collective-permute-start | bytes 307208 | tf_op jit(solution)/shard_map/ppermute | solution.py:32

commit v8 on v6

--- a/solution.py
+++ b/solution.py
@@ -204,7 +204,10 @@
     test_onehot = (
         (seg == jnp.arange(TEST_SEQS, dtype=jnp.int32)[:, None]) & (mask != 0)
     ).astype(jnp.float32)
-    grad_other, act_other = swap(grad_y, "h"), swap(act_y, "h")
+    grad_pair = lax.all_gather(grad_y, "h")
+    grad_y, grad_other = grad_pair[0], grad_pair[1]
+    act_pair = lax.all_gather(act_y, "h")
+    act_y, act_other = act_pair[0], act_pair[1]
     rows = call(
         joint_kernel,
         (TEST_SEQS, BLOCKS * LANES),

time: 129 us -> 128 us (level)
  the two profiles are of different devices: /device:TPU:1 before, /device:TPU:6 now
where the time goes in v8:
time: 128 us; the launch traced here: 125 us
  blocking collectives  63.7 us (50%)
  starting transfers between devices  27.9 us (22%)
  waiting for transfers between devices  19.9 us (16%)
  Pallas kernels  5.35 us (4%)
  local copies, waits for them, and re-layouts  3.45 us (3%)
  matrix products  2.89 us (2%)
  other arithmetic  1.93 us (2%)
    all_gather x1, blocking collectives, on_device(): lax.all_gather(jnp.concatenate([test_act, test_grad], 1), 'z', axis=0, ti...  18 us
    all_gather x1, blocking collectives, on_device(): grads = lax.all_gather(grad_z, 'x', axis=0, tiled=True)  13.4 us
    all_to_all x2, starting transfers between devices, sum_over_y(): got = lax.all_to_all(packed, 'y', 0, 0, tiled=True)  12.4 us
    all_gather x1, blocking collectives, on_device(): grad_pair = lax.all_gather(grad_y, 'h')  11.3 us
    all_to_all x1, blocking collectives, on_device(): got = lax.all_to_all(spread, ('y', 'c'), 0, 0, tiled=True)  11 us
    all_to_all x2, waiting for transfers between devices, sum_over_y(): got = lax.all_to_all(packed, 'y', 0, 0, tiled=True)  10.1 us
    all_gather x1, blocking collectives, on_device(): act_pair = lax.all_gather(act_y, 'h')  9.98 us
    ppermute x3, waiting for transfers between devices, over_x(): lax.ppermute(value, 'x', [(i, (i + step) % NX) for i in range(NX)])  9.84 us
  transfers between devices with their start and end apart: 8, of which 4 were waited for; matrix products, arithmetic and copies ran while one was open for 5% of the time, Pallas kernels for 4%

profile of v8, /device:TPU:6, one launch (start us, length us, event | category | flops | bytes accessed | tf_op | source)
XLA Modules:
  0.0 125.4 jit_solution(1608263009908005286)
XLA Ops:
  0.0 1.9 %collective-permute-start = (bf16[512,1600]{0,1:T(8,128)(2,1)}, bf16[512,1600]{0,1:T(8,128)(2,1)}, u32[]{:S(2)}, u32[]{:S(2)}) collective-permute-start(bf16[512,1600]{0,1:T(8,128)(2,1)} %param.8), channel_id=1, source_target_pairs={{0,16},{16,0},{1,17},{17,1},{2,18},{18,2},{3,19},{19,3},{4,20},{20... | collective-permute-start | bytes 4915208 | tf_op jit(solution)/shard_map/ppermute | solution.py:32
  1.9 2.4 %collective-permute-start.4 = (bf16[320,512]{1,0:T(8,128)(2,1)}, bf16[320,512]{1,0:T(8,128)(2,1)S(1)}, u32[]{:S(2)}, u32[]{:S(2)}) collective-permute-start(bf16[320,512]{1,0:T(8,128)(2,1)} %bitcast.14), channel_id=1, source_target_pairs={{0,16},{16,0},{1,17},{17,1},{2,18},{18,2},{3,19},{19,3},{4,20},{20... | collective-permute-start | bytes 983048 | tf_op jit(solution)/shard_map/ppermute | solution.py:32
  4.3 1.1 pad_maximum_fusion
  5.5 18.0 %all_gather.18 = bf16[128,1920]{1,0:T(8,128)(2,1)S(1)} all-gather(bf16[32,1920]{1,0:T(8,128)(2,1)S(1)} %pad_maximum_fusion), channel_id=1, replica_groups=mesh['x'=4,'z'=4,'c'=2,'y'=8,'h'=2] {'z'}, dimensions={0}, use_global_device_ids=true | all-gather | bytes 614400 | tf_op jit(solution)/shard_map/all_gather | solution.py:183
  23.7 13.4 %all_gather.21.test = bf16[512,320]{1,0:T(8,128)(2,1)S(1)} all-gather(bf16[128,320]{1,0:T(8,128)(2,1)S(1)} %slice.43), channel_id=1, replica_groups=mesh['x'=4,'z'=4,'c'=2,'y'=8,'h'=2] {'x'}, dimensions={0}, use_global_device_ids=true | all-gather | bytes 409600 | tf_op jit(solution)/shard_map/all_gather | solution.py:186
  37.1 1.0 copy-done
  38.1 2.8 %shard_map.84 = s16[8,528,128]{2,1,0:T(8,128)(2,1)} custom-call(s32[4]{0:T(128)S(1)} %pad_add_fusion.order, bf16[512,320]{1,0:T(8,128)(2,1)S(1)} %all_gather.21.test, bf16[320,512]{1,0:T(8,128)(2,1)S(1)} %bitcast.15, bf16[320,512]{1,0:T(8,128)(2,1)S(1)} %collective-permute-done.4.other), custom_call_target="tpu_custom_call" | custom-call | tf_op jit(solution)/shard_map/pallas_call | solution.py:168
  40.8 6.2 %all-to-all-start.1 = ((s16[8,528,128]{2,1,0:T(8,128)(2,1)}), s16[8,528,128]{2,1,0:T(8,128)(2,1)S(1)}, u32[]{:S(2)}, u32[]{:S(2)}) async-start(s16[8,528,128]{2,1,0:T(8,128)(2,1)} %shard_map.84), calls=%async_computation.1 | async-start | bytes 2162688 | tf_op jit(solution)/shard_map/all_to_all | solution.py:157
  47.1 3.2 %collective-permute-start.1 = (bf16[128,1600]{1,0:T(8,128)(2,1)S(1)}, bf16[128,1600]{1,0:T(8,128)(2,1)S(1)}, u32[]{:S(2)}, u32[]{:S(2)}) collective-permute-start(bf16[128,1600]{1,0:T(8,128)(2,1)S(1)} %slice.40), channel_id=1, source_target_pairs={{0,128},{128,256},{256,384},{384,0},{1,129},{129,257},{257,385},{3... | collective-permute-start | bytes 1228808 | tf_op jit(solution)/shard_map/ppermute | solution.py:37
  50.3 2.7 %collective-permute-start.2 = (bf16[128,1600]{1,0:T(8,128)(2,1)S(1)}, bf16[128,1600]{1,0:T(8,128)(2,1)S(1)}, u32[]{:S(2)}, u32[]{:S(2)}) collective-permute-start(bf16[128,1600]{1,0:T(8,128)(2,1)S(1)} %slice.40), channel_id=1, source_target_pairs={{0,384},{128,0},{256,128},{384,256},{1,385},{129,1},{257,129},{385... | collective-permute-start | bytes 1228808 | tf_op jit(solution)/shard_map/ppermute | solution.py:37
  52.9 3.4 %collective-permute-start.3 = (bf16[128,1600]{1,0:T(8,128)(2,1)S(1)}, bf16[128,1600]{1,0:T(8,128)(2,1)S(1)}, u32[]{:S(2)}, u32[]{:S(2)}) collective-permute-start(bf16[128,1600]{1,0:T(8,128)(2,1)S(1)} %slice.40), channel_id=1, source_target_pairs={{0,256},{128,384},{256,0},{384,128},{1,257},{129,385},{257,1},{385... | collective-permute-start | bytes 1228808 | tf_op jit(solution)/shard_map/ppermute | solution.py:37
  56.6 1.7 %constant_dynamic-update-slice_fusion = bf16[1024,1600]{0,1:T(8,128)(2,1)S(1)} fusion(bf16[1024,1600]{0,1:T(8,128)(2,1)S(1)} %constant_dynamic-update-slice_fusion.1, bf16[512,1600]{0,1:T(8,128)(2,1)} %collective-permute-done), kind=kLoop, calls=%fused_computation.9 | loop fusion | bytes 3276800 | tf_op jit(solution)/shard_map/concatenate | solution.py:190
  58.3 0.7 fusion.9.refs_0_
  59.0 2.0 %collective-permute-done.1 = bf16[128,1600]{1,0:T(8,128)(2,1)S(1)} collective-permute-done((bf16[128,1600]{1,0:T(8,128)(2,1)S(1)}, bf16[128,1600]{1,0:T(8,128)(2,1)S(1)}, u32[]{:S(2)}, u32[]{:S(2)}) %collective-permute-start.1) | collective-permute-done | bytes 409632 | tf_op jit(solution)/shard_map/ppermute | solution.py:37
  60.9 0.7 fusion.13.refs_1_
  61.6 7.9 %collective-permute-done.2 = bf16[128,1600]{1,0:T(8,128)(2,1)S(1)} collective-permute-done((bf16[128,1600]{1,0:T(8,128)(2,1)S(1)}, bf16[128,1600]{1,0:T(8,128)(2,1)S(1)}, u32[]{:S(2)}, u32[]{:S(2)}) %collective-permute-start.2) | collective-permute-done | bytes 409632 | tf_op jit(solution)/shard_map/ppermute | solution.py:37
  70.8 1.5 %shard_map.82 = s16[8,528,128]{2,1,0:T(8,128)(2,1)} custom-call(f32[128,1024]{1,0:T(8,128)S(1)} %fusion.9.refs_0_, f32[128,1024]{1,0:T(8,128)S(1)} %fusion.13.refs_1_, f32[128,1024]{1,0:T(8,128)S(1)} %fusion.14.refs_2_, f32[128,1024]{1,0:T(8,128)S(1)} %fusion.15.refs_3_), custom_call_target="tpu_custom_call" | custom-call | tf_op jit(solution)/shard_map/pallas_call | solution.py:147
  72.3 0.7 all-to-all-done.1.got
  73.1 6.2 %all-to-all-start = ((s16[8,528,128]{2,1,0:T(8,128)(2,1)}), s16[8,528,128]{2,1,0:T(8,128)(2,1)S(1)}, u32[]{:S(2)}, u32[]{:S(2)}) async-start(s16[8,528,128]{2,1,0:T(8,128)(2,1)} %shard_map.82), calls=%async_computation | async-start | bytes 2162688 | tf_op jit(solution)/shard_map/all_to_all | solution.py:157
  79.3 1.9 %collective-permute-start.5 = (s32[1,512]{1,0:T(1,128)S(1)}, s32[1,512]{1,0:T(1,128)S(1)}, u32[]{:S(2)}, u32[]{:S(2)}) collective-permute-start(s32[1,512]{1,0:T(1,128)S(1)} %compare_select_fusion), channel_id=1, source_target_pairs={{0,16},{16,0},{1,17},{17,1},{2,18},{18,2},{3,19},{19,3},{4,20},{20... | collective-permute-start | bytes 6152 | tf_op jit(solution)/shard_map/ppermute | solution.py:32
  82.1 11.3 %all-gather.1 = s16[1056,128]{1,0:T(8,128)(2,1)S(1)} all-gather(s16[528,128]{1,0:T(8,128)(2,1)S(1)} %shard_map.85), channel_id=3, replica_groups=mesh['x'=4,'z'=4,'c'=2,'y'=8,'h'=2] {'h'}, dimensions={0}, use_global_device_ids=true | all-gather | bytes 405504 | tf_op jit(solution)/shard_map/all_gather | solution.py:207
  93.4 9.3 %all-to-all-done.got = s16[8,528,128]{2,1,0:T(8,128)(2,1)S(1)} async-done(((s16[8,528,128]{2,1,0:T(8,128)(2,1)}), s16[8,528,128]{2,1,0:T(8,128)(2,1)S(1)}, u32[]{:S(2)}, u32[]{:S(2)}) %all-to-all-start) | async-done | bytes 1081376 | tf_op jit(solution)/shard_map/all_to_all | solution.py:157
  103.1 10.0 %all-gather = s16[1056,128]{1,0:T(8,128)(2,1)S(1)} all-gather(s16[528,128]{1,0:T(8,128)(2,1)S(1)} %shard_map.83), channel_id=2, replica_groups=mesh['x'=4,'z'=4,'c'=2,'y'=8,'h'=2] {'h'}, dimensions={0}, use_global_device_ids=true | all-gather | bytes 405504 | tf_op jit(solution)/shard_map/all_gather | solution.py:209
  113.9 11.0 %all_to_all.15 = f32[16,8,128]{2,1,0:T(8,128)S(1)} all-to-all(f32[16,8,128]{2,1,0:T(8,128)S(1)} %broadcast_select_fusion), channel_id=1, replica_groups=mesh['x'=4,'z'=4,'c'=2,'y'=8,'h'=2] {'y','c'}, dimensions={0} | all-to-all | bytes 131072 | tf_op jit(solution)/shard_map/all_to_all | solution.py:234
  (42 shorter events, 4.3 us)
Async XLA Ops:
  0.0 56.6 %collective-permute-start = (bf16[512,1600]{0,1:T(8,128)(2,1)}, bf16[512,1600]{0,1:T(8,128)(2,1)}, u32[]{:S(2)}, u32[]{:S(2)}) collective-permute-start(bf16[512,1600]{0,1:T(8,128)(2,1)} %param.8), channel_id=1, source_target_pairs={{0,16},{16,0},{1,17},{17,1},{2,18},{18,2},{3,19},{19,3},{4,20},{20... | collective-permute-start | bytes 4915208 | tf_op jit(solution)/shard_map/ppermute | solution.py:32
  1.9 35.2 %collective-permute-start.4 = (bf16[320,512]{1,0:T(8,128)(2,1)}, bf16[320,512]{1,0:T(8,128)(2,1)S(1)}, u32[]{:S(2)}, u32[]{:S(2)}) collective-permute-start(bf16[320,512]{1,0:T(8,128)(2,1)} %bitcast.14), channel_id=1, source_target_pairs={{0,16},{16,0},{1,17},{17,1},{2,18},{18,2},{3,19},{19,3},{4,20},{20... | collective-permute-start | bytes 983048 | tf_op jit(solution)/shard_map/ppermute | solution.py:32
  4.3 52.0 %copy-start.1 = (bf16[512,1600]{0,1:T(8,128)(2,1)S(1)}, bf16[512,1600]{0,1:T(8,128)(2,1)}, u32[]{:S(2)}) copy-start(bf16[512,1600]{0,1:T(8,128)(2,1)} %param.8) | copy-start | bytes 4915204
  37.1 1.0 copy-start
  40.8 32.2 %all-to-all-start.1 = ((s16[8,528,128]{2,1,0:T(8,128)(2,1)}), s16[8,528,128]{2,1,0:T(8,128)(2,1)S(1)}, u32[]{:S(2)}, u32[]{:S(2)}) async-start(s16[8,528,128]{2,1,0:T(8,128)(2,1)} %shard_map.84), calls=%async_computation.1 | async-start | bytes 2162688 | tf_op jit(solution)/shard_map/all_to_all | solution.py:157
  47.1 13.9 %collective-permute-start.1 = (bf16[128,1600]{1,0:T(8,128)(2,1)S(1)}, bf16[128,1600]{1,0:T(8,128)(2,1)S(1)}, u32[]{:S(2)}, u32[]{:S(2)}) collective-permute-start(bf16[128,1600]{1,0:T(8,128)(2,1)S(1)} %slice.40), channel_id=1, source_target_pairs={{0,128},{128,256},{256,384},{384,0},{1,129},{129,257},{257,385},{3... | collective-permute-start | bytes 1228808 | tf_op jit(solution)/shard_map/ppermute | solution.py:37
  50.3 19.2 %collective-permute-start.2 = (bf16[128,1600]{1,0:T(8,128)(2,1)S(1)}, bf16[128,1600]{1,0:T(8,128)(2,1)S(1)}, u32[]{:S(2)}, u32[]{:S(2)}) collective-permute-start(bf16[128,1600]{1,0:T(8,128)(2,1)S(1)} %slice.40), channel_id=1, source_target_pairs={{0,384},{128,0},{256,128},{384,256},{1,385},{129,1},{257,129},{385... | collective-permute-start | bytes 1228808 | tf_op jit(solution)/shard_map/ppermute | solution.py:37
  52.9 17.2 %collective-permute-start.3 = (bf16[128,1600]{1,0:T(8,128)(2,1)S(1)}, bf16[128,1600]{1,0:T(8,128)(2,1)S(1)}, u32[]{:S(2)}, u32[]{:S(2)}) collective-permute-start(bf16[128,1600]{1,0:T(8,128)(2,1)S(1)} %slice.40), channel_id=1, source_target_pairs={{0,256},{128,384},{256,0},{384,128},{1,257},{129,385},{257,1},{385... | collective-permute-start | bytes 1228808 | tf_op jit(solution)/shard_map/ppermute | solution.py:37
  70.8 8.5 %copy-start.4 = (s32[1,512]{1,0:T(1,128)S(1)}, s32[1,512]{1,0:T(1,128)}, u32[]{:S(2)}) copy-start(s32[1,512]{1,0:T(1,128)} %param.10) | copy-start | bytes 6148
  70.8 8.5 %copy-start.5 = (s32[1,512]{1,0:T(1,128)S(1)}, s32[1,512]{1,0:T(1,128)}, u32[]{:S(2)}) copy-start(s32[1,512]{1,0:T(1,128)} %param.11) | copy-start | bytes 6148
  70.8 10.4 %copy-start.2 = (s32[1024]{0:T(1024)S(1)}, s32[1024]{0:T(1024)}, u32[]{:S(2)}) copy-start(s32[1024]{0:T(1024)} %param.14) | copy-start | bytes 12292
  70.8 10.7 %copy-start.3 = (s32[1024]{0:T(1024)S(1)}, s32[1024]{0:T(1024)}, u32[]{:S(2)}) copy-start(s32[1024]{0:T(1024)} %param.15) | copy-start | bytes 12292
  73.1 29.7 %all-to-all-start = ((s16[8,528,128]{2,1,0:T(8,128)(2,1)}), s16[8,528,128]{2,1,0:T(8,128)(2,1)S(1)}, u32[]{:S(2)}, u32[]{:S(2)}) async-start(s16[8,528,128]{2,1,0:T(8,128)(2,1)} %shard_map.82), calls=%async_computation | async-start | bytes 2162688 | tf_op jit(solution)/shard_map/all_to_all | solution.py:157
  79.3 34.2 %collective-permute-start.5 = (s32[1,512]{1,0:T(1,128)S(1)}, s32[1,512]{1,0:T(1,128)S(1)}, u32[]{:S(2)}, u32[]{:S(2)}) collective-permute-start(s32[1,512]{1,0:T(1,128)S(1)} %compare_select_fusion), channel_id=1, source_target_pairs={{0,16},{16,0},{1,17},{17,1},{2,18},{18,2},{3,19},{19,3},{4,20},{20... | collective-permute-start | bytes 6152 | tf_op jit(solution)/shard_map/ppermute | solution.py:32

commit v9 on v6

--- a/solution.py
+++ b/solution.py
@@ -71,20 +71,6 @@
     return jnp.exp(tail.astype(jnp.float32) * (1.0 / STEPS)) * (1.0 / TOP)
 
 
-def pack_kernel(*refs):
-    chunks, out = refs[:-1], refs[-1]
-    rows = chunks[0].shape[0] * len(chunks) // NY
-    per = chunks[0].shape[0] // rows
-
-    def pieces(b):
-        cols = slice(b * LANES, (b + 1) * LANES)
-        return [
-            chunks[d // per][(d % per) * rows : (d % per + 1) * rows, cols] for d in range(NY)
-        ]
-
-    pack(Pieces(chunks[0].shape[1] // LANES, pieces), out, [(d,) for d in range(NY)])
-
-
 def grad_kernel(order, test, own, other, out, gram):
     n = own.shape[1]
     gram[:, :n] = jnp.dot(test[...], own[...], preferred_element_type=jnp.float32)
@@ -119,21 +105,34 @@
     pack(Pieces(blocks, pieces), out, [()])
 
 
-def joint_kernel(onehot, act_own, act_other, grad_own, grad_other, out):
-    blocks = BLOCKS
-    rows = (act_own.shape[0] - SCALE_ROWS) // blocks
-
-    def part(ref, factor, b):
-        return ref[b * rows : (b + 1) * rows, :].astype(jnp.float32) * factor[b : b + 1]
-
-    refs = (act_own, act_other, grad_own, grad_other)
-    f = [factors_of(r[blocks * rows :, :]) for r in refs]
-    for b in range(blocks):
-        a0, a1, g0, g1 = (part(r, k, b) for r, k in zip(refs, f))
-        joint = (a0 + a1) * (g0 + g1)
-        out[:, b * LANES : (b + 1) * LANES] = lax.dot_general(
+def both_kernel(pair, out):
+    rows = (pair.shape[1] - SCALE_ROWS) // BLOCKS
+    factors = [factors_of(pair[i, BLOCKS * rows :, :]) for i in range(NH)]
+
+    def pieces(b):
+        at = slice(b * rows, (b + 1) * rows)
+        low, high = (
+            pair[i, at, :].astype(jnp.float32) * factors[i][b : b + 1] for i in range(NH)
+        )
+        return [low + high]
+
+    pack(Pieces(BLOCKS, pieces), out, [()])
+
+
+def joint_kernel(onehot, grads, *refs):
+    chunks, out = refs[:-1], refs[-1]
+    rows = (grads.shape[1] - SCALE_ROWS) // BLOCKS
+    per = chunks[0].shape[0] // rows
+    factors = [factors_of(grads[d, BLOCKS * rows :, :]) for d in range(NY)]
+    for b in range(BLOCKS):
+        cols = slice(b * LANES, (b + 1) * LANES)
+        parts = []
+        for d in range(NY):
+            grad = grads[d, b * rows : (b + 1) * rows, :].astype(jnp.float32) * factors[d][b : b + 1]
+            parts.append(chunks[d // per][(d % per) * rows : (d % per + 1) * rows, cols] * grad)
+        out[:, cols] = lax.dot_general(
             onehot[...],
-            joint,
+            jnp.concatenate(parts, 0),
             (((1,), (0,)), ((), ())),
             precision=lax.Precision.HIGHEST,
             preferred_element_type=jnp.float32,
@@ -156,11 +155,6 @@
 def sum_over_y(packed):
     got = lax.all_to_all(packed, "y", 0, 0, tiled=True)
     return call(unpack_kernel, packed.shape[1:], jnp.int16, got)
-
-
-def pack_acts(chunks):
-    rows = chunks[0].shape[0] * len(chunks) // NY
-    return call(pack_kernel, (NY, BLOCKS * rows + SCALE_ROWS, LANES), jnp.int16, *chunks)
 
 
 def pack_grads(order, test, own, other):
@@ -192,28 +186,28 @@
 
     order = jnp.stack([(x - step) % NX for step in (0, 1, 3, 2)])
     grad_y = sum_over_y(pack_grads(order, grads, train_grad.T, other_grad))
-    act_y = sum_over_y(pack_acts(grams(acts, train_act, other_act)))
-    behind = (y // 2) ^ (y // 4)
+    pair = lax.all_gather(grad_y, "h")
+    grad_all = lax.all_gather(call(both_kernel, grad_y.shape, jnp.int16, pair), "y")
+    chunks = grams(acts, train_act, other_act)
     local = test_act.shape[0]
-    seg, mask = (
-        lax.dynamic_slice(
-            v.reshape(NX, NZ, NC, local), ((x - behind) % NX, 2 * (y % 2), c, 0), (1, 2, 1, local)
-        ).reshape(1, -1)
-        for v in (test_seg, test_mask)
-    )
+
+    def here(values):
+        cut = lax.dynamic_slice(
+            values.reshape(NX, NZ, NC, local), (0, 0, c, 0), (NX, NZ, 1, local)
+        ).reshape(NX, NZ * local)
+        return jnp.concatenate(
+            [
+                jnp.sum(jnp.where(jnp.arange(NX)[:, None] == (x - s) % NX, cut, 0), 0, keepdims=True)
+                for s in (0, 1, 3, 2)
+            ],
+            1,
+        )
+
     test_onehot = (
-        (seg == jnp.arange(TEST_SEQS, dtype=jnp.int32)[:, None]) & (mask != 0)
+        (here(test_seg) == jnp.arange(TEST_SEQS, dtype=jnp.int32)[:, None]) & (here(test_mask) != 0)
     ).astype(jnp.float32)
-    grad_other, act_other = swap(grad_y, "h"), swap(act_y, "h")
     rows = call(
-        joint_kernel,
-        (TEST_SEQS, BLOCKS * LANES),
-        jnp.float32,
-        test_onehot,
-        act_y,
-        act_other,
-        grad_y,
-        grad_other,
+        joint_kernel, (TEST_SEQS, BLOCKS * LANES), jnp.float32, test_onehot, grad_all, *chunks
     )
     n = train_act.shape[0]
     masked = jnp.where(train_mask != 0, train_seg, -1)
@@ -229,7 +223,8 @@
     to = jnp.arange(NY * NC)[:, None, None] % NC
     spread = jnp.where(to == c, mine[None], theirs[None])
     got = lax.all_to_all(spread, ("y", "c"), 0, 0, tiled=True)
-    scores = jnp.sum(got, 0)[:SEQ_PACK, :TEST_SEQS]
+    scores = jnp.sum(got, 0)
+    scores = (scores + swap(scores, "h"))[:SEQ_PACK, :TEST_SEQS]
     return scores * (1.0 / (SEG_LEN * math.sqrt(FF * D)))
 
 

time: 129 us -> 158 us (1.22)
  the two profiles are of different devices: /device:TPU:1 before, /device:TPU:6 now
where the time goes in v9:
time: 158 us; the launch traced here: 157 us
  blocking collectives  80.6 us (51%)
  starting transfers between devices  32.9 us (21%)
  waiting for transfers between devices  24.6 us (16%)
  local copies, waits for them, and re-layouts  7.43 us (5%)
  Pallas kernels  4.27 us (3%)
  matrix products  3.98 us (3%)
  other arithmetic  2.74 us (2%)
    all_gather x1, blocking collectives, on_device(): lax.all_gather(call(both_kernel, grad_y.shape, jnp.int16, pair), 'y')  26.6 us
    all_to_all x1, waiting for transfers between devices, sum_over_y(): got = lax.all_to_all(packed, 'y', 0, 0, tiled=True)  23 us
    all_gather x1, blocking collectives, on_device(): lax.all_gather(jnp.concatenate([test_act, test_grad], 1), 'z', axis=0, ti...  17.9 us
    ppermute x4, starting transfers between devices, swap(): return lax.ppermute(value, axis, [(0, 1), (1, 0)])  15.5 us
    all_gather x1, blocking collectives, on_device(): grads = lax.all_gather(grad_z, 'x', axis=0, tiled=True)  14.6 us
    ppermute x3, starting transfers between devices, over_x(): lax.ppermute(value, 'x', [(i, (i + step) % NX) for i in range(NX)])  11 us
    all_gather x1, blocking collectives, on_device(): pair = lax.all_gather(grad_y, 'h')  10.9 us
    all_to_all x1, blocking collectives, on_device(): got = lax.all_to_all(spread, ('y', 'c'), 0, 0, tiled=True)  10.5 us
  transfers between devices with their start and end apart: 8, of which 2 were waited for; matrix products, arithmetic and copies ran while one was open for 7% of the time, Pallas kernels for 3%

profile of v9, /device:TPU:6, one launch (start us, length us, event | category | flops | bytes accessed | tf_op | source)
XLA Modules:
  0.0 156.8 jit_solution(65173424775743749)
XLA Ops:
  0.0 1.0 pad_maximum_fusion
  1.0 17.9 %all_gather.18 = bf16[128,1920]{1,0:T(8,128)(2,1)S(1)} all-gather(bf16[32,1920]{1,0:T(8,128)(2,1)S(1)} %pad_maximum_fusion), channel_id=1, replica_groups=mesh['x'=4,'z'=4,'c'=2,'y'=8,'h'=2] {'z'}, dimensions={0}, use_global_device_ids=true | all-gather | bytes 614400 | tf_op jit(solution)/shard_map/all_gather | solution.py:177
  18.9 0.8 slice.21
  19.7 5.7 %collective-permute-start.2 = (bf16[128,1600]{1,0:T(8,128)(2,1)}, bf16[128,1600]{1,0:T(8,128)(2,1)S(1)}, u32[]{:S(2)}, u32[]{:S(2)}) collective-permute-start(bf16[128,1600]{1,0:T(8,128)(2,1)} %slice.21), channel_id=1, source_target_pairs={{0,128},{128,256},{256,384},{384,0},{1,129},{129,257},{257,385},{3... | collective-permute-start | bytes 1228808 | tf_op jit(solution)/shard_map/ppermute | solution.py:37
  25.4 1.9 %collective-permute-start.3 = (bf16[128,1600]{1,0:T(8,128)(2,1)}, bf16[128,1600]{1,0:T(8,128)(2,1)S(1)}, u32[]{:S(2)}, u32[]{:S(2)}) collective-permute-start(bf16[128,1600]{1,0:T(8,128)(2,1)} %slice.21), channel_id=1, source_target_pairs={{0,384},{128,0},{256,128},{384,256},{1,385},{129,1},{257,129},{385... | collective-permute-start | bytes 1228808 | tf_op jit(solution)/shard_map/ppermute | solution.py:37
  27.3 3.4 %collective-permute-start.4 = (bf16[128,1600]{1,0:T(8,128)(2,1)}, bf16[128,1600]{1,0:T(8,128)(2,1)}, u32[]{:S(2)}, u32[]{:S(2)}) collective-permute-start(bf16[128,1600]{1,0:T(8,128)(2,1)} %slice.21), channel_id=1, source_target_pairs={{0,256},{128,384},{256,0},{384,128},{1,257},{129,385},{257,1},{385... | collective-permute-start | bytes 1228808 | tf_op jit(solution)/shard_map/ppermute | solution.py:37
  30.7 1.9 %collective-permute-start = (bf16[320,512]{1,0:T(8,128)(2,1)}, bf16[320,512]{1,0:T(8,128)(2,1)S(1)}, u32[]{:S(2)}, u32[]{:S(2)}) collective-permute-start(bf16[320,512]{1,0:T(8,128)(2,1)} %bitcast.27), channel_id=1, source_target_pairs={{0,16},{16,0},{1,17},{17,1},{2,18},{18,2},{3,19},{19,3},{4,20},{20... | collective-permute-start | bytes 983048 | tf_op jit(solution)/shard_map/ppermute | solution.py:32
  32.7 2.4 %collective-permute-start.1 = (bf16[512,1600]{0,1:T(8,128)(2,1)}, bf16[512,1600]{0,1:T(8,128)(2,1)}, u32[]{:S(2)}, u32[]{:S(2)}) collective-permute-start(bf16[512,1600]{0,1:T(8,128)(2,1)} %param.8), channel_id=1, source_target_pairs={{0,16},{16,0},{1,17},{17,1},{2,18},{18,2},{3,19},{19,3},{4,20},{20... | collective-permute-start | bytes 4915208 | tf_op jit(solution)/shard_map/ppermute | solution.py:32
  35.3 0.8 reshape.161
  37.8 14.6 %all_gather.19.test = bf16[512,320]{1,0:T(8,128)(2,1)S(1)} all-gather(bf16[128,320]{1,0:T(8,128)(2,1)S(1)} %slice.20), channel_id=1, replica_groups=mesh['x'=4,'z'=4,'c'=2,'y'=8,'h'=2] {'x'}, dimensions={0}, use_global_device_ids=true | all-gather | bytes 409600 | tf_op jit(solution)/shard_map/all_gather | solution.py:180
  53.2 1.9 %collective-permute-start.5 = (s32[1,512]{1,0:T(1,128)S(1)}, s32[1,512]{1,0:T(1,128)S(1)}, u32[]{:S(2)}, u32[]{:S(2)}) collective-permute-start(s32[1,512]{1,0:T(1,128)S(1)} %compare_select_fusion), channel_id=1, source_target_pairs={{0,16},{16,0},{1,17},{17,1},{2,18},{18,2},{3,19},{19,3},{4,20},{20... | collective-permute-start | bytes 6152 | tf_op jit(solution)/shard_map/ppermute | solution.py:32
  55.2 1.0 copy-done
  56.1 2.7 %shard_map.82 = s16[8,528,128]{2,1,0:T(8,128)(2,1)} custom-call(s32[4]{0:T(128)S(1)} %pad_add_fusion.1.order, bf16[512,320]{1,0:T(8,128)(2,1)S(1)} %all_gather.19.test, bf16[320,512]{1,0:T(8,128)(2,1)S(1)} %bitcast.28, bf16[320,512]{1,0:T(8,128)(2,1)S(1)} %collective-permute-done.other), custom_call_target="tpu_custom_call" | custom-call | tf_op jit(solution)/shard_map/pallas_call | solution.py:162
  58.9 6.4 %all-to-all-start = ((s16[8,528,128]{2,1,0:T(8,128)(2,1)}), s16[8,528,128]{2,1,0:T(8,128)(2,1)S(1)}, u32[]{:S(2)}, u32[]{:S(2)}) async-start(s16[8,528,128]{2,1,0:T(8,128)(2,1)} %shard_map.82), calls=%async_computation | async-start | bytes 2162688 | tf_op jit(solution)/shard_map/all_to_all | solution.py:156
  65.3 1.7 %constant_dynamic-update-slice_fusion.1 = bf16[1024,1600]{0,1:T(8,128)(2,1)S(1)} fusion(bf16[512,1600]{0,1:T(8,128)(2,1)} %param.8), kind=kLoop, calls=%fused_computation.21 | loop fusion | bytes 3276800
  67.0 1.7 %constant_dynamic-update-slice_fusion = bf16[1024,1600]{0,1:T(8,128)(2,1)S(1)} fusion(bf16[1024,1600]{0,1:T(8,128)(2,1)S(1)} %constant_dynamic-update-slice_fusion.1, bf16[512,1600]{0,1:T(8,128)(2,1)} %collective-permute-done.1), kind=kLoop, calls=%fused_computation.20 | loop fusion | bytes 3276800 | tf_op jit(solution)/shard_map/concatenate | solution.py:184
  70.8 1.7 %fusion.13.refs_3_ = f32[128,1024]{1,0:T(8,128)S(1)} fusion(bf16[128,1600]{1,0:T(8,128)(2,1)} %collective-permute-done.4, bf16[1024,1600]{0,1:T(8,128)(2,1)S(1)} %constant_dynamic-update-slice_fusion), kind=kOutput, calls=%fused_computation.40 | convolution fusion | flops 419430400 | bytes 4210688 | tf_op jit(solution)/shard_map/dot_general | solution.py:26
  72.5 23.0 %all-to-all-done.got = s16[8,528,128]{2,1,0:T(8,128)(2,1)S(1)} async-done(((s16[8,528,128]{2,1,0:T(8,128)(2,1)}), s16[8,528,128]{2,1,0:T(8,128)(2,1)S(1)}, u32[]{:S(2)}, u32[]{:S(2)}) %all-to-all-start) | async-done | bytes 1081376 | tf_op jit(solution)/shard_map/all_to_all | solution.py:156
  95.8 10.9 %all-gather = s16[1056,128]{1,0:T(8,128)(2,1)S(1)} all-gather(s16[528,128]{1,0:T(8,128)(2,1)S(1)} %shard_map.83), channel_id=2, replica_groups=mesh['x'=4,'z'=4,'c'=2,'y'=8,'h'=2] {'h'}, dimensions={0}, use_global_device_ids=true | all-gather | bytes 405504 | tf_op jit(solution)/shard_map/all_gather | solution.py:189
  106.8 26.6 %all-gather.3 = s16[4224,128]{1,0:T(8,128)(2,1)S(1)} all-gather(s16[528,128]{1,0:T(8,128)(2,1)S(1)} %shard_map.84), channel_id=3, replica_groups=mesh['x'=4,'z'=4,'c'=2,'y'=8,'h'=2] {'y'}, dimensions={0}, use_global_device_ids=true | all-gather | bytes 1216512 | tf_op jit(solution)/shard_map/all_gather | solution.py:190
  133.5 1.0 shard_map.85
  134.9 10.5 %all_to_all.10 = f32[16,8,128]{2,1,0:T(8,128)S(1)} all-to-all(f32[16,8,128]{2,1,0:T(8,128)S(1)} %broadcast_select_fusion), channel_id=1, replica_groups=mesh['x'=4,'z'=4,'c'=2,'y'=8,'h'=2] {'y','c'}, dimensions={0} | all-to-all | bytes 131072 | tf_op jit(solution)/shard_map/all_to_all | solution.py:225
  145.4 9.2 %collective-permute-start.6 = (f32[8,128]{1,0:T(8,128)S(1)}, f32[8,128]{1,0:T(8,128)S(1)}, u32[]{:S(2)}, u32[]{:S(2)}) collective-permute-start(f32[8,128]{1,0:T(8,128)S(1)} %reduce_sum.89), channel_id=1, source_target_pairs={{0,1},{1,0},{2,3},{3,2},{4,5},{5,4},{6,7},{7,6},{8,9},{9,8},{10,11... | collective-permute-start | bytes 12296 | tf_op jit(solution)/shard_map/ppermute | solution.py:32
  154.6 1.6 %collective-permute-done.6 = f32[8,128]{1,0:T(8,128)S(1)} collective-permute-done((f32[8,128]{1,0:T(8,128)S(1)}, f32[8,128]{1,0:T(8,128)S(1)}, u32[]{:S(2)}, u32[]{:S(2)}) %collective-permute-start.6) | collective-permute-done | bytes 4128 | tf_op jit(solution)/shard_map/ppermute | solution.py:32
  (47 shorter events, 6.1 us)
Async XLA Ops:
  19.7 49.7 %collective-permute-start.2 = (bf16[128,1600]{1,0:T(8,128)(2,1)}, bf16[128,1600]{1,0:T(8,128)(2,1)S(1)}, u32[]{:S(2)}, u32[]{:S(2)}) collective-permute-start(bf16[128,1600]{1,0:T(8,128)(2,1)} %slice.21), channel_id=1, source_target_pairs={{0,128},{128,256},{256,384},{384,0},{1,129},{129,257},{257,385},{3... | collective-permute-start | bytes 1228808 | tf_op jit(solution)/shard_map/ppermute | solution.py:37
  25.4 44.6 %collective-permute-start.3 = (bf16[128,1600]{1,0:T(8,128)(2,1)}, bf16[128,1600]{1,0:T(8,128)(2,1)S(1)}, u32[]{:S(2)}, u32[]{:S(2)}) collective-permute-start(bf16[128,1600]{1,0:T(8,128)(2,1)} %slice.21), channel_id=1, source_target_pairs={{0,384},{128,0},{256,128},{384,256},{1,385},{129,1},{257,129},{385... | collective-permute-start | bytes 1228808 | tf_op jit(solution)/shard_map/ppermute | solution.py:37
  27.3 43.4 %collective-permute-start.4 = (bf16[128,1600]{1,0:T(8,128)(2,1)}, bf16[128,1600]{1,0:T(8,128)(2,1)}, u32[]{:S(2)}, u32[]{:S(2)}) collective-permute-start(bf16[128,1600]{1,0:T(8,128)(2,1)} %slice.21), channel_id=1, source_target_pairs={{0,256},{128,384},{256,0},{384,128},{1,257},{129,385},{257,1},{385... | collective-permute-start | bytes 1228808 | tf_op jit(solution)/shard_map/ppermute | solution.py:37
  30.7 22.5 %collective-permute-start = (bf16[320,512]{1,0:T(8,128)(2,1)}, bf16[320,512]{1,0:T(8,128)(2,1)S(1)}, u32[]{:S(2)}, u32[]{:S(2)}) collective-permute-start(bf16[320,512]{1,0:T(8,128)(2,1)} %bitcast.27), channel_id=1, source_target_pairs={{0,16},{16,0},{1,17},{17,1},{2,18},{18,2},{3,19},{19,3},{4,20},{20... | collective-permute-start | bytes 983048 | tf_op jit(solution)/shard_map/ppermute | solution.py:32
  32.7 34.3 %collective-permute-start.1 = (bf16[512,1600]{0,1:T(8,128)(2,1)}, bf16[512,1600]{0,1:T(8,128)(2,1)}, u32[]{:S(2)}, u32[]{:S(2)}) collective-permute-start(bf16[512,1600]{0,1:T(8,128)(2,1)} %param.8), channel_id=1, source_target_pairs={{0,16},{16,0},{1,17},{17,1},{2,18},{18,2},{3,19},{19,3},{4,20},{20... | collective-permute-start | bytes 4915208 | tf_op jit(solution)/shard_map/ppermute | solution.py:32
  53.2 81.2 %collective-permute-start.5 = (s32[1,512]{1,0:T(1,128)S(1)}, s32[1,512]{1,0:T(1,128)S(1)}, u32[]{:S(2)}, u32[]{:S(2)}) collective-permute-start(s32[1,512]{1,0:T(1,128)S(1)} %compare_select_fusion), channel_id=1, source_target_pairs={{0,16},{16,0},{1,17},{17,1},{2,18},{18,2},{3,19},{19,3},{4,20},{20... | collective-permute-start | bytes 6152 | tf_op jit(solution)/shard_map/ppermute | solution.py:32
  55.2 1.0 copy-start
  58.9 36.5 %all-to-all-start = ((s16[8,528,128]{2,1,0:T(8,128)(2,1)}), s16[8,528,128]{2,1,0:T(8,128)(2,1)S(1)}, u32[]{:S(2)}, u32[]{:S(2)}) async-start(s16[8,528,128]{2,1,0:T(8,128)(2,1)} %shard_map.82), calls=%async_computation | async-start | bytes 2162688 | tf_op jit(solution)/shard_map/all_to_all | solution.py:156
  145.4 10.8 %collective-permute-start.6 = (f32[8,128]{1,0:T(8,128)S(1)}, f32[8,128]{1,0:T(8,128)S(1)}, u32[]{:S(2)}, u32[]{:S(2)}) collective-permute-start(f32[8,128]{1,0:T(8,128)S(1)} %reduce_sum.89), channel_id=1, source_target_pairs={{0,1},{1,0},{2,3},{3,2},{4,5},{5,4},{6,7},{7,6},{8,9},{9,8},{10,11... | collective-permute-start | bytes 12296 | tf_op jit(solution)/shard_map/ppermute | solution.py:32

commit v10 on v8

--- a/solution.py
+++ b/solution.py
@@ -119,18 +119,18 @@
     pack(Pieces(blocks, pieces), out, [()])
 
 
-def joint_kernel(onehot, act_own, act_other, grad_own, grad_other, out):
+def joint_kernel(onehot, act_own, grad_own, grad_other, out):
     blocks = BLOCKS
     rows = (act_own.shape[0] - SCALE_ROWS) // blocks
 
     def part(ref, factor, b):
         return ref[b * rows : (b + 1) * rows, :].astype(jnp.float32) * factor[b : b + 1]
 
-    refs = (act_own, act_other, grad_own, grad_other)
+    refs = (act_own, grad_own, grad_other)
     f = [factors_of(r[blocks * rows :, :]) for r in refs]
     for b in range(blocks):
-        a0, a1, g0, g1 = (part(r, k, b) for r, k in zip(refs, f))
-        joint = (a0 + a1) * (g0 + g1)
+        act, g0, g1 = (part(r, k, b) for r, k in zip(refs, f))
+        joint = act * (g0 + g1)
         out[:, b * LANES : (b + 1) * LANES] = lax.dot_general(
             onehot[...],
             joint,
@@ -206,15 +206,12 @@
     ).astype(jnp.float32)
     grad_pair = lax.all_gather(grad_y, "h")
     grad_y, grad_other = grad_pair[0], grad_pair[1]
-    act_pair = lax.all_gather(act_y, "h")
-    act_y, act_other = act_pair[0], act_pair[1]
     rows = call(
         joint_kernel,
         (TEST_SEQS, BLOCKS * LANES),
         jnp.float32,
         test_onehot,
         act_y,
-        act_other,
         grad_y,
         grad_other,
     )
@@ -232,7 +229,7 @@
     to = jnp.arange(NY * NC)[:, None, None] % NC
     spread = jnp.where(to == c, mine[None], theirs[None])
     got = lax.all_to_all(spread, ("y", "c"), 0, 0, tiled=True)
-    scores = jnp.sum(got, 0)[:SEQ_PACK, :TEST_SEQS]
+    scores = lax.psum(jnp.sum(got, 0), "h")[:SEQ_PACK, :TEST_SEQS]
     return scores * (1.0 / (SEG_LEN * math.sqrt(FF * D)))
 
 

time: 128 us -> 126 us (0.984)
  blocking collectives: 63.7 us -> 62.3 us
    all_gather x1 -> x0, blocking collectives: 9.98 us -> none  [on_device(): act_pair = lax.all_gather(act_y, 'h')]
    psum x0 -> x1, blocking collectives: none -> 9.18 us  [on_device(): scores = lax.psum(jnp.sum(got, 0), 'h')[:SEQ_PACK, :TEST_SEQS]]
where the time goes in v10:
time: 126 us; the launch traced here: 124 us
  blocking collectives  62.3 us (49%)
  starting transfers between devices  27.9 us (22%)
  waiting for transfers between devices  19.9 us (16%)
  Pallas kernels  5.3 us (4%)
  local copies, waits for them, and re-layouts  3.43 us (3%)
  matrix products  2.91 us (2%)
  other arithmetic  1.93 us (2%)
    all_gather x1, blocking collectives, on_device(): lax.all_gather(jnp.concatenate([test_act, test_grad], 1), 'z', axis=0, ti...  18 us
    all_gather x1, blocking collectives, on_device(): grads = lax.all_gather(grad_z, 'x', axis=0, tiled=True)  13.4 us
    all_to_all x2, starting transfers between devices, sum_over_y(): got = lax.all_to_all(packed, 'y', 0, 0, tiled=True)  12.4 us
    all_gather x1, blocking collectives, on_device(): grad_pair = lax.all_gather(grad_y, 'h')  11.3 us
    all_to_all x1, blocking collectives, on_device(): got = lax.all_to_all(spread, ('y', 'c'), 0, 0, tiled=True)  10.4 us
    all_to_all x2, waiting for transfers between devices, sum_over_y(): got = lax.all_to_all(packed, 'y', 0, 0, tiled=True)  10.1 us
    ppermute x3, waiting for transfers between devices, over_x(): lax.ppermute(value, 'x', [(i, (i + step) % NX) for i in range(NX)])  9.84 us
    ppermute x3, starting transfers between devices, over_x(): lax.ppermute(value, 'x', [(i, (i + step) % NX) for i in range(NX)])  9.22 us
  transfers between devices with their start and end apart: 8, of which 4 were waited for; matrix products, arithmetic and copies ran while one was open for 5% of the time, Pallas kernels for 4%

profile of v10, /device:TPU:6, one launch (start us, length us, event | category | flops | bytes accessed | tf_op | source)
XLA Modules:
  0.0 124.0 jit_solution(1887431455296219744)
XLA Ops:
  0.0 1.9 %collective-permute-start = (bf16[512,1600]{0,1:T(8,128)(2,1)}, bf16[512,1600]{0,1:T(8,128)(2,1)}, u32[]{:S(2)}, u32[]{:S(2)}) collective-permute-start(bf16[512,1600]{0,1:T(8,128)(2,1)} %param.8), channel_id=1, source_target_pairs={{0,16},{16,0},{1,17},{17,1},{2,18},{18,2},{3,19},{19,3},{4,20},{20... | collective-permute-start | bytes 4915208 | tf_op jit(solution)/shard_map/ppermute | solution.py:32
  1.9 2.4 %collective-permute-start.4 = (bf16[320,512]{1,0:T(8,128)(2,1)}, bf16[320,512]{1,0:T(8,128)(2,1)S(1)}, u32[]{:S(2)}, u32[]{:S(2)}) collective-permute-start(bf16[320,512]{1,0:T(8,128)(2,1)} %bitcast.14), channel_id=1, source_target_pairs={{0,16},{16,0},{1,17},{17,1},{2,18},{18,2},{3,19},{19,3},{4,20},{20... | collective-permute-start | bytes 983048 | tf_op jit(solution)/shard_map/ppermute | solution.py:32
  4.3 1.1 pad_maximum_fusion
  5.5 18.0 %all_gather.12 = bf16[128,1920]{1,0:T(8,128)(2,1)S(1)} all-gather(bf16[32,1920]{1,0:T(8,128)(2,1)S(1)} %pad_maximum_fusion), channel_id=1, replica_groups=mesh['x'=4,'z'=4,'c'=2,'y'=8,'h'=2] {'z'}, dimensions={0}, use_global_device_ids=true | all-gather | bytes 614400 | tf_op jit(solution)/shard_map/all_gather | solution.py:183
  23.7 13.4 %all_gather.13.test = bf16[512,320]{1,0:T(8,128)(2,1)S(1)} all-gather(bf16[128,320]{1,0:T(8,128)(2,1)S(1)} %slice.31), channel_id=1, replica_groups=mesh['x'=4,'z'=4,'c'=2,'y'=8,'h'=2] {'x'}, dimensions={0}, use_global_device_ids=true | all-gather | bytes 409600 | tf_op jit(solution)/shard_map/all_gather | solution.py:186
  37.1 1.0 copy-done
  38.1 2.7 %shard_map.84 = s16[8,528,128]{2,1,0:T(8,128)(2,1)} custom-call(s32[4]{0:T(128)S(1)} %pad_add_fusion.order, bf16[512,320]{1,0:T(8,128)(2,1)S(1)} %all_gather.13.test, bf16[320,512]{1,0:T(8,128)(2,1)S(1)} %bitcast.15, bf16[320,512]{1,0:T(8,128)(2,1)S(1)} %collective-permute-done.4.other), custom_call_target="tpu_custom_call" | custom-call | tf_op jit(solution)/shard_map/pallas_call | solution.py:168
  40.8 6.2 %all-to-all-start.1 = ((s16[8,528,128]{2,1,0:T(8,128)(2,1)}), s16[8,528,128]{2,1,0:T(8,128)(2,1)S(1)}, u32[]{:S(2)}, u32[]{:S(2)}) async-start(s16[8,528,128]{2,1,0:T(8,128)(2,1)} %shard_map.84), calls=%async_computation.1 | async-start | bytes 2162688 | tf_op jit(solution)/shard_map/all_to_all | solution.py:157
  47.1 3.2 %collective-permute-start.1 = (bf16[128,1600]{1,0:T(8,128)(2,1)S(1)}, bf16[128,1600]{1,0:T(8,128)(2,1)S(1)}, u32[]{:S(2)}, u32[]{:S(2)}) collective-permute-start(bf16[128,1600]{1,0:T(8,128)(2,1)S(1)} %slice.30), channel_id=1, source_target_pairs={{0,128},{128,256},{256,384},{384,0},{1,129},{129,257},{257,385},{3... | collective-permute-start | bytes 1228808 | tf_op jit(solution)/shard_map/ppermute | solution.py:37
  50.2 2.7 %collective-permute-start.2 = (bf16[128,1600]{1,0:T(8,128)(2,1)S(1)}, bf16[128,1600]{1,0:T(8,128)(2,1)S(1)}, u32[]{:S(2)}, u32[]{:S(2)}) collective-permute-start(bf16[128,1600]{1,0:T(8,128)(2,1)S(1)} %slice.30), channel_id=1, source_target_pairs={{0,384},{128,0},{256,128},{384,256},{1,385},{129,1},{257,129},{385... | collective-permute-start | bytes 1228808 | tf_op jit(solution)/shard_map/ppermute | solution.py:37
  52.9 3.4 %collective-permute-start.3 = (bf16[128,1600]{1,0:T(8,128)(2,1)S(1)}, bf16[128,1600]{1,0:T(8,128)(2,1)S(1)}, u32[]{:S(2)}, u32[]{:S(2)}) collective-permute-start(bf16[128,1600]{1,0:T(8,128)(2,1)S(1)} %slice.30), channel_id=1, source_target_pairs={{0,256},{128,384},{256,0},{384,128},{1,257},{129,385},{257,1},{385... | collective-permute-start | bytes 1228808 | tf_op jit(solution)/shard_map/ppermute | solution.py:37
  56.6 1.7 %constant_dynamic-update-slice_fusion = bf16[1024,1600]{0,1:T(8,128)(2,1)S(1)} fusion(bf16[1024,1600]{0,1:T(8,128)(2,1)S(1)} %constant_dynamic-update-slice_fusion.1, bf16[512,1600]{0,1:T(8,128)(2,1)} %collective-permute-done), kind=kLoop, calls=%fused_computation.9 | loop fusion | bytes 3276800 | tf_op jit(solution)/shard_map/concatenate | solution.py:190
  58.3 0.7 fusion.9.refs_0_
  58.9 2.0 %collective-permute-done.1 = bf16[128,1600]{1,0:T(8,128)(2,1)S(1)} collective-permute-done((bf16[128,1600]{1,0:T(8,128)(2,1)S(1)}, bf16[128,1600]{1,0:T(8,128)(2,1)S(1)}, u32[]{:S(2)}, u32[]{:S(2)}) %collective-permute-start.1) | collective-permute-done | bytes 409632 | tf_op jit(solution)/shard_map/ppermute | solution.py:37
  60.9 0.7 fusion.12.refs_1_
  61.6 7.9 %collective-permute-done.2 = bf16[128,1600]{1,0:T(8,128)(2,1)S(1)} collective-permute-done((bf16[128,1600]{1,0:T(8,128)(2,1)S(1)}, bf16[128,1600]{1,0:T(8,128)(2,1)S(1)}, u32[]{:S(2)}, u32[]{:S(2)}) %collective-permute-start.2) | collective-permute-done | bytes 409632 | tf_op jit(solution)/shard_map/ppermute | solution.py:37
  70.8 1.5 %shard_map.82 = s16[8,528,128]{2,1,0:T(8,128)(2,1)} custom-call(f32[128,1024]{1,0:T(8,128)S(1)} %fusion.9.refs_0_, f32[128,1024]{1,0:T(8,128)S(1)} %fusion.12.refs_1_, f32[128,1024]{1,0:T(8,128)S(1)} %fusion.13.refs_2_, f32[128,1024]{1,0:T(8,128)S(1)} %fusion.14.refs_3_), custom_call_target="tpu_custom_call" | custom-call | tf_op jit(solution)/shard_map/pallas_call | solution.py:147
  72.3 0.7 all-to-all-done.1.got
  73.0 6.2 %all-to-all-start = ((s16[8,528,128]{2,1,0:T(8,128)(2,1)}), s16[8,528,128]{2,1,0:T(8,128)(2,1)S(1)}, u32[]{:S(2)}, u32[]{:S(2)}) async-start(s16[8,528,128]{2,1,0:T(8,128)(2,1)} %shard_map.82), calls=%async_computation | async-start | bytes 2162688 | tf_op jit(solution)/shard_map/all_to_all | solution.py:157
  79.3 1.9 %collective-permute-start.5 = (s32[1,512]{1,0:T(1,128)S(1)}, s32[1,512]{1,0:T(1,128)S(1)}, u32[]{:S(2)}, u32[]{:S(2)}) collective-permute-start(s32[1,512]{1,0:T(1,128)S(1)} %compare_select_fusion), channel_id=1, source_target_pairs={{0,16},{16,0},{1,17},{17,1},{2,18},{18,2},{3,19},{19,3},{4,20},{20... | collective-permute-start | bytes 6152 | tf_op jit(solution)/shard_map/ppermute | solution.py:32
  82.1 11.3 %all-gather = s16[1056,128]{1,0:T(8,128)(2,1)S(1)} all-gather(s16[528,128]{1,0:T(8,128)(2,1)S(1)} %shard_map.85), channel_id=2, replica_groups=mesh['x'=4,'z'=4,'c'=2,'y'=8,'h'=2] {'h'}, dimensions={0}, use_global_device_ids=true | all-gather | bytes 405504 | tf_op jit(solution)/shard_map/all_gather | solution.py:207
  93.4 9.3 %all-to-all-done.got = s16[8,528,128]{2,1,0:T(8,128)(2,1)S(1)} async-done(((s16[8,528,128]{2,1,0:T(8,128)(2,1)}), s16[8,528,128]{2,1,0:T(8,128)(2,1)S(1)}, u32[]{:S(2)}, u32[]{:S(2)}) %all-to-all-start) | async-done | bytes 1081376 | tf_op jit(solution)/shard_map/all_to_all | solution.py:157
  103.8 10.4 %all_to_all.15 = f32[16,8,128]{2,1,0:T(8,128)S(1)} all-to-all(f32[16,8,128]{2,1,0:T(8,128)S(1)} %broadcast_select_fusion), channel_id=1, replica_groups=mesh['x'=4,'z'=4,'c'=2,'y'=8,'h'=2] {'y','c'}, dimensions={0} | all-to-all | bytes 131072 | tf_op jit(solution)/shard_map/all_to_all | solution.py:231
  114.2 9.2 %psum.7 = f32[8,128]{1,0:T(8,128)S(1)} all-reduce(f32[8,128]{1,0:T(8,128)S(1)} %reduce_sum.9), channel_id=1, replica_groups=mesh['x'=4,'z'=4,'c'=2,'y'=8,'h'=2] {'h'}, use_global_device_ids=true, to_apply=%region_1.2 | all-reduce | flops 1024 | bytes 8192 | tf_op jit(solution)/shard_map/psum | solution.py:232
  (41 shorter events, 4.2 us)
Async XLA Ops:
  0.0 56.6 %collective-permute-start = (bf16[512,1600]{0,1:T(8,128)(2,1)}, bf16[512,1600]{0,1:T(8,128)(2,1)}, u32[]{:S(2)}, u32[]{:S(2)}) collective-permute-start(bf16[512,1600]{0,1:T(8,128)(2,1)} %param.8), channel_id=1, source_target_pairs={{0,16},{16,0},{1,17},{17,1},{2,18},{18,2},{3,19},{19,3},{4,20},{20... | collective-permute-start | bytes 4915208 | tf_op jit(solution)/shard_map/ppermute | solution.py:32
  1.9 35.2 %collective-permute-start.4 = (bf16[320,512]{1,0:T(8,128)(2,1)}, bf16[320,512]{1,0:T(8,128)(2,1)S(1)}, u32[]{:S(2)}, u32[]{:S(2)}) collective-permute-start(bf16[320,512]{1,0:T(8,128)(2,1)} %bitcast.14), channel_id=1, source_target_pairs={{0,16},{16,0},{1,17},{17,1},{2,18},{18,2},{3,19},{19,3},{4,20},{20... | collective-permute-start | bytes 983048 | tf_op jit(solution)/shard_map/ppermute | solution.py:32
  4.3 52.0 %copy-start.1 = (bf16[512,1600]{0,1:T(8,128)(2,1)S(1)}, bf16[512,1600]{0,1:T(8,128)(2,1)}, u32[]{:S(2)}) copy-start(bf16[512,1600]{0,1:T(8,128)(2,1)} %param.8) | copy-start | bytes 4915204
  37.1 1.0 copy-start
  40.8 32.2 %all-to-all-start.1 = ((s16[8,528,128]{2,1,0:T(8,128)(2,1)}), s16[8,528,128]{2,1,0:T(8,128)(2,1)S(1)}, u32[]{:S(2)}, u32[]{:S(2)}) async-start(s16[8,528,128]{2,1,0:T(8,128)(2,1)} %shard_map.84), calls=%async_computation.1 | async-start | bytes 2162688 | tf_op jit(solution)/shard_map/all_to_all | solution.py:157
  47.1 13.9 %collective-permute-start.1 = (bf16[128,1600]{1,0:T(8,128)(2,1)S(1)}, bf16[128,1600]{1,0:T(8,128)(2,1)S(1)}, u32[]{:S(2)}, u32[]{:S(2)}) collective-permute-start(bf16[128,1600]{1,0:T(8,128)(2,1)S(1)} %slice.30), channel_id=1, source_target_pairs={{0,128},{128,256},{256,384},{384,0},{1,129},{129,257},{257,385},{3... | collective-permute-start | bytes 1228808 | tf_op jit(solution)/shard_map/ppermute | solution.py:37
  50.2 19.2 %collective-permute-start.2 = (bf16[128,1600]{1,0:T(8,128)(2,1)S(1)}, bf16[128,1600]{1,0:T(8,128)(2,1)S(1)}, u32[]{:S(2)}, u32[]{:S(2)}) collective-permute-start(bf16[128,1600]{1,0:T(8,128)(2,1)S(1)} %slice.30), channel_id=1, source_target_pairs={{0,384},{128,0},{256,128},{384,256},{1,385},{129,1},{257,129},{385... | collective-permute-start | bytes 1228808 | tf_op jit(solution)/shard_map/ppermute | solution.py:37
  52.9 17.2 %collective-permute-start.3 = (bf16[128,1600]{1,0:T(8,128)(2,1)S(1)}, bf16[128,1600]{1,0:T(8,128)(2,1)S(1)}, u32[]{:S(2)}, u32[]{:S(2)}) collective-permute-start(bf16[128,1600]{1,0:T(8,128)(2,1)S(1)} %slice.30), channel_id=1, source_target_pairs={{0,256},{128,384},{256,0},{384,128},{1,257},{129,385},{257,1},{385... | collective-permute-start | bytes 1228808 | tf_op jit(solution)/shard_map/ppermute | solution.py:37
  70.8 8.5 %copy-start.4 = (s32[1,512]{1,0:T(1,128)S(1)}, s32[1,512]{1,0:T(1,128)}, u32[]{:S(2)}) copy-start(s32[1,512]{1,0:T(1,128)} %param.10) | copy-start | bytes 6148
  70.8 8.4 %copy-start.5 = (s32[1,512]{1,0:T(1,128)S(1)}, s32[1,512]{1,0:T(1,128)}, u32[]{:S(2)}) copy-start(s32[1,512]{1,0:T(1,128)} %param.11) | copy-start | bytes 6148
  70.8 10.4 %copy-start.2 = (s32[1024]{0:T(1024)S(1)}, s32[1024]{0:T(1024)}, u32[]{:S(2)}) copy-start(s32[1024]{0:T(1024)} %param.14) | copy-start | bytes 12292
  70.8 10.6 %copy-start.3 = (s32[1024]{0:T(1024)S(1)}, s32[1024]{0:T(1024)}, u32[]{:S(2)}) copy-start(s32[1024]{0:T(1024)} %param.15) | copy-start | bytes 12292
  73.0 29.7 %all-to-all-start = ((s16[8,528,128]{2,1,0:T(8,128)(2,1)}), s16[8,528,128]{2,1,0:T(8,128)(2,1)S(1)}, u32[]{:S(2)}, u32[]{:S(2)}) async-start(s16[8,528,128]{2,1,0:T(8,128)(2,1)} %shard_map.82), calls=%async_computation | async-start | bytes 2162688 | tf_op jit(solution)/shard_map/all_to_all | solution.py:157
  79.3 24.2 %collective-permute-start.5 = (s32[1,512]{1,0:T(1,128)S(1)}, s32[1,512]{1,0:T(1,128)S(1)}, u32[]{:S(2)}, u32[]{:S(2)}) collective-permute-start(s32[1,512]{1,0:T(1,128)S(1)} %compare_select_fusion), channel_id=1, source_target_pairs={{0,16},{16,0},{1,17},{17,1},{2,18},{18,2},{3,19},{19,3},{4,20},{20... | collective-permute-start | bytes 6152 | tf_op jit(solution)/shard_map/ppermute | solution.py:32
